TPU v7x, 512 devices: a whole 4x4x16 slice. The times are simulated.
512 devices in a mesh: grp: 16 (over z), pb: 32 (over x, y, core).
Axes of the slice: x: 4, y: 4, z: 16, core: 2. Of those that a mesh axis runs over, the one named last changes fastest.
Arguments:
- queries: bfloat16 [8192, 4096], P('grp', 'pb'), may hold values from -12 to 12
- outputs: bfloat16 [8192, 4096], P('grp', 'pb'), may hold values from -3 to 3
- readout_grad: bfloat16 [8192, 8192], P('grp', 'pb'), may hold values from -24 to 24
- readout_weight: bfloat16 [4096, 8192], P('pb'), may hold values from -0.125 to 0.125
- log_norm: float32 [8192, 32], P('grp', 'pb'), may hold values from 9 to 11
- probes: int32 [32, 8192, 4], P('pb', 'grp'), may hold values from 0 to 127, all different within a row; in each aligned block of 512 rows (0 to 511, 512 to 1023, ..., all dimensions but the last counted through in order) at most 32 rows name the same one
- owner_slots: int32 [32, 128], P('pb'), may hold values from 0 to 127, each once within a row
- counts: int32 [32, 128], P('pb', 'grp'), may hold values from 1 to 512
- cluster_keys: bfloat16 [32, 128, 512, 128], P('pb', 'grp'), may hold values from -6 to 6
- values: bfloat16 [32, 128, 512, 128], P('pb', 'grp'), may hold values from -6 to 6
Outputs:
- query_grad: bfloat16 [8192, 4096], P('grp', 'pb')
Inputs may be any that keep to these rules, and one draw needn't show every extreme that they name: `probes`: each token names 4 different clusters for each head. Within the 512 tokens of one index of grp and one head, no cluster is named by more than 32 tokens, a bound that some block reaches. `owner_slots`: for each head a permutation of the 128 clusters; slot s is stored on index s // 8 of grp.
All inputs are finite; a program needn't handle non-finite values.
Results may differ from a plain program's by a relative error of at most 0.029.
Values may be sent and summed in bfloat16 or wider, within the bound.
No kernel may reach another device: no remote copies, remote signals or barrier semaphores. Data moves between devices by JAX's collectives and lax.ppermute only.
A program may use at most 64 MiB of HBM per device.

v0:
```python
import jax
import jax.numpy as jnp
from jax import lax
from jax.sharding import PartitionSpec as P


def slot_places(probe_ids, slot_table, capacity):
    cluster_ids = jnp.arange(slot_table.shape[1], dtype=jnp.int32)
    matches = probe_ids[..., None] == cluster_ids
    slot_ids = jnp.sum(jnp.where(matches, slot_table[:, None, None, :], 0), axis=3, dtype=jnp.int32)
    same_slot = slot_ids[..., None] == cluster_ids
    marked = jnp.sum(same_slot.astype(jnp.int32), axis=2, dtype=jnp.int32)
    before = jnp.cumsum(marked, axis=1, dtype=jnp.int32) - marked
    ranking = jnp.sum(jnp.where(same_slot, before[:, :, None, :], 0), axis=3, dtype=jnp.int32)
    return slot_ids * capacity + ranking


def to_slots(rows, places, slot_total):
    head_count, token_count, probe_count = places.shape
    repeated = jnp.repeat(rows, probe_count, axis=1)
    flat_places = places.reshape(head_count, token_count * probe_count)
    blank_rows = jnp.zeros((head_count, slot_total) + rows.shape[2:], rows.dtype)

    def place_head(blank_head, place_head_ids, rows_head):
        return blank_head.at[place_head_ids].set(rows_head)

    return jax.vmap(place_head)(blank_rows, flat_places, repeated)


def shards(
    queries,
    outputs,
    readout_grad,
    readout_weight,
    log_norm,
    probes,
    owner_slots,
    counts,
    cluster_keys,
    values,
):
    token_count = queries.shape[0]
    head_count = probes.shape[0]
    probe_count = probes.shape[2]
    local_clusters = cluster_keys.shape[1]
    cluster_span = cluster_keys.shape[2]
    head_width = cluster_keys.shape[3]
    clusters = owner_slots.shape[1]
    groups = lax.axis_size("grp")
    capacity = 2 * token_count * probe_count // clusters
    slot_total = clusters * capacity
    score_scale = head_width ** (-0.5)
    places = slot_places(probes, owner_slots, capacity)

    def shaped(rows):
        return to_slots(rows, places, slot_total).reshape(
            (head_count, clusters, capacity) + rows.shape[2:]
        )

    query_slots = shaped(queries.reshape(token_count, head_count, head_width).transpose(1, 0, 2))
    norm_slots = shaped(log_norm.T[:, :, None])[..., 0]
    grad_out = lax.dot_general(
        lax.all_gather(readout_grad, "pb", axis=1, tiled=True),
        readout_weight,
        (((1,), (1,)), ((), ())),
        preferred_element_type=jnp.float32,
    ).astype(jnp.bfloat16)
    row_delta = jnp.sum(
        (grad_out.astype(jnp.float32) * outputs.astype(jnp.float32)).reshape(
            token_count, head_count, head_width
        ),
        axis=2,
    )
    grad_slots = shaped(grad_out.reshape(token_count, head_count, head_width).transpose(1, 0, 2))
    delta_slots = shaped(row_delta.T[:, :, None])[..., 0]
    grad_slots, delta_slots = (grad_slots, delta_slots)
    query_recv, grad_recv = (
        lax.all_to_all(query_slots, "grp", split_axis=1, concat_axis=2, tiled=True),
        lax.all_to_all(grad_slots, "grp", split_axis=1, concat_axis=2, tiled=True),
    )
    norm_recv, delta_recv = (
        lax.all_to_all(norm_slots, "grp", split_axis=1, concat_axis=2, tiled=True),
        lax.all_to_all(delta_slots, "grp", split_axis=1, concat_axis=2, tiled=True),
    )
    arrivals = groups * capacity
    key_index = jnp.arange(cluster_span, dtype=jnp.int32)
    contract_last = (((1,), (1,)), ((), ()))

    def block_grad(pieces):
        query_block, grad_block, norm_block, delta_block, key_block, value_block, valid = pieces
        scores = (
            lax.dot_general(
                query_block, key_block, contract_last, preferred_element_type=jnp.float32
            )
            * score_scale
        )
        weights = jnp.where(
            key_index[None, :] < valid,
            jnp.exp(scores - norm_block[:, None]),
            jnp.zeros_like(scores),
        )
        grad_prob = lax.dot_general(
            grad_block, value_block, contract_last, preferred_element_type=jnp.float32
        )
        grad_score = (weights * (grad_prob - delta_block[:, None])).astype(jnp.bfloat16)
        return (
            jnp.dot(grad_score, key_block, preferred_element_type=jnp.float32) * score_scale
        ).astype(jnp.bfloat16)

    block_count = head_count * local_clusters
    partials = lax.map(
        block_grad,
        (
            query_recv.reshape(block_count, arrivals, head_width),
            grad_recv.reshape(block_count, arrivals, head_width),
            norm_recv.reshape(block_count, arrivals),
            delta_recv.reshape(block_count, arrivals),
            cluster_keys.reshape(block_count, cluster_span, head_width),
            values.reshape(block_count, cluster_span, head_width),
            counts.reshape(block_count),
        ),
    )
    returned = lax.all_to_all(
        partials.reshape(head_count, local_clusters, arrivals, head_width),
        "grp",
        split_axis=2,
        concat_axis=1,
        tiled=True,
    )
    returned = returned.reshape(head_count, slot_total, head_width)

    def pick_head(returned_head, place_head_ids):
        return returned_head[place_head_ids]

    picked = jax.vmap(pick_head)(returned, places.reshape(head_count, token_count * probe_count))
    summed = jnp.sum(
        picked.reshape(head_count, token_count, probe_count, head_width).astype(jnp.float32), axis=2
    )
    return (
        summed.astype(jnp.bfloat16).transpose(1, 0, 2).reshape(token_count, head_count * head_width)
    )


def solution(mesh):
    placed = (
        P("grp", "pb"),
        P("grp", "pb"),
        P("grp", "pb"),
        P("pb", None),
        P("grp", "pb"),
        P("pb", "grp", None),
        P("pb", None),
        P("pb", "grp"),
        P("pb", "grp", None, None),
        P("pb", "grp", None, None),
    )
    return jax.shard_map(
        shards, mesh=mesh, in_specs=placed, out_specs=P("grp", "pb"), check_vma=False
    )
```

profile of v0, /device:TPU:24, one launch (start us, length us, event | category | flops | bytes accessed | tf_op | source)
XLA Modules:
  0.0 319.5 jit_solution(2050619712548263774)
XLA Ops:
  7.3 1.3 select_reduce_fusion.1
  12.8 8.1 %scatter_custom_fusion.1 = f32[4096]{0:T(1024)S(1)} fusion(s32[2048]{0:T(1024)S(1)} %broadcast_select_fusion, f32[2048]{0:T(1024)S(1)} %reshape.295, f32[]{:T(128)} %constant.36.clone.1), kind=kCustom, calls=%fused_computation.66 | custom fusion | bytes 16388
  23.0 15.2 %all-to-all-start.1 = ((f32[16,1,256]{2,1,0:T(1,128)}), f32[16,1,256]{2,1,0:T(1,128)S(1)}, u32[]{:S(2)}, u32[]{:S(2)}) async-start(f32[16,1,256]{2,1,0:T(1,128)} %reshape.336), calls=%async_computation.1 | async-start | bytes 32768 | tf_op jit(solution)/shard_map/all_to_all | solution.py:82
  39.3 6.9 %scatter_custom_fusion = bf16[4096,128]{1,0:T(8,128)(2,1)} fusion(s32[2048]{0:T(1024)S(1)} %broadcast_select_fusion, bf16[2048,128]{1,0:T(8,128)(2,1)S(1)} %bitcast.124, bf16[]{:T(256)} %constant.24.clone.1), kind=kCustom, calls=%fused_computation.46 | custom fusion | bytes 1048578
  46.2 4.5 %all-to-all-done.1 = f32[16,1,256]{2,1,0:T(1,128)S(1)} async-done(((f32[16,1,256]{2,1,0:T(1,128)}), f32[16,1,256]{2,1,0:T(1,128)S(1)}, u32[]{:S(2)}, u32[]{:S(2)}) %all-to-all-start.1) | async-done | bytes 16416 | tf_op jit(solution)/shard_map/all_to_all | solution.py:82
  51.3 7.5 %all-to-all-start = ((bf16[1,128,32,128]{3,2,0,1:T(8,128)(2,1)}), bf16[1,128,32,128]{3,2,0,1:T(8,128)(2,1)S(1)}, u32[]{:S(2)}, u32[]{:S(2)}) async-start(bf16[1,128,32,128]{3,2,0,1:T(8,128)(2,1)} %bitcast.115), calls=%async_computation | async-start | bytes 2097152 | tf_op jit(solution)/shard_map/all_to_all | solution.py:78
  59.8 29.3 %all-gather.2.cloned.1.call-done = bf16[512,8192]{1,0:T(8,128)(2,1)} async-done(((bf16[512,256]{1,0:T(8,128)(2,1)}), bf16[512,8192]{1,0:T(8,128)(2,1)}) %all-gather.2.cloned.1.call-update) | async-done | bytes 8388624 | tf_op jit(solution)/shard_map/all_gather | solution.py:63
  89.1 6.3 %multiply_reduce_fusion = (f32[512]{0:T(512)S(1)}, bf16[512,128]{0,1:T(8,128)(2,1)S(1)}) fusion(bf16[512,128]{0,1:T(8,128)(2,1)S(1)} %copy.52, bf16[512,8192]{1,0:T(8,128)(2,1)} %all-gather.2.cloned.1.call-done, bf16[128,8192]{1,0:T(8,128)(2,1)S(1)} %copy-done), kind=kOutput, calls=%fused_computation.53 | convolution fusion | flops 1074068992 | bytes 10749952 | tf_op jit(solution)/shard_map/dot_general | solution.py:62
  96.3 8.3 %scatter_custom_fusion.3 = f32[4096]{0:T(1024)S(1)} fusion(s32[2048]{0:T(1024)} %copy-done.3, f32[2048]{0:T(1024)} %reshape.313, f32[]{:T(128)} %constant.36.clone.1), kind=kCustom, calls=%fused_computation.64 | custom fusion | bytes 16896
  106.3 1.9 all-to-all-done
  108.1 10.4 %all-to-all-start.3 = ((f32[16,1,256]{2,1,0:T(1,128)}), f32[16,1,256]{2,1,0:T(1,128)S(1)}, u32[]{:S(2)}, u32[]{:S(2)}) async-start(f32[16,1,256]{2,1,0:T(1,128)} %reshape.338), calls=%async_computation.3 | async-start | bytes 32768 | tf_op jit(solution)/shard_map/all_to_all | solution.py:83
  119.6 7.2 %scatter_custom_fusion.2 = bf16[4096,128]{1,0:T(8,128)(2,1)} fusion(s32[2048]{0:T(1024)} %copy-done.3, bf16[2048,128]{1,0:T(8,128)(2,1)} %bitcast.123, bf16[]{:T(256)} %constant.24.clone.1), kind=kCustom, calls=%fused_computation.44 | custom fusion | bytes 1049088
  126.8 4.2 %all-to-all-done.3 = f32[16,1,256]{2,1,0:T(1,128)S(1)} async-done(((f32[16,1,256]{2,1,0:T(1,128)}), f32[16,1,256]{2,1,0:T(1,128)S(1)}, u32[]{:S(2)}, u32[]{:S(2)}) %all-to-all-start.3) | async-done | bytes 16416 | tf_op jit(solution)/shard_map/all_to_all | solution.py:83
  131.1 7.8 %all-to-all-start.2 = ((bf16[1,128,32,128]{3,2,0,1:T(8,128)(2,1)}), bf16[1,128,32,128]{3,2,0,1:T(8,128)(2,1)}, u32[]{:S(2)}, u32[]{:S(2)}) async-start(bf16[1,128,32,128]{3,2,0,1:T(8,128)(2,1)} %bitcast.116), calls=%async_computation.2 | async-start | bytes 2097152 | tf_op jit(solution)/shard_map/all_to_all | solution.py:79
  138.9 1.4 reduce.20
  142.6 46.2 %all-to-all-done.2 = bf16[1,128,32,128]{3,2,0,1:T(8,128)(2,1)} async-done(((bf16[1,128,32,128]{3,2,0,1:T(8,128)(2,1)}), bf16[1,128,32,128]{3,2,0,1:T(8,128)(2,1)}, u32[]{:S(2)}, u32[]{:S(2)}) %all-to-all-start.2) | async-done | bytes 1048608 | tf_op jit(solution)/shard_map/all_to_all | solution.py:79
  188.8 2.4 copy.51
  191.1 38.2 %while.11 = (s32[]{:T(128)}, bf16[8,512,128]{2,1,0:T(8,128)(2,1)}, s32[8]{0:T(128)S(1)}, bf16[8,512,128]{2,1,0:T(8,128)(2,1)}, bf16[8,512,128]{2,1,0:T(8,128)(2,...) while((s32[]{:T(128)}, bf16[8,512,128]{2,1,0:T(8,128)(2,1)}, ...), condition=%wide.region_11.12_spmd.clone, body=%wide.region_10.11_spmd.clone.sunk | while | flops 203031040 | bytes 2900097 | solution.py:111
  193.7 2.2 fusion.61
  198.4 2.2 fusion.61
  203.2 2.2 fusion.61
  208.0 2.2 fusion.61
  212.8 2.2 fusion.61
  217.6 2.2 fusion.61
  222.3 2.2 fusion.61
  227.1 2.2 fusion.61
  229.4 2.9 copy.60
  232.2 7.9 %all-to-all-start.4 = ((bf16[1,8,512,128]{3,1,0,2:T(8,128)(2,1)}), bf16[1,8,512,128]{3,1,0,2:T(8,128)(2,1)S(1)}, u32[]{:S(2)}, u32[]{:S(2)}) async-start(bf16[1,8,512,128]{3,1,0,2:T(8,128)(2,1)} %bitcast.118), calls=%async_computation.4 | async-start | bytes 2097152 | tf_op jit(solution)/shard_map/all_to_all | solution.py:123
  240.2 50.1 %all-to-all-done.4 = bf16[1,8,512,128]{3,1,0,2:T(8,128)(2,1)S(1)} async-done(((bf16[1,8,512,128]{3,1,0,2:T(8,128)(2,1)}), bf16[1,8,512,128]{3,1,0,2:T(8,128)(2,1)S(1)}, u32[]{:S(2)}, u32[]{:S(2)}) %all-to-all-start.4) | async-done | bytes 1048608 | tf_op jit(solution)/shard_map/all_to_all | solution.py:123
  291.3 1.5 copy.56
  292.7 17.6 %gather_fusion = bf16[2048,128]{1,0:T(8,128)(2,1)} fusion(bf16[1,4096,128]{2,1,0:T(8,128)(2,1)S(1)} %bitcast.113, s32[2048]{0:T(1024)S(1)} %bitcast.112), kind=kCustom, calls=%fused_computation | custom fusion | bytes 1064960 | tf_op jit(solution)/shard_map/vmap()/gather | solution.py:133
  310.3 2.3 reduce_sum.55
  (84 shorter events, 36.5 us)
Async XLA Ops:
  6.5 82.6 %copy-start = (bf16[128,8192]{1,0:T(8,128)(2,1)S(1)}, bf16[128,8192]{1,0:T(8,128)(2,1)}, u32[]{:S(2)}) copy-start(bf16[128,8192]{1,0:T(8,128)(2,1)} %param.15) | copy-start | bytes 6291460
  6.5 82.6 %all-gather.2.cloned.1.call-start = ((), (), s32[]{:S(2)}) async-start(), calls=%async_computation.5 | async-start | bytes 8650752 | tf_op jit(solution)/shard_map/all_gather | solution.py:63
  12.8 38.0 %copy-start.3 = (s32[2048]{0:T(1024)}, s32[2048]{0:T(1024)S(1)}, u32[]{:S(2)}) copy-start(s32[2048]{0:T(1024)S(1)} %broadcast_select_fusion) | copy-start | bytes 24580
  23.0 27.7 %all-to-all-start.1 = ((f32[16,1,256]{2,1,0:T(1,128)}), f32[16,1,256]{2,1,0:T(1,128)S(1)}, u32[]{:S(2)}, u32[]{:S(2)}) async-start(f32[16,1,256]{2,1,0:T(1,128)} %reshape.336), calls=%async_computation.1 | async-start | bytes 32768 | tf_op jit(solution)/shard_map/all_to_all | solution.py:82
  50.7 0.6 copy-start.2
  51.3 56.8 %all-to-all-start = ((bf16[1,128,32,128]{3,2,0,1:T(8,128)(2,1)}), bf16[1,128,32,128]{3,2,0,1:T(8,128)(2,1)S(1)}, u32[]{:S(2)}, u32[]{:S(2)}) async-start(bf16[1,128,32,128]{3,2,0,1:T(8,128)(2,1)} %bitcast.115), calls=%async_computation | async-start | bytes 2097152 | tf_op jit(solution)/shard_map/all_to_all | solution.py:78
  96.3 94.8 %copy-start.4 = (s32[1,8]{1,0:T(1,128)S(1)}, s32[1,8]{1,0:T(1,128)}, u32[]{:S(2)}) copy-start(s32[1,8]{1,0:T(1,128)} %param.19) | copy-start | bytes 100
  108.1 22.9 %all-to-all-start.3 = ((f32[16,1,256]{2,1,0:T(1,128)}), f32[16,1,256]{2,1,0:T(1,128)S(1)}, u32[]{:S(2)}, u32[]{:S(2)}) async-start(f32[16,1,256]{2,1,0:T(1,128)} %reshape.338), calls=%async_computation.3 | async-start | bytes 32768 | tf_op jit(solution)/shard_map/all_to_all | solution.py:83
  131.1 57.7 %all-to-all-start.2 = ((bf16[1,128,32,128]{3,2,0,1:T(8,128)(2,1)}), bf16[1,128,32,128]{3,2,0,1:T(8,128)(2,1)}, u32[]{:S(2)}, u32[]{:S(2)}) async-start(bf16[1,128,32,128]{3,2,0,1:T(8,128)(2,1)} %bitcast.116), calls=%async_computation.2 | async-start | bytes 2097152 | tf_op jit(solution)/shard_map/all_to_all | solution.py:79
  232.2 58.0 %all-to-all-start.4 = ((bf16[1,8,512,128]{3,1,0,2:T(8,128)(2,1)}), bf16[1,8,512,128]{3,1,0,2:T(8,128)(2,1)S(1)}, u32[]{:S(2)}, u32[]{:S(2)}) async-start(bf16[1,8,512,128]{3,1,0,2:T(8,128)(2,1)} %bitcast.118), calls=%async_computation.4 | async-start | bytes 2097152 | tf_op jit(solution)/shard_map/all_to_all | solution.py:123
  290.3 1.0 copy-start.1
Sparse Core Ops, SparseCore 0:
  10.4 78.6 all-gather.1
where the time goes:
time: 321 us; the launch traced here: 320 us
  waiting for transfers between devices  137 us (43%)
  local copies, waits for them, and re-layouts  70.2 us (22%)
  starting transfers between devices  48.8 us (15%)
  matrix products  34.4 us (11%)
  other arithmetic  15.3 us (5%)
  between operations  13.7 us (4%)
    all_to_all x1, waiting for transfers between devices, shards(): lax.all_to_all(partials.reshape(head_count, local_clusters, arrivals, hea...  50.1 us
    all_to_all x1, waiting for transfers between devices, shards(): lax.all_to_all(grad_slots, 'grp', split_axis=1, concat_axis=2, tiled=True)  46.2 us
    unnamed x20, local copies, waits for them, and re-layouts  35.4 us
    all_gather x1, waiting for transfers between devices, shards(): lax.all_gather(readout_grad, 'pb', axis=1, tiled=True)  29.3 us
    dot_general x8, matrix products, block_grad(): jnp.dot(grad_score, key_block, preferred_element_type=jnp.float32)  17.9 us
    gather x1, local copies, waits for them, and re-layouts, pick_head(): return returned_head[place_head_ids]  17.6 us
    all_to_all x1, starting transfers between devices, shards(): lax.all_to_all(norm_slots, 'grp', split_axis=1, concat_axis=2, tiled=True)  15.2 us
    all_to_all x1, starting transfers between devices, shards(): lax.all_to_all(delta_slots, 'grp', split_axis=1, concat_axis=2, tiled=True)  10.4 us
  transfers between devices with their start and end apart: 6, of which 6 were waited for; matrix products, arithmetic and copies ran while one was open for 17% of the time, Pallas kernels for 0%

commit v1 on v0

v1 whole, which is shorter than its diff:
```python
import functools

import jax
import jax.numpy as jnp
from jax import lax
from jax.experimental import pallas as pl
from jax.experimental.pallas import tpu as pltpu
from jax.sharding import PartitionSpec as P

F32 = jnp.float32
BF16 = jnp.bfloat16
EXTRA = 8
NT = (((1,), (1,)), ((), ()))
TN = (((0,), (0,)), ((), ()))
VMEM_BYTES = 48 * 1024 * 1024


def params():
    return pltpu.CompilerParams(vmem_limit_bytes=VMEM_BYTES)


def split_rows(row):
    high = row.astype(BF16).astype(F32)
    rest = row - high
    middle = rest.astype(BF16).astype(F32)
    low = (rest - middle).astype(BF16).astype(F32)
    pad = jnp.zeros((EXTRA - 3,) + row.shape[1:], F32)
    return jnp.concatenate([high, middle, low, pad], axis=0)


def store_extra(out_ref, extra, tokens):
    for i in range(0, tokens // 128, 2):
        both = [extra[:, (i + k) * 128 : (i + k + 1) * 128] for k in range(2)]
        start = tokens + i * EXTRA
        out_ref[start : start + 2 * EXTRA, :] = jnp.concatenate(both, axis=0).astype(BF16)


def rank_kernel(probes_ref, table_ref, ranks_ref):
    clusters, tokens = ranks_ref.shape[1:]
    probe_count = probes_ref.shape[1]
    cluster = lax.broadcasted_iota(jnp.int32, (clusters, tokens), 0)
    named = jnp.zeros((clusters, tokens), F32)
    for j in range(probe_count):
        named += jnp.where(probes_ref[0, j : j + 1, :] == cluster, 1.0, 0.0)
    slot = lax.broadcasted_iota(jnp.int32, (clusters, clusters), 0)
    table = jnp.where(table_ref[...] == slot, 1.0, 0.0).astype(BF16)
    marked = jnp.dot(table, named.astype(BF16), preferred_element_type=F32)
    earlier = lax.broadcasted_iota(jnp.int32, (tokens, tokens), 0)
    later = lax.broadcasted_iota(jnp.int32, (tokens, tokens), 1)
    before = jnp.where(earlier < later, 1.0, 0.0).astype(BF16)
    ranking = jnp.dot(marked.astype(BF16), before, preferred_element_type=F32)
    ranks_ref[0] = jnp.where(marked > 0.5, ranking, -1.0)


def rank_slots(probes_t, table):
    blocks, probe_count, tokens = probes_t.shape
    clusters = table.shape[1]
    return pl.pallas_call(
        rank_kernel,
        grid=(blocks,),
        in_specs=[
            pl.BlockSpec((1, probe_count, tokens), lambda b: (b, 0, 0)),
            pl.BlockSpec((1, clusters), lambda b: (0, 0)),
        ],
        out_specs=pl.BlockSpec((1, clusters, tokens), lambda b: (b, 0, 0)),
        out_shape=jax.ShapeDtypeStruct((blocks, clusters, tokens), F32),
        compiler_params=params(),
    )(probes_t, table)


def query_kernel(query_ref, norm_ref, out_ref):
    tokens = query_ref.shape[0]
    out_ref[0:tokens, :] = query_ref[...]
    store_extra(out_ref, split_rows(norm_ref[...]), tokens)


def query_payload(queries, norm_row):
    tokens, width = queries.shape
    return pl.pallas_call(
        query_kernel,
        out_shape=jax.ShapeDtypeStruct((tokens + EXTRA * tokens // 128, width), BF16),
        compiler_params=params(),
    )(queries, norm_row)


def grad_kernel(readout_ref, weight_ref, outputs_ref, out_ref, total_ref):
    step = pl.program_id(0)
    tokens = outputs_ref.shape[0]
    pieces, _, piece = readout_ref.shape

    @pl.when(step == 0)
    def _():
        total_ref[...] = jnp.zeros_like(total_ref)

    total = total_ref[...]
    for i in range(pieces):
        total += lax.dot_general(
            readout_ref[i],
            weight_ref[:, i * piece : (i + 1) * piece],
            NT,
            preferred_element_type=F32,
        )
    total_ref[...] = total

    @pl.when(step == pl.num_programs(0) - 1)
    def _():
        grad = total.astype(BF16)
        out_ref[0:tokens, :] = grad
        product = grad.astype(F32) * outputs_ref[...].astype(F32)
        delta = jnp.sum(product.T, axis=0, keepdims=True)
        store_extra(out_ref, split_rows(delta), tokens)


def grad_payload(readout, weight, outputs):
    shards_of, tokens, piece = readout.shape
    width = weight.shape[0]
    per_step = 4
    return pl.pallas_call(
        grad_kernel,
        grid=(shards_of // per_step,),
        in_specs=[
            pl.BlockSpec((per_step, tokens, piece), lambda i: (i, 0, 0)),
            pl.BlockSpec((width, per_step * piece), lambda i: (0, i)),
            pl.BlockSpec((tokens, width), lambda i: (0, 0)),
        ],
        out_specs=pl.BlockSpec((tokens + EXTRA * tokens // 128, width), lambda i: (0, 0)),
        out_shape=jax.ShapeDtypeStruct((tokens + EXTRA * tokens // 128, width), BF16),
        scratch_shapes=[pltpu.VMEM((tokens, width), F32)],
        compiler_params=params(),
    )(readout, weight, outputs)


def choices(ranks, capacity):
    slots, tokens = ranks.shape
    place = lax.broadcasted_iota(jnp.int32, (capacity, tokens), 0).astype(F32)
    rows = [jnp.where(ranks[s : s + 1, :] == place, 1.0, 0.0) for s in range(slots)]
    return jnp.concatenate(rows, axis=0).astype(BF16)


def gather_kernel(capacity, owners_ref, ranks_ref, payload_ref, out_ref):
    del owners_ref
    tokens = ranks_ref.shape[2]
    chosen = choices(ranks_ref[0], capacity)
    picked = chosen.shape[0]
    out_ref[0, 0, 0:picked, :] = jnp.dot(
        chosen, payload_ref[0, 0:tokens, :], preferred_element_type=F32
    ).astype(BF16)
    parts = [
        payload_ref[0, tokens + i * 2 * EXTRA : tokens + (i + 1) * 2 * EXTRA, :].astype(F32)
        for i in range(tokens // 256)
    ]
    wide = [part[k * EXTRA : (k + 1) * EXTRA] for part in parts for k in range(2)]
    extra = jnp.concatenate(wide, axis=1).astype(BF16)
    moved = lax.dot_general(extra, chosen, NT, preferred_element_type=F32)
    both = [moved[:, i * 128 : (i + 1) * 128] for i in range(picked // 128)]
    out_ref[0, 0, picked:, :] = jnp.concatenate(both, axis=0).astype(BF16)


def gather_rows(owners, ranks, payload, local_clusters, capacity):
    blocks, _, tokens = ranks.shape
    rows, width = payload.shape[1:]
    picked = local_clusters * capacity
    out_rows = picked + EXTRA * picked // 128
    return pl.pallas_call(
        functools.partial(gather_kernel, capacity),
        grid_spec=pltpu.PrefetchScalarGridSpec(
            num_scalar_prefetch=1,
            grid=(blocks, owners.shape[0]),
            in_specs=[
                pl.BlockSpec((1, local_clusters, tokens), lambda b, i, own: (b, own[i], 0)),
                pl.BlockSpec((1, rows, width), lambda b, i, own: (b, 0, 0)),
            ],
            out_specs=pl.BlockSpec((1, 1, out_rows, width), lambda b, i, own: (i, b, 0, 0)),
        ),
        out_shape=jax.ShapeDtypeStruct((owners.shape[0], blocks, out_rows, width), BF16),
        compiler_params=params(),
    )(owners, ranks, payload)


def scatter_kernel(capacity, owners_ref, ranks_ref, partial_ref, out_ref, total_ref):
    del owners_ref
    step = pl.program_id(1)
    chosen = choices(ranks_ref[0], capacity)
    added = lax.dot_general(partial_ref[0, 0], chosen, TN, preferred_element_type=F32)

    @pl.when(step == 0)
    def _():
        total_ref[...] = added

    @pl.when(step > 0)
    def _():
        total_ref[...] += added

    @pl.when(step == pl.num_programs(1) - 1)
    def _():
        out_ref[0] = total_ref[...].T.astype(BF16)


def scatter_rows(owners, ranks, partials, capacity):
    blocks, _, tokens = ranks.shape
    _, _, rows, width = partials.shape
    local_clusters = rows // capacity
    return pl.pallas_call(
        functools.partial(scatter_kernel, capacity),
        grid_spec=pltpu.PrefetchScalarGridSpec(
            num_scalar_prefetch=1,
            grid=(blocks, owners.shape[0]),
            in_specs=[
                pl.BlockSpec((1, local_clusters, tokens), lambda b, i, own: (b, own[i], 0)),
                pl.BlockSpec((1, 1, rows, width), lambda b, i, own: (i, b, 0, 0)),
            ],
            out_specs=pl.BlockSpec((1, tokens, width), lambda b, i, own: (b, 0, 0)),
            scratch_shapes=[pltpu.VMEM((width, tokens), F32)],
        ),
        out_shape=jax.ShapeDtypeStruct((blocks, tokens, width), BF16),
        compiler_params=params(),
    )(owners, ranks, partials)


def unpack_extra(extra_ref, rows_ref, capacity):
    senders = extra_ref.shape[0]
    per_row = 128 // capacity
    lane = lax.broadcasted_iota(jnp.int32, (2 * EXTRA, 128), 1) // capacity
    for sub in range(per_row):
        for group in range(senders // per_row):
            total = jnp.zeros((2 * EXTRA, 128), F32)
            for k in range(per_row):
                packed = extra_ref[group * per_row + k].astype(F32)
                turn = (k - sub) * capacity % 128
                if turn:
                    packed = pltpu.roll(packed, turn, 1)
                total += jnp.where(lane == k, packed, 0.0)
            lanes = slice(group * 128, (group + 1) * 128)
            for half in range(2):
                rows = total[half * EXTRA : half * EXTRA + 3]
                cluster = half * per_row + sub
                rows_ref[cluster : cluster + 1, lanes] = rows[0:1] + rows[1:2] + rows[2:3]


def block_kernel(
    capacity,
    counts_ref,
    query_ref,
    query_extra_ref,
    grad_ref,
    grad_extra_ref,
    key_ref,
    value_ref,
    out_ref,
    norm_ref,
    delta_ref,
):
    cluster = pl.program_id(0)
    senders, _, width = query_ref.shape
    span = key_ref.shape[2]
    arrivals = senders * capacity
    score_scale = width ** (-0.5)

    @pl.when(cluster == 0)
    def _():
        unpack_extra(query_extra_ref, norm_ref, capacity)
        unpack_extra(grad_extra_ref, delta_ref, capacity)

    keys, vals = key_ref[0, 0], value_ref[0, 0]
    query = query_ref[...].reshape(arrivals, width)
    grad = grad_ref[...].reshape(arrivals, width)
    scores = lax.dot_general(keys, query, NT, preferred_element_type=F32) * score_scale
    place = lax.broadcasted_iota(jnp.int32, (span, arrivals), 0)
    weights = jnp.where(
        place < counts_ref[cluster], jnp.exp(scores - norm_ref[pl.ds(cluster, 1), :]), 0.0
    )
    grad_prob = lax.dot_general(vals, grad, NT, preferred_element_type=F32)
    grad_score = (weights * (grad_prob - delta_ref[pl.ds(cluster, 1), :])).astype(BF16)
    partial = lax.dot_general(keys, grad_score, TN, preferred_element_type=F32) * score_scale
    out_ref[...] = partial.T.astype(BF16).reshape(senders, capacity, width)


def block_grads(counts, query_rows, grad_rows, keys, values, capacity):
    senders, _, width = query_rows.shape
    local_clusters, span = keys.shape[1:3]
    picked = local_clusters * capacity
    rows = pl.BlockSpec((senders, capacity, width), lambda c, _: (0, c, 0))
    extra = pl.BlockSpec(
        (senders, 2 * EXTRA, width), lambda c, _: (0, picked // (2 * EXTRA), 0)
    )
    stored = pl.BlockSpec((1, 1, span, width), lambda c, _: (0, c, 0, 0))
    return pl.pallas_call(
        functools.partial(block_kernel, capacity),
        grid_spec=pltpu.PrefetchScalarGridSpec(
            num_scalar_prefetch=1,
            grid=(local_clusters,),
            in_specs=[rows, extra, rows, extra, stored, stored],
            out_specs=rows,
            scratch_shapes=[pltpu.VMEM((local_clusters, senders * capacity), F32)] * 2,
        ),
        out_shape=jax.ShapeDtypeStruct((senders, picked, width), BF16),
        compiler_params=params(),
    )(counts, query_rows, query_rows, grad_rows, grad_rows, keys, values)


def shards(
    queries,
    outputs,
    readout_grad,
    readout_weight,
    log_norm,
    probes,
    owner_slots,
    counts,
    cluster_keys,
    values,
):
    token_count = queries.shape[0]
    probe_count = probes.shape[2]
    local_clusters = cluster_keys.shape[1]
    clusters = owner_slots.shape[1]
    capacity = 2 * token_count * probe_count // clusters
    owners = jnp.arange(lax.axis_size("grp"), dtype=jnp.int32)

    readout = lax.all_gather(readout_grad, "pb")
    ranks = rank_slots(probes.transpose(0, 2, 1), owner_slots)

    def dispatch(payload):
        rows = gather_rows(owners, ranks, payload[None], local_clusters, capacity)[:, 0]
        return lax.all_to_all(rows, "grp", split_axis=0, concat_axis=0)

    query_rows = dispatch(query_payload(queries, log_norm.reshape(1, token_count)))
    grad_rows = dispatch(grad_payload(readout, readout_weight, outputs))
    partials = block_grads(
        counts.reshape(local_clusters), query_rows, grad_rows, cluster_keys, values, capacity
    )
    returned = lax.all_to_all(partials, "grp", split_axis=0, concat_axis=0)
    return scatter_rows(owners, ranks, returned[:, None], capacity)[0]


def solution(mesh):
    placed = (
        P("grp", "pb"),
        P("grp", "pb"),
        P("grp", "pb"),
        P("pb", None),
        P("grp", "pb"),
        P("pb", "grp", None),
        P("pb", None),
        P("pb", "grp"),
        P("pb", "grp", None, None),
        P("pb", "grp", None, None),
    )
    return jax.shard_map(
        shards, mesh=mesh, in_specs=placed, out_specs=P("grp", "pb"), check_vma=False
    )
```

time: 321 us -> 241 us (0.75)
  blocking collectives: 0 us -> 125 us
  waiting for transfers between devices: 137 us -> 49.8 us
  local copies, waits for them, and re-layouts: 70.2 us -> 4.55 us
  matrix products: 34.4 us -> 0 us
  starting transfers between devices: 48.8 us -> 15.3 us
  Pallas kernels: 0 us -> 32.4 us
  other arithmetic: 15.3 us -> 0 us
    all_to_all x0 -> x2, blocking collectives: none -> 125 us  [the longest x1 70 us: dispatch(): return lax.all_to_all(rows, 'grp', split_axis=0, concat_axis=0)]
    all_to_all x5 -> x1, waiting for transfers between devices: 107 us -> 0.01 us  [dispatch(): return lax.all_to_all(rows, 'grp', split_axis=0, concat_axis=0)]
    dot_general x17 -> x0, matrix products: 34.4 us -> none  [the longest x8 17.9 us: block_grad(): jnp.dot(grad_score, key_block, preferred_element_type=jnp.float32)]
    all_to_all x5 -> x1, starting transfers between devices: 48.8 us -> 15.3 us  [dispatch(): return lax.all_to_all(rows, 'grp', split_axis=0, concat_axis=0)]
    pallas_call x0 -> x7, Pallas kernels: none -> 32.4 us  [the longest x2 11.9 us: gather_rows(): pl.pallas_call(functools.partial(gather_kernel, capacity), grid_spec=pltp...]
    unnamed x20 -> x18, local copies, waits for them, and re-layouts: 35.4 us -> 4.54 us
    all_gather x1, waiting for transfers between devices: 29.3 us -> 49.1 us  [shards(): readout = lax.all_gather(readout_grad, 'pb')]
    gather x1 -> x0, local copies, waits for them, and re-layouts: 17.6 us -> none  [pick_head(): return returned_head[place_head_ids]]
  transfers between devices with their start and end apart: 6 -> 2, of which waited for: 6 -> 1; matrix products, arithmetic and copies ran while one was open for 17% -> 0% of each run, Pallas kernels for 0% -> 8%
where the time goes in v1:
time: 241 us; the launch traced here: 240 us
  blocking collectives  125 us (52%)
  waiting for transfers between devices  49.8 us (21%)
  Pallas kernels  32.4 us (13%)
  starting transfers between devices  15.3 us (6%)
  between operations  13.5 us (6%)
  local copies, waits for them, and re-layouts  4.55 us (2%)
    all_to_all x1, blocking collectives, dispatch(): return lax.all_to_all(rows, 'grp', split_axis=0, concat_axis=0)  70 us
    all_to_all x1, blocking collectives, shards(): returned = lax.all_to_all(partials, 'grp', split_axis=0, concat_axis=0)  54.6 us
    all_gather x1, waiting for transfers between devices, shards(): readout = lax.all_gather(readout_grad, 'pb')  49.1 us
    all_to_all x1, starting transfers between devices, dispatch(): return lax.all_to_all(rows, 'grp', split_axis=0, concat_axis=0)  15.3 us
    pallas_call x2, Pallas kernels, gather_rows(): pl.pallas_call(functools.partial(gather_kernel, capacity), grid_spec=pltp...  11.9 us
    pallas_call x1, Pallas kernels, grad_payload(): pl.pallas_call(grad_kernel, grid=(shards_of // per_step,), in_specs=[pl.B...  7.54 us
    pallas_call x1, Pallas kernels, block_grads(): pl.pallas_call(functools.partial(block_kernel, capacity), grid_spec=pltpu...  7.28 us
    pallas_call x1, Pallas kernels, scatter_rows(): pl.pallas_call(functools.partial(scatter_kernel, capacity), grid_spec=plt...  5.25 us
  transfers between devices with their start and end apart: 2, of which 1 were waited for; matrix products, arithmetic and copies ran while one was open for 0% of the time, Pallas kernels for 8%

profile of v1, /device:TPU:24, one launch (start us, length us, event | category | flops | bytes accessed | tf_op | source)
XLA Modules:
  0.0 240.2 jit_solution(7192273044051954499)
XLA Ops:
  6.5 0.0 all-gather.3.cloned.1.call-start
  6.5 0.7 all-gather.3.cloned.1.call-update
  7.3 0.0 copy-start.4
  7.3 0.9 copy-done.4
  8.2 0.0 copy-start.6
  8.2 0.7 copy-done.6
  8.9 0.0 copy-start.5
  8.9 0.7 copy-done.5
  9.6 0.0 copy-start.7
  9.6 0.7 copy-done.7
  10.2 0.4 shard_map.100.ranks_ref
  10.6 7.6 %shard_map.102 = bf16[16,1,272,128]{3,2,1,0:T(8,128)(2,1)} custom-call(s32[16]{0:T(128)S(1)} %iota.8.owners_ref, f32[1,128,512]{2,1,0:T(8,128)S(1)} %shard_map.100.ranks_ref, bf16[1,544,128]{2,1,0:T(8,128)(2,1)S(1)} %bitcast.13), custom_call_target="tpu_custom_call" | custom-call | tf_op jit(solution)/shard_map/pallas_call | solution.py:164
  18.3 0.0 copy-start.3
  18.3 15.3 %all-to-all-start = ((bf16[16,272,128]{2,1,0:T(8,128)(2,1)}), bf16[16,272,128]{2,1,0:T(8,128)(2,1)S(1)}, u32[]{:S(2)}, u32[]{:S(2)}) async-start(bf16[16,272,128]{2,1,0:T(8,128)(2,1)} %bitcast.4), calls=%async_computation | async-start | bytes 2228224 | tf_op jit(solution)/shard_map/all_to_all | solution.py:325
  33.6 49.1 %all-gather.3.cloned.1.call-done = bf16[16384,256]{1,0:T(8,128)(2,1)} async-done(((bf16[512,256]{1,0:T(8,128)(2,1)}), bf16[16384,256]{1,0:T(8,128)(2,1)}) %all-gather.3.cloned.1.call-update) | async-done | bytes 8388624 | tf_op jit(solution)/shard_map/all_gather | solution.py:320
  82.7 0.0 copy-done.3
  82.7 0.0 copy-start
  82.7 1.6 copy-done
  84.3 7.5 %shard_map.103 = bf16[544,128]{1,0:T(8,128)(2,1)S(1)} custom-call(bf16[32,512,256]{2,1,0:T(8,128)(2,1)} %bitcast.17, bf16[128,8192]{1,0:T(8,128)(2,1)S(1)} %copy-done, bf16[512,128]{1,0:T(8,128)(2,1)S(1)} %copy-done.3), custom_call_target="tpu_custom_call" | custom-call | tf_op jit(solution)/shard_map/pallas_call | solution.py:118
  91.9 4.3 %shard_map.104 = bf16[16,1,272,128]{3,2,1,0:T(8,128)(2,1)S(1)} custom-call(s32[16]{0:T(128)S(1)} %iota.9.owners_ref, f32[1,128,512]{2,1,0:T(8,128)S(1)} %shard_map.100.ranks_ref, bf16[1,544,128]{2,1,0:T(8,128)(2,1)S(1)} %bitcast.12), custom_call_target="tpu_custom_call" | custom-call | tf_op jit(solution)/shard_map/pallas_call | solution.py:164
  96.1 0.0 all-to-all-done.query_ref.query_extra_ref
  96.2 0.0 copy-start.1
  96.2 0.0 copy-start.2
  96.2 0.0 copy-start.8
  96.2 70.0 %all_to_all.15.grad_ref.grad_extra_ref = bf16[16,272,128]{2,1,0:T(8,128)(2,1)S(1)} all-to-all(bf16[16,272,128]{2,1,0:T(8,128)(2,1)S(1)} %bitcast.10), channel_id=1, replica_groups=mesh['grp'=16,'pb'=32] {'grp'}, dimensions={0} | all-to-all | bytes 2228224 | tf_op jit(solution)/shard_map/all_to_all | solution.py:325
  166.2 0.0 copy-done.1
  166.2 0.0 copy-done.2
  166.2 0.0 copy-done.8
  166.2 7.3 %shard_map.105 = bf16[16,256,128]{2,1,0:T(8,128)(2,1)S(1)} custom-call(s32[8]{0:T(128)S(1)} %bitcast.16, bf16[16,272,128]{2,1,0:T(8,128)(2,1)S(1)} %all-to-all-done.query_ref.query_extra_ref, bf16[16,272,128]{2,1,0:T(8,128)(2,1)S(1)} %all-to-all-done.query_ref.query_extra_ref, bf16[16,272,128]{2,1,0:T(8,128)(2,1)S(1)} %all_to_all.15.grad_ref.grad_extra_ref, ...), custom_call_target="tpu_custom_call" | custom-call | tf_op jit(solution)/shard_map/pallas_call | solution.py:287
  173.5 54.6 %all_to_all.16 = bf16[16,256,128]{2,1,0:T(8,128)(2,1)S(1)} all-to-all(bf16[16,256,128]{2,1,0:T(8,128)(2,1)S(1)} %shard_map.105), channel_id=1, replica_groups=mesh['grp'=16,'pb'=32] {'grp'}, dimensions={0} | all-to-all | bytes 2097152 | tf_op jit(solution)/shard_map/all_to_all | solution.py:332
  228.1 5.2 %shard_map.106 = bf16[1,512,128]{2,1,0:T(8,128)(2,1)} custom-call(s32[16]{0:T(128)S(1)} %iota.7.owners_ref, f32[1,128,512]{2,1,0:T(8,128)S(1)} %shard_map.100.ranks_ref, bf16[16,1,256,128]{3,2,1,0:T(8,128)(2,1)S(1)} %bitcast.11), custom_call_target="tpu_custom_call" | custom-call | tf_op jit(solution)/shard_map/pallas_call | solution.py:203
  (4 shorter events, 0.0 us)
Async XLA Ops:
  6.5 76.2 %all-gather.3.cloned.1.call-start = ((), (), s32[]{:S(2)}) async-start(), calls=%async_computation.3 | async-start | bytes 8650752 | tf_op jit(solution)/shard_map/all_gather | solution.py:320
  7.3 0.9 copy-start.4
  8.2 0.7 copy-start.6
  8.9 0.7 copy-start.5
  9.6 0.7 copy-start.7
  18.3 64.5 %copy-start.3 = (bf16[512,128]{1,0:T(8,128)(2,1)S(1)}, bf16[512,128]{1,0:T(8,128)(2,1)}, u32[]{:S(2)}) copy-start(bf16[512,128]{1,0:T(8,128)(2,1)} %outputs_ref.1) | copy-start | bytes 393220
  18.3 77.9 %all-to-all-start = ((bf16[16,272,128]{2,1,0:T(8,128)(2,1)}), bf16[16,272,128]{2,1,0:T(8,128)(2,1)S(1)}, u32[]{:S(2)}, u32[]{:S(2)}) async-start(bf16[16,272,128]{2,1,0:T(8,128)(2,1)} %bitcast.4), calls=%async_computation | async-start | bytes 2228224 | tf_op jit(solution)/shard_map/all_to_all | solution.py:325
  82.7 1.6 copy-start
  96.2 70.0 %copy-start.1 = (bf16[1,8,512,128]{3,2,1,0:T(8,128)(2,1)S(1)}, bf16[1,8,512,128]{3,2,1,0:T(8,128)(2,1)}, u32[]{:S(2)}) copy-start(bf16[1,8,512,128]{3,2,1,0:T(8,128)(2,1)} %key_ref.1) | copy-start | bytes 3145732
  96.2 70.0 %copy-start.2 = (bf16[1,8,512,128]{3,2,1,0:T(8,128)(2,1)S(1)}, bf16[1,8,512,128]{3,2,1,0:T(8,128)(2,1)}, u32[]{:S(2)}) copy-start(bf16[1,8,512,128]{3,2,1,0:T(8,128)(2,1)} %value_ref.1) | copy-start | bytes 3145732
  96.2 70.0 %copy-start.8 = (s32[1,8]{1,0:T(1,128)S(1)}, s32[1,8]{1,0:T(1,128)}, u32[]{:S(2)}) copy-start(s32[1,8]{1,0:T(1,128)} %param.17) | copy-start | bytes 100
Sparse Core Ops, SparseCore 0:
  10.5 72.1 all-gather.2

commit v2 on v1

v2 whole, which is shorter than its diff:
```python
import functools

import jax
import jax.numpy as jnp
from jax import lax
from jax.experimental import pallas as pl
from jax.experimental.pallas import tpu as pltpu
from jax.sharding import PartitionSpec as P

F32 = jnp.float32
BF16 = jnp.bfloat16
EXTRA = 8
NT = (((1,), (1,)), ((), ()))
TN = (((0,), (0,)), ((), ()))
SIDE, CORES = 4, 2
TURNS = (1, 3, 2)
SHARED = 4
NEAR = ((1, 1), (-1, -1), (2, -2))
VMEM_BYTES = 48 * 1024 * 1024


def params():
    return pltpu.CompilerParams(vmem_limit_bytes=VMEM_BYTES)


def split_rows(row):
    high = row.astype(BF16).astype(F32)
    rest = row - high
    middle = rest.astype(BF16).astype(F32)
    low = (rest - middle).astype(BF16).astype(F32)
    pad = jnp.zeros((EXTRA - 3,) + row.shape[1:], F32)
    return jnp.concatenate([high, middle, low, pad], axis=0)


def store_extra(out_ref, extra, tokens):
    for i in range(0, tokens // 128, 2):
        both = [extra[:, (i + k) * 128 : (i + k + 1) * 128] for k in range(2)]
        start = tokens + i * EXTRA
        out_ref[start : start + 2 * EXTRA, :] = jnp.concatenate(both, axis=0).astype(BF16)


def probe_rows(packed, tokens):
    packed, pieces = packed.astype(F32), tokens // 128
    return [
        jnp.concatenate([packed[j + i : j + i + 1] for i in range(pieces)], axis=1)
        for j in range(0, packed.shape[0], pieces)
    ]


def earlier_tokens(tokens):
    earlier = lax.broadcasted_iota(jnp.int32, (tokens, tokens), 0)
    later = lax.broadcasted_iota(jnp.int32, (tokens, tokens), 1)
    return jnp.where(earlier < later, 1.0, 0.0).astype(BF16)


def rank_kernel(table_ref, held_ref, packed_ref, ranks_ref):
    blocks, clusters, tokens = ranks_ref.shape
    cluster = lax.broadcasted_iota(jnp.int32, (clusters, tokens), 0).astype(F32)
    slot = lax.broadcasted_iota(jnp.int32, (clusters, clusters), 0)
    table = jnp.where(table_ref[...] == slot, 1.0, 0.0).astype(BF16)
    before = earlier_tokens(tokens)
    for b in range(blocks):
        named = jnp.zeros((clusters, tokens), F32)
        for row in probe_rows(packed_ref[held_ref[b]], tokens):
            named += jnp.where(row == cluster, 1.0, 0.0)
        marked = jnp.dot(table, named.astype(BF16), preferred_element_type=F32)
        ranking = jnp.dot(marked.astype(BF16), before, preferred_element_type=F32)
        ranks_ref[b] = jnp.where(marked > 0.5, ranking, -1.0)


def rank_slots(held, packed, table, tokens):
    blocks, clusters = held.shape[0], table.shape[1]
    return pl.pallas_call(
        rank_kernel,
        in_specs=[
            pl.BlockSpec(memory_space=pltpu.VMEM),
            pl.BlockSpec(memory_space=pltpu.SMEM),
            pl.BlockSpec(memory_space=pltpu.VMEM),
        ],
        out_shape=jax.ShapeDtypeStruct((blocks, clusters, tokens), F32),
        compiler_params=params(),
    )(table, held, packed)


def query_kernel(query_ref, norm_ref, probes_ref, out_ref):
    tokens = query_ref.shape[0]
    pieces = tokens // 128
    out_ref[0:tokens, :] = query_ref[...]
    store_extra(out_ref, split_rows(norm_ref[...]), tokens)
    probes = probes_ref[...].astype(F32)
    rows = [
        probes[j : j + 1, i * 128 : (i + 1) * 128]
        for j in range(probes.shape[0])
        for i in range(pieces)
    ]
    out_ref[tokens + EXTRA * pieces :, :] = jnp.concatenate(rows, axis=0).astype(BF16)


def query_payload(queries, norm_row, probes_t):
    tokens, width = queries.shape
    rows = tokens + (EXTRA + probes_t.shape[0]) * tokens // 128
    return pl.pallas_call(
        query_kernel,
        out_shape=jax.ShapeDtypeStruct((rows, width), BF16),
        compiler_params=params(),
    )(queries, norm_row, probes_t)


def weight_kernel(core_ref, weight_ref, own_ref, other_ref):
    pieces, _, piece = own_ref.shape
    core = core_ref[0]
    for i in range(pieces):
        for ref, side in ((own_ref, core), (other_ref, 1 - core)):
            start = pl.multiple_of((2 * i + side) * piece, piece)
            ref[i] = weight_ref[:, pl.ds(start, piece)]


def split_weight(core, weight, piece):
    width, depth = weight.shape
    half = jax.ShapeDtypeStruct((depth // piece // 2, width, piece), BF16)
    return pl.pallas_call(
        weight_kernel,
        in_specs=[
            pl.BlockSpec(memory_space=pltpu.SMEM),
            pl.BlockSpec(memory_space=pltpu.VMEM),
        ],
        out_shape=[half, half],
        compiler_params=params(),
    )(core, weight)


def product_kernel(first, count, added, order_ref, own_ref, other_ref, *refs):
    pieces, sums, results = refs[:count], refs[count : count + added], refs[count + added :]
    rows = results[0].shape[0] // 2
    for half in range(2):
        span = slice(half * rows, (half + 1) * rows)
        total = None
        for k, ref in enumerate(pieces):
            for m in range(ref.shape[0]):
                shard = order_ref[(first + k) * ref.shape[0] + m]
                both = jnp.concatenate([own_ref[shard], other_ref[shard]], axis=0)
                term = lax.dot_general(ref[m, span, :], both, NT, preferred_element_type=F32)
                total = term if total is None else total + term
        width = total.shape[1] // 2
        for i, out_ref in enumerate(results):
            part = total[:, i * width : (i + 1) * width]
            out_ref[span, :] = part + sums[i][span, :] if added else part


def partial_product(first, order, own, other, pieces, sums):
    result = jax.ShapeDtypeStruct((pieces[0].shape[1], own.shape[1]), F32)
    return pl.pallas_call(
        functools.partial(product_kernel, first, len(pieces), len(sums)),
        in_specs=[pl.BlockSpec(memory_space=pltpu.SMEM)]
        + [pl.BlockSpec(memory_space=pltpu.VMEM)] * (2 + len(pieces) + len(sums)),
        out_shape=[result, result],
        compiler_params=params(),
    )(order, own, other, *pieces, *sums)


def grad_kernel(own_ref, other_ref, outputs_ref, out_ref):
    tokens = outputs_ref.shape[0]
    grad = (own_ref[...] + other_ref[...]).astype(BF16)
    out_ref[0:tokens, :] = grad
    product = grad.astype(F32) * outputs_ref[...].astype(F32)
    delta = jnp.sum(product.T, axis=0, keepdims=True)
    store_extra(out_ref, split_rows(delta), tokens)


def grad_payload(own, other, outputs):
    tokens, width = outputs.shape
    return pl.pallas_call(
        grad_kernel,
        out_shape=jax.ShapeDtypeStruct((tokens + EXTRA * tokens // 128, width), BF16),
        compiler_params=params(),
    )(own, other, outputs)


def choices(ranks, capacity):
    slots, tokens = ranks.shape
    place = lax.broadcasted_iota(jnp.int32, (capacity, tokens), 0).astype(F32)
    rows = [jnp.where(ranks[s : s + 1, :] == place, 1.0, 0.0) for s in range(slots)]
    return jnp.concatenate(rows, axis=0).astype(BF16)


def owner_ranks(ranks_ref, block, owner, local_clusters):
    start = pl.multiple_of(owner * local_clusters, local_clusters)
    return ranks_ref[block, pl.ds(start, local_clusters), :]


def pick_rows(payload_ref, chosen, tokens, out_ref):
    picked = chosen.shape[0]
    parts = [
        payload_ref[tokens + i * 2 * EXTRA : tokens + (i + 1) * 2 * EXTRA, :].astype(F32)
        for i in range(tokens // 256)
    ]
    wide = [part[k * EXTRA : (k + 1) * EXTRA] for part in parts for k in range(2)]
    extra = jnp.concatenate(wide, axis=1).astype(BF16)
    out_ref[0:picked, :] = jnp.dot(
        chosen, payload_ref[0:tokens, :], preferred_element_type=F32
    ).astype(BF16)
    moved = lax.dot_general(extra, chosen, NT, preferred_element_type=F32)
    both = [moved[:, k * 128 : (k + 1) * 128] for k in range(picked // 128)]
    out_ref[picked:, :] = jnp.concatenate(both, axis=0).astype(BF16)


def gather_kernel(capacity, local_clusters, owners_ref, ranks_ref, payload_ref, *refs):
    blocks, _, tokens = ranks_ref.shape
    for b in range(blocks):
        for i, out_ref in enumerate(refs):
            chosen = choices(
                owner_ranks(ranks_ref, b, owners_ref[i], local_clusters), capacity
            )
            pick_rows(payload_ref.at[b], chosen, tokens, out_ref.at[b])


def gather_rows(owners, ranks, payloads, local_clusters, capacity):
    blocks, width = ranks.shape[0], payloads.shape[-1]
    picked = local_clusters * capacity
    rows = jax.ShapeDtypeStruct((blocks, picked + EXTRA * picked // 128, width), BF16)
    return pl.pallas_call(
        functools.partial(gather_kernel, capacity, local_clusters),
        in_specs=[pl.BlockSpec(memory_space=pltpu.SMEM)]
        + [pl.BlockSpec(memory_space=pltpu.VMEM)] * 2,
        out_shape=[rows] * owners.shape[0],
        compiler_params=params(),
    )(owners, ranks, payloads)


def own_kernel(capacity, tokens, group_ref, sources_ref, table_ref, payload_ref, *refs):
    sides = sources_ref.shape[0]
    blocks, out_rows, _ = refs[0].shape
    local_clusters = out_rows * 128 // (128 + EXTRA) // capacity
    clusters = table_ref.shape[1]
    slot = lax.broadcasted_iota(jnp.int32, (local_clusters, clusters), 0)
    cluster = lax.broadcasted_iota(jnp.int32, (local_clusters, clusters), 1)
    mine = table_ref[...] == slot + group_ref[0] * local_clusters
    stored = jnp.sum(jnp.where(mine, cluster.astype(F32), 0.0), axis=1, keepdims=True)
    start = tokens + EXTRA * tokens // 128
    marks = []
    for i in range(sides):
        for b in range(blocks):
            packed = payload_ref[sources_ref[i, b], start:, :]
            named = jnp.zeros((local_clusters, tokens), F32)
            for row in probe_rows(packed, tokens):
                named += jnp.where(row == stored, 1.0, 0.0)
            marks.append(named)
    marks = jnp.concatenate(marks, axis=0)
    ranking = jnp.dot(marks.astype(BF16), earlier_tokens(tokens), preferred_element_type=F32)
    ranks = jnp.where(marks > 0.5, ranking, -1.0)
    for i in range(sides):
        for b in range(blocks):
            first = (i * blocks + b) * local_clusters
            chosen = choices(ranks[first : first + local_clusters], capacity)
            pick_rows(payload_ref.at[sources_ref[i, b]], chosen, tokens, refs[i].at[b])


def own_rows(group, sources, table, payloads, tokens, local_clusters, capacity):
    sides, blocks = sources.shape
    picked = local_clusters * capacity
    width = payloads.shape[-1]
    rows = jax.ShapeDtypeStruct((blocks, picked + EXTRA * picked // 128, width), BF16)
    return pl.pallas_call(
        functools.partial(own_kernel, capacity, tokens),
        in_specs=[pl.BlockSpec(memory_space=pltpu.SMEM)] * 2
        + [pl.BlockSpec(memory_space=pltpu.VMEM)] * 2,
        out_shape=[rows] * sides,
        compiler_params=params(),
    )(group, sources, table, payloads)


def scatter_kernel(capacity, owners_ref, ranks_ref, *refs):
    partial_refs, out_ref = refs[:-1], refs[-1]
    local_clusters = partial_refs[0].shape[1] // capacity
    for b in range(ranks_ref.shape[0]):
        total = None
        for i, partial_ref in enumerate(partial_refs):
            chosen = choices(
                owner_ranks(ranks_ref, b, owners_ref[i], local_clusters), capacity
            )
            term = lax.dot_general(partial_ref[b], chosen, TN, preferred_element_type=F32)
            total = term if total is None else total + term
        out_ref[b] = total.T.astype(out_ref.dtype)


def scatter_rows(owners, ranks, partials, capacity):
    blocks, _, tokens = ranks.shape
    width = partials[0].shape[2]
    return pl.pallas_call(
        functools.partial(scatter_kernel, capacity),
        in_specs=[pl.BlockSpec(memory_space=pltpu.SMEM)]
        + [pl.BlockSpec(memory_space=pltpu.VMEM)] * (1 + len(partials)),
        out_shape=jax.ShapeDtypeStruct((blocks, tokens, width), BF16),
        compiler_params=params(),
    )(owners, ranks, *partials)


def unpack_extra(extra_refs, rows_ref, capacity):
    per_ref = extra_refs[0].shape[0]
    senders = per_ref * len(extra_refs)
    per_row = 128 // capacity
    lane = lax.broadcasted_iota(jnp.int32, (2 * EXTRA, 128), 1) // capacity
    for sub in range(per_row):
        for group in range(senders // per_row):
            total = jnp.zeros((2 * EXTRA, 128), F32)
            for k in range(per_row):
                sender = group * per_row + k
                packed = extra_refs[sender // per_ref][sender % per_ref].astype(F32)
                turn = (k - sub) * capacity % 128
                if turn:
                    packed = pltpu.roll(packed, turn, 1)
                total += jnp.where(lane == k, packed, 0.0)
            lanes = slice(group * 128, (group + 1) * 128)
            for half in range(2):
                rows = total[half * EXTRA : half * EXTRA + 3]
                cluster = half * per_row + sub
                rows_ref[cluster : cluster + 1, lanes] = rows[0:1] + rows[1:2] + rows[2:3]


def block_kernel(capacity, sides, counts_ref, *refs):
    query_refs, query_extras = refs[:sides], refs[sides : 2 * sides]
    grad_refs, grad_extras = refs[2 * sides : 3 * sides], refs[3 * sides : 4 * sides]
    key_ref, value_ref = refs[4 * sides : 4 * sides + 2]
    out_refs = refs[4 * sides + 2 : 5 * sides + 2]
    norm_ref, delta_ref = refs[5 * sides + 2 :]
    cluster = pl.program_id(0)
    senders, _, width = query_refs[0].shape
    span = key_ref.shape[2]
    score_scale = width ** (-0.5)
    each = senders * capacity
    arrivals = sides * each

    @pl.when(cluster == 0)
    def _():
        unpack_extra(query_extras, norm_ref, capacity)
        unpack_extra(grad_extras, delta_ref, capacity)

    keys, vals = key_ref[0, 0], value_ref[0, 0]
    query = jnp.concatenate([ref[...].reshape(each, width) for ref in query_refs], axis=0)
    grad = jnp.concatenate([ref[...].reshape(each, width) for ref in grad_refs], axis=0)
    scores = lax.dot_general(keys, query, NT, preferred_element_type=F32) * score_scale
    place = lax.broadcasted_iota(jnp.int32, (span, arrivals), 0)
    weights = jnp.where(
        place < counts_ref[cluster], jnp.exp(scores - norm_ref[pl.ds(cluster, 1), :]), 0.0
    )
    grad_prob = lax.dot_general(vals, grad, NT, preferred_element_type=F32)
    grad_score = (weights * (grad_prob - delta_ref[pl.ds(cluster, 1), :])).astype(BF16)
    partial = lax.dot_general(keys, grad_score, TN, preferred_element_type=F32) * score_scale
    partial = partial.T.astype(BF16)
    for i, out_ref in enumerate(out_refs):
        out_ref[...] = partial[i * each : (i + 1) * each].reshape(senders, capacity, width)


def block_grads(counts, query_rows, grad_rows, keys, values, capacity):
    sides = len(query_rows)
    senders, _, width = query_rows[0].shape
    local_clusters, span = keys.shape[1:3]
    picked = local_clusters * capacity
    rows = pl.BlockSpec((senders, capacity, width), lambda c, _: (0, c, 0))
    extra = pl.BlockSpec(
        (senders, 2 * EXTRA, width), lambda c, _: (0, picked // (2 * EXTRA), 0)
    )
    stored = pl.BlockSpec((1, 1, span, width), lambda c, _: (0, c, 0, 0))
    arrivals = sides * senders * capacity
    return pl.pallas_call(
        functools.partial(block_kernel, capacity, sides),
        grid_spec=pltpu.PrefetchScalarGridSpec(
            num_scalar_prefetch=1,
            grid=(local_clusters,),
            in_specs=([rows] * sides + [extra] * sides) * 2 + [stored, stored],
            out_specs=[rows] * sides,
            scratch_shapes=[pltpu.VMEM((local_clusters, arrivals), F32)] * 2,
        ),
        out_shape=[jax.ShapeDtypeStruct((senders, picked, width), BF16)] * sides,
        compiler_params=params(),
    )(counts, *query_rows, *query_rows, *grad_rows, *grad_rows, keys, values)


def plane_shift(array, turn, phase):
    pairs = []
    for x in range(SIDE):
        for y in range(SIDE):
            for core in range(CORES):
                across, along = (turn, 0) if core == phase else (0, turn)
                target = (x + across) % SIDE * SIDE + (y + along) % SIDE
                pairs.append(((x * SIDE + y) * CORES + core, target * CORES + core))
    return lax.ppermute(array, "pb", pairs)


def swap_cores(array):
    return lax.ppermute(array, "pb", [(i, i ^ 1) for i in range(SIDE * SIDE * CORES)])


def group_shift(array, steps):
    groups, width = lax.axis_size("grp"), lax.axis_size("pb")
    pairs = [
        (g * width + p, (g + steps[p % CORES]) % groups * width + p)
        for g in range(groups)
        for p in range(width)
    ]
    return lax.ppermute(array, ("grp", "pb"), pairs)


def exchange_far(blocks):
    groups, count = lax.axis_size("grp"), blocks.shape[0]
    apart = groups // count
    sets = [[g + apart * i for i in range(count)] for g in range(apart)]
    return lax.all_to_all(blocks, "grp", 0, 0, axis_index_groups=sets)


def share(payload):
    return exchange_far(jnp.broadcast_to(payload[None], (SHARED,) + payload.shape))


def shards(
    queries,
    outputs,
    readout_grad,
    readout_weight,
    log_norm,
    probes,
    owner_slots,
    counts,
    cluster_keys,
    values,
):
    token_count = queries.shape[0]
    probe_count = probes.shape[2]
    local_clusters = cluster_keys.shape[1]
    clusters = owner_slots.shape[1]
    capacity = 2 * token_count * probe_count // clusters
    groups = lax.axis_size("grp")
    group, place = lax.axis_index("grp"), lax.axis_index("pb")
    core, column, line = place % CORES, place // (CORES * SIDE), place // CORES % SIDE
    near = jnp.stack([0 * core, 0 * core + 1, 0 * core - 1, 2 - 4 * core])
    apart = groups // SHARED
    members = apart * jnp.arange(SHARED, dtype=jnp.int32)
    owners = (group + near) % groups
    held = group % apart + members
    sources = (group - near[:, None]) % groups % apart + members[None, :]

    payload = query_payload(queries, log_norm.reshape(1, token_count), probes[0].T)
    query_all = lax.all_gather(payload, "grp")

    piece = readout_grad.shape[1]
    first = jnp.stack([readout_grad] + [plane_shift(readout_grad, d, 0) for d in TURNS])
    own, other = split_weight(core.reshape(1), readout_weight, piece)
    other = swap_cores(other)
    second = [plane_shift(first, d, 1) for d in TURNS]
    turns = jnp.asarray((0,) + TURNS, jnp.int32)
    xs, ys = (column - turns) % SIDE, (line - turns) % SIDE
    order = jnp.where(
        core == 0,
        xs[None, :] * SIDE + ys[:, None],
        xs[:, None] * SIDE + ys[None, :],
    ).reshape(-1)
    sums = partial_product(0, order, own, other, [first], [])
    sums = partial_product(1, order, own, other, second, sums)
    grads_held = share(grad_payload(sums[0], swap_cores(sums[1]), outputs))

    packed = query_all[:, token_count + EXTRA * token_count // 128 :]
    ranks = rank_slots(held, packed, owner_slots, token_count)
    query_rows = own_rows(
        group.reshape(1), sources, owner_slots, query_all, token_count, local_clusters, capacity
    )
    rows = gather_rows(owners, ranks, grads_held, local_clusters, capacity)
    grad_rows = [rows[0]] + [group_shift(r, n) for r, n in zip(rows[1:], NEAR)]
    partials = block_grads(
        counts.reshape(local_clusters), query_rows, grad_rows, cluster_keys, values, capacity
    )
    returned = [partials[0]] + [
        group_shift(p, [-n for n in steps]) for p, steps in zip(partials[1:], NEAR)
    ]
    summed = exchange_far(scatter_rows(owners, ranks, returned, capacity))
    return jnp.sum(summed.astype(F32), axis=0).astype(BF16)


def solution(mesh):
    placed = (
        P("grp", "pb"),
        P("grp", "pb"),
        P("grp", "pb"),
        P("pb", None),
        P("grp", "pb"),
        P("pb", "grp", None),
        P("pb", None),
        P("pb", "grp"),
        P("pb", "grp", None, None),
        P("pb", "grp", None, None),
    )
    return jax.shard_map(
        shards, mesh=mesh, in_specs=placed, out_specs=P("grp", "pb"), check_vma=False
    )
```

time: 241 us -> 207 us (0.86)
  blocking collectives: 125 us -> 31.5 us
  starting transfers between devices: 15.3 us -> 60.8 us
  waiting for transfers between devices: 49.8 us -> 65.7 us
  Pallas kernels: 32.4 us -> 24 us
    all_to_all x2 -> x1, blocking collectives: 125 us -> 31.5 us  [exchange_far(): return lax.all_to_all(blocks, 'grp', 0, 0, axis_index_groups=sets)]
    ppermute x0 -> x14, starting transfers between devices: none -> 48.6 us  [the longest x6 24.3 us: group_shift(): return lax.ppermute(array, ('grp', 'pb'), pairs)]
    ppermute x0 -> x14, waiting for transfers between devices: none -> 40.8 us  [the longest x6 25.3 us: plane_shift(): return lax.ppermute(array, 'pb', pairs)]
    all_gather x1, waiting for transfers between devices: 49.1 us -> 16.2 us  [shards(): query_all = lax.all_gather(payload, 'grp')]
    all_to_all x1, waiting for transfers between devices: 0.01 us -> 8.73 us  [exchange_far(): return lax.all_to_all(blocks, 'grp', 0, 0, axis_index_groups=sets)]
    pallas_call x7 -> x10, Pallas kernels: 32.4 us -> 24 us  [the longest x1 8.48 us: block_grads(): pl.pallas_call(functools.partial(block_kernel, capacity, sides), grid_spe...]
    all_to_all x1, starting transfers between devices: 15.3 us -> 12.2 us  [exchange_far(): return lax.all_to_all(blocks, 'grp', 0, 0, axis_index_groups=sets)]
  transfers between devices with their start and end apart: 2 -> 16, of which waited for: 1 -> 9; matrix products, arithmetic and copies ran while one was open for 0% -> 2% of each run, Pallas kernels for 8% -> 5%
where the time goes in v2:
time: 207 us; the launch traced here: 204 us
  waiting for transfers between devices  65.7 us (32%)
  starting transfers between devices  60.8 us (29%)
  blocking collectives  31.5 us (15%)
  Pallas kernels  24 us (12%)
  between operations  13.7 us (7%)
  local copies, waits for them, and re-layouts  5.85 us (3%)
  other arithmetic  2.33 us (1%)
    all_to_all x1, blocking collectives, exchange_far(): return lax.all_to_all(blocks, 'grp', 0, 0, axis_index_groups=sets)  31.5 us
    ppermute x6, waiting for transfers between devices, plane_shift(): return lax.ppermute(array, 'pb', pairs)  25.3 us
    ppermute x6, starting transfers between devices, group_shift(): return lax.ppermute(array, ('grp', 'pb'), pairs)  24.3 us
    ppermute x6, starting transfers between devices, plane_shift(): return lax.ppermute(array, 'pb', pairs)  20.5 us
    all_gather x1, waiting for transfers between devices, shards(): query_all = lax.all_gather(payload, 'grp')  16.2 us
    ppermute x6, waiting for transfers between devices, group_shift(): return lax.ppermute(array, ('grp', 'pb'), pairs)  14 us
    all_to_all x1, starting transfers between devices, exchange_far(): return lax.all_to_all(blocks, 'grp', 0, 0, axis_index_groups=sets)  12.2 us
    all_to_all x1, waiting for transfers between devices, exchange_far(): return lax.all_to_all(blocks, 'grp', 0, 0, axis_index_groups=sets)  8.73 us
  transfers between devices with their start and end apart: 16, of which 9 were waited for; matrix products, arithmetic and copies ran while one was open for 2% of the time, Pallas kernels for 5%

profile of v2, /device:TPU:24, one launch (start us, length us, event | category | flops | bytes accessed | tf_op | source)
XLA Modules:
  0.0 204.0 jit_solution(12717667510090117673)
XLA Ops:
  9.5 4.7 %collective-permute-start.2 = (bf16[512,256]{1,0:T(8,128)(2,1)}, bf16[512,256]{1,0:T(8,128)(2,1)}, u32[]{:S(2)}, u32[]{:S(2)}) collective-permute-start(bf16[512,256]{1,0:T(8,128)(2,1)} %param.13), channel_id=1, source_target_pairs={{0,24},{1,7},{2,26},{3,1},{4,28},{5,3},{6,30},{7,5},{8,0},{9,15},{... | collective-permute-start | bytes 786440 | tf_op jit(solution)/shard_map/ppermute | solution.py:387
  14.2 2.7 %collective-permute-start.3 = (bf16[512,256]{1,0:T(8,128)(2,1)}, bf16[512,256]{1,0:T(8,128)(2,1)}, u32[]{:S(2)}, u32[]{:S(2)}) collective-permute-start(bf16[512,256]{1,0:T(8,128)(2,1)} %param.13), channel_id=1, source_target_pairs={{0,16},{1,5},{2,18},{3,7},{4,20},{5,1},{6,22},{7,3},{8,24},{9,13},... | collective-permute-start | bytes 786440 | tf_op jit(solution)/shard_map/ppermute | solution.py:387
  16.9 2.8 %collective-permute-start.1 = (bf16[512,256]{1,0:T(8,128)(2,1)}, bf16[512,256]{1,0:T(8,128)(2,1)}, u32[]{:S(2)}, u32[]{:S(2)}) collective-permute-start(bf16[512,256]{1,0:T(8,128)(2,1)} %param.13), channel_id=1, source_target_pairs={{0,8},{1,3},{2,10},{3,5},{4,12},{5,7},{6,14},{7,1},{8,16},{9,11},{... | collective-permute-start | bytes 786440 | tf_op jit(solution)/shard_map/ppermute | solution.py:387
  19.8 1.6 copy-done.1
  21.4 1.2 shard_map.112
  22.6 1.9 collective-permute-start
  24.5 2.6 %collective-permute-done.1 = bf16[512,256]{1,0:T(8,128)(2,1)} collective-permute-done((bf16[512,256]{1,0:T(8,128)(2,1)}, bf16[512,256]{1,0:T(8,128)(2,1)}, u32[]{:S(2)}, u32[]{:S(2)}) %collective-permute-start.1) | collective-permute-done | bytes 262176 | tf_op jit(solution)/shard_map/ppermute | solution.py:387
  28.4 5.0 %collective-permute-start.4 = (bf16[4,512,256]{2,1,0:T(8,128)(2,1)S(1)}, bf16[4,512,256]{2,1,0:T(8,128)(2,1)}, u32[]{:S(2)}, u32[]{:S(2)}) collective-permute-start(bf16[4,512,256]{2,1,0:T(8,128)(2,1)S(1)} %pad_maximum_fusion.refs_0_), channel_id=1, source_target_pairs={{0,2},{1,9},{2,4},{3,11},{4,6},{5,13},{6,0},{7,15},{8,10},{9,17},{... | collective-permute-start | bytes 3145736 | tf_op jit(solution)/shard_map/ppermute | solution.py:387
  33.4 1.9 collective-permute-start.5
  35.3 3.4 %collective-permute-start.6 = (bf16[4,512,256]{2,1,0:T(8,128)(2,1)S(1)}, bf16[4,512,256]{2,1,0:T(8,128)(2,1)}, u32[]{:S(2)}, u32[]{:S(2)}) collective-permute-start(bf16[4,512,256]{2,1,0:T(8,128)(2,1)S(1)} %pad_maximum_fusion.refs_0_), channel_id=1, source_target_pairs={{0,4},{1,17},{2,6},{3,19},{4,0},{5,21},{6,2},{7,23},{8,12},{9,25},... | collective-permute-start | bytes 3145736 | tf_op jit(solution)/shard_map/ppermute | solution.py:387
  40.0 17.0 %collective-permute-done.4.refs_0_ = bf16[4,512,256]{2,1,0:T(8,128)(2,1)} collective-permute-done((bf16[4,512,256]{2,1,0:T(8,128)(2,1)S(1)}, bf16[4,512,256]{2,1,0:T(8,128)(2,1)}, u32[]{:S(2)}, u32[]{:S(2)}) %collective-permute-start.4) | collective-permute-done | bytes 1048608 | tf_op jit(solution)/shard_map/ppermute | solution.py:387
  56.9 5.7 %collective-permute-done.5.refs_1_ = bf16[4,512,256]{2,1,0:T(8,128)(2,1)} collective-permute-done((bf16[4,512,256]{2,1,0:T(8,128)(2,1)S(1)}, bf16[4,512,256]{2,1,0:T(8,128)(2,1)}, u32[]{:S(2)}, u32[]{:S(2)}) %collective-permute-start.5) | collective-permute-done | bytes 1048608 | tf_op jit(solution)/shard_map/ppermute | solution.py:387
  62.7 2.9 %shard_map.114 = (f32[512,128]{1,0:T(8,128)S(1)}, f32[512,128]{1,0:T(8,128)S(1)}) custom-call(s32[16]{0:T(128)S(1)} %select_n.80.order_ref, bf16[16,128,256]{2,1,0:T(8,128)(2,1)S(1)} %get-tuple-element.27.own_ref, bf16[16,128,256]{2,1,0:T(8,128)(2,1)S(1)} %collective-permute-done.other_ref, bf16[4,512,256]{2,1,0:T(8,128)(2,1)} %collective-permute-done.4.refs_0_, ...), custom_call_target="tpu_custom_call" | custom-call | tf_op jit(solution)/shard_map/pallas_call | solution.py:152
  65.6 1.9 collective-permute-start.7
  67.5 1.5 collective-permute-done.7.other_ref
  70.1 12.2 %all-to-all-start = ((bf16[4,544,128]{2,1,0:T(8,128)(2,1)}), bf16[4,544,128]{2,1,0:T(8,128)(2,1)}, u32[]{:S(2)}, u32[]{:S(2)}) async-start(bf16[4,544,128]{2,1,0:T(8,128)(2,1)} %broadcast_in_dim.2), calls=%async_computation | async-start | bytes 1114112 | tf_op jit(solution)/shard_map/all_to_all | solution.py:408
  82.4 16.2 %all-gather.3.cloned.1.call-done = bf16[8960,128]{1,0:T(8,128)(2,1)} async-done(((bf16[560,128]{1,0:T(8,128)(2,1)}), bf16[8960,128]{1,0:T(8,128)(2,1)}) %all-gather.3.cloned.1.call-update) | async-done | bytes 2293776 | tf_op jit(solution)/shard_map/all_gather | solution.py:443
  99.5 1.6 shard_map.110.ranks_ref
  101.1 8.7 %all-to-all-done.payload_ref = bf16[4,544,128]{2,1,0:T(8,128)(2,1)} async-done(((bf16[4,544,128]{2,1,0:T(8,128)(2,1)}), bf16[4,544,128]{2,1,0:T(8,128)(2,1)}, u32[]{:S(2)}, u32[]{:S(2)}) %all-to-all-start) | async-done | bytes 557088 | tf_op jit(solution)/shard_map/all_to_all | solution.py:408
  109.8 3.5 %shard_map.116 = (bf16[4,272,128]{2,1,0:T(8,128)(2,1)S(1)}, bf16[4,272,128]{2,1,0:T(8,128)(2,1)S(1)}, bf16[4,272,128]{2,1,0:T(8,128)(2,1)S(1)}, bf16[4,272,128]{2,1,0:T(8,128)(2,1)S(1)}) custom-call(s32[4]{0:T(128)S(1)} %and_select_fusion.4.owners_ref, f32[4,128,512]{2,1,0:T(8,128)S(1)} %shard_map.110.ranks_ref, bf16[4,544,128]{2,1,0:T(8,128)(2,1)} %all-to-all-done.payload_ref), custom_call_target="tpu_custom_call" | custom-call | tf_op jit(solution)/shard_map/pallas_call | solution.py:221
  113.3 8.3 %collective-permute-start.10 = (bf16[4,272,128]{2,1,0:T(8,128)(2,1)S(1)}, bf16[4,272,128]{2,1,0:T(8,128)(2,1)S(1)}, u32[]{:S(2)}, u32[]{:S(2)}) collective-permute-start(bf16[4,272,128]{2,1,0:T(8,128)(2,1)S(1)} %get-tuple-element.36), channel_id=1, source_target_pairs={{0,64},{1,449},{2,66},{3,451},{4,68},{5,453},{6,70},{7,455},{8,72}... | collective-permute-start | bytes 835592 | tf_op jit(solution)/shard_map/ppermute | solution.py:401
  121.7 1.9 collective-permute-start.8
  123.6 5.1 %collective-permute-start.9 = (bf16[4,272,128]{2,1,0:T(8,128)(2,1)S(1)}, bf16[4,272,128]{2,1,0:T(8,128)(2,1)S(1)}, u32[]{:S(2)}, u32[]{:S(2)}) collective-permute-start(bf16[4,272,128]{2,1,0:T(8,128)(2,1)S(1)} %get-tuple-element.35), channel_id=1, source_target_pairs={{0,480},{1,481},{2,482},{3,483},{4,484},{5,485},{6,486},{7,487},{8... | collective-permute-start | bytes 835592 | tf_op jit(solution)/shard_map/ppermute | solution.py:401
  128.9 3.1 %shard_map.111 = (bf16[4,272,128]{2,1,0:T(8,128)(2,1)S(1)}, bf16[4,272,128]{2,1,0:T(8,128)(2,1)S(1)}, bf16[4,272,128]{2,1,0:T(8,128)(2,1)S(1)}, bf16[4,272,128]{2,1,0:T(8,128)(2,1)S(1)}) custom-call(s32[1]{0:T(128)} %bitcast.6.group_ref, s32[4,4]{1,0:T(4,128)S(1)} %broadcast_add_fusion.sources_ref, s32[1,128]{1,0:T(1,128)S(1)} %copy-done.7, ...), custom_call_target="tpu_custom_call" | custom-call | tf_op jit(solution)/shard_map/pallas_call | solution.py:263
  132.5 4.6 %collective-permute-done.8.refs_9_.refs_13_ = bf16[4,272,128]{2,1,0:T(8,128)(2,1)S(1)} collective-permute-done((bf16[4,272,128]{2,1,0:T(8,128)(2,1)S(1)}, bf16[4,272,128]{2,1,0:T(8,128)(2,1)S(1)}, u32[]{:S(2)}, u32[]{:S(2)}) %collective-permute-start.8) | collective-permute-done | bytes 278560 | tf_op jit(solution)/shard_map/ppermute | solution.py:401
  137.2 8.5 %shard_map.117 = (bf16[4,256,128]{2,1,0:T(8,128)(2,1)S(1)}, bf16[4,256,128]{2,1,0:T(8,128)(2,1)S(1)}, bf16[4,256,128]{2,1,0:T(8,128)(2,1)S(1)}, bf16[4,256,128]{2,1,0:T(8,128)(2,1)S(1)}) custom-call(s32[8]{0:T(128)S(1)} %bitcast.17, bf16[4,272,128]{2,1,0:T(8,128)(2,1)S(1)} %get-tuple-element.23.refs_0_.refs_4_, ...), custom_call_target="tpu_custom_call" | custom-call | tf_op jit(solution)/shard_map/pallas_call | solution.py:365
  145.7 2.8 %collective-permute-start.11 = (bf16[4,256,128]{2,1,0:T(8,128)(2,1)S(1)}, bf16[4,256,128]{2,1,0:T(8,128)(2,1)S(1)}, u32[]{:S(2)}, u32[]{:S(2)}) collective-permute-start(bf16[4,256,128]{2,1,0:T(8,128)(2,1)S(1)} %get-tuple-element.38), channel_id=1, source_target_pairs={{0,480},{1,481},{2,482},{3,483},{4,484},{5,485},{6,486},{7,487},{8... | collective-permute-start | bytes 786440 | tf_op jit(solution)/shard_map/ppermute | solution.py:401
  148.5 3.0 %collective-permute-start.12 = (bf16[4,256,128]{2,1,0:T(8,128)(2,1)S(1)}, bf16[4,256,128]{2,1,0:T(8,128)(2,1)S(1)}, u32[]{:S(2)}, u32[]{:S(2)}) collective-permute-start(bf16[4,256,128]{2,1,0:T(8,128)(2,1)S(1)} %get-tuple-element.39), channel_id=1, source_target_pairs={{0,32},{1,33},{2,34},{3,35},{4,36},{5,37},{6,38},{7,39},{8,40},{9,... | collective-permute-start | bytes 786440 | tf_op jit(solution)/shard_map/ppermute | solution.py:401
  151.5 3.1 %collective-permute-start.13 = (bf16[4,256,128]{2,1,0:T(8,128)(2,1)S(1)}, bf16[4,256,128]{2,1,0:T(8,128)(2,1)S(1)}, u32[]{:S(2)}, u32[]{:S(2)}) collective-permute-start(bf16[4,256,128]{2,1,0:T(8,128)(2,1)S(1)} %get-tuple-element.40), channel_id=1, source_target_pairs={{0,448},{1,65},{2,450},{3,67},{4,452},{5,69},{6,454},{7,71},{8,456... | collective-permute-start | bytes 786440 | tf_op jit(solution)/shard_map/ppermute | solution.py:401
  154.6 8.9 %collective-permute-done.12.refs_2_ = bf16[4,256,128]{2,1,0:T(8,128)(2,1)S(1)} collective-permute-done((bf16[4,256,128]{2,1,0:T(8,128)(2,1)S(1)}, bf16[4,256,128]{2,1,0:T(8,128)(2,1)S(1)}, u32[]{:S(2)}, u32[]{:S(2)}) %collective-permute-start.12) | collective-permute-done | bytes 262176 | tf_op jit(solution)/shard_map/ppermute | solution.py:401
  163.5 1.4 shard_map.118
  164.8 31.5 %all_to_all.10 = bf16[4,512,128]{2,1,0:T(8,128)(2,1)S(1)} all-to-all(bf16[4,512,128]{2,1,0:T(8,128)(2,1)S(1)} %shard_map.118), channel_id=1, replica_groups={{0,128,256,384},{32,160,288,416},{64,192,320,448},{96,224,352,480},{1,1..., dimensions={0} | all-to-all | bytes 1048576 | tf_op jit(solution)/shard_map/all_to_all | solution.py:408
  (47 shorter events, 9.0 us)
Async XLA Ops:
  6.5 92.0 %all-gather.3.cloned.1.call-start = ((), (), s32[]{:S(2)}) async-start(), calls=%async_computation.2 | async-start | bytes 2437120 | tf_op jit(solution)/shard_map/all_gather | solution.py:443
  6.5 0.9 copy-start.5
  7.4 0.7 copy-start.6
  8.1 0.7 copy-start.8
  8.8 18.3 %copy-start.10 = (bf16[512,256]{1,0:T(8,128)(2,1)S(1)}, bf16[512,256]{1,0:T(8,128)(2,1)}, u32[]{:S(2)}) copy-start(bf16[512,256]{1,0:T(8,128)(2,1)} %param.13) | copy-start | bytes 786436
  8.8 29.9 %copy-start.11 = (s32[4]{0:T(128)S(1)}, s32[4]{0:T(128)}, u32[]{:S(2)}) copy-start(s32[4]{0:T(128)} %constant.122) | copy-start | bytes 52
  9.5 15.0 %collective-permute-start.2 = (bf16[512,256]{1,0:T(8,128)(2,1)}, bf16[512,256]{1,0:T(8,128)(2,1)}, u32[]{:S(2)}, u32[]{:S(2)}) collective-permute-start(bf16[512,256]{1,0:T(8,128)(2,1)} %param.13), channel_id=1, source_target_pairs={{0,24},{1,7},{2,26},{3,1},{4,28},{5,3},{6,30},{7,5},{8,0},{9,15},{... | collective-permute-start | bytes 786440 | tf_op jit(solution)/shard_map/ppermute | solution.py:387
  14.2 10.3 %collective-permute-start.3 = (bf16[512,256]{1,0:T(8,128)(2,1)}, bf16[512,256]{1,0:T(8,128)(2,1)}, u32[]{:S(2)}, u32[]{:S(2)}) collective-permute-start(bf16[512,256]{1,0:T(8,128)(2,1)} %param.13), channel_id=1, source_target_pairs={{0,16},{1,5},{2,18},{3,7},{4,20},{5,1},{6,22},{7,3},{8,24},{9,13},... | collective-permute-start | bytes 786440 | tf_op jit(solution)/shard_map/ppermute | solution.py:387
  16.9 10.2 %collective-permute-start.1 = (bf16[512,256]{1,0:T(8,128)(2,1)}, bf16[512,256]{1,0:T(8,128)(2,1)}, u32[]{:S(2)}, u32[]{:S(2)}) collective-permute-start(bf16[512,256]{1,0:T(8,128)(2,1)} %param.13), channel_id=1, source_target_pairs={{0,8},{1,3},{2,10},{3,5},{4,12},{5,7},{6,14},{7,1},{8,16},{9,11},{... | collective-permute-start | bytes 786440 | tf_op jit(solution)/shard_map/ppermute | solution.py:387
  19.8 1.6 copy-start.1
  22.6 16.4 %collective-permute-start = (bf16[16,128,256]{2,1,0:T(8,128)(2,1)}, bf16[16,128,256]{2,1,0:T(8,128)(2,1)S(1)}, u32[]{:S(2)}, u32[]{:S(2)}) collective-permute-start(bf16[16,128,256]{2,1,0:T(8,128)(2,1)} %get-tuple-element.28), channel_id=1, source_target_pairs={{0,1},{1,0},{2,3},{3,2},{4,5},{5,4},{6,7},{7,6},{8,9},{9,8},{10,11... | collective-permute-start | bytes 3145736 | tf_op jit(solution)/shard_map/ppermute | solution.py:391
  28.4 28.6 %collective-permute-start.4 = (bf16[4,512,256]{2,1,0:T(8,128)(2,1)S(1)}, bf16[4,512,256]{2,1,0:T(8,128)(2,1)}, u32[]{:S(2)}, u32[]{:S(2)}) collective-permute-start(bf16[4,512,256]{2,1,0:T(8,128)(2,1)S(1)} %pad_maximum_fusion.refs_0_), channel_id=1, source_target_pairs={{0,2},{1,9},{2,4},{3,11},{4,6},{5,13},{6,0},{7,15},{8,10},{9,17},{... | collective-permute-start | bytes 3145736 | tf_op jit(solution)/shard_map/ppermute | solution.py:387
  33.4 29.2 %collective-permute-start.5 = (bf16[4,512,256]{2,1,0:T(8,128)(2,1)S(1)}, bf16[4,512,256]{2,1,0:T(8,128)(2,1)}, u32[]{:S(2)}, u32[]{:S(2)}) collective-permute-start(bf16[4,512,256]{2,1,0:T(8,128)(2,1)S(1)} %pad_maximum_fusion.refs_0_), channel_id=1, source_target_pairs={{0,6},{1,25},{2,0},{3,27},{4,2},{5,29},{6,4},{7,31},{8,14},{9,1},{... | collective-permute-start | bytes 3145736 | tf_op jit(solution)/shard_map/ppermute | solution.py:387
  35.3 27.3 %collective-permute-start.6 = (bf16[4,512,256]{2,1,0:T(8,128)(2,1)S(1)}, bf16[4,512,256]{2,1,0:T(8,128)(2,1)}, u32[]{:S(2)}, u32[]{:S(2)}) collective-permute-start(bf16[4,512,256]{2,1,0:T(8,128)(2,1)S(1)} %pad_maximum_fusion.refs_0_), channel_id=1, source_target_pairs={{0,4},{1,17},{2,6},{3,19},{4,0},{5,21},{6,2},{7,23},{8,12},{9,25},... | collective-permute-start | bytes 3145736 | tf_op jit(solution)/shard_map/ppermute | solution.py:387
  62.7 6.4 %copy-start.4 = (bf16[512,128]{1,0:T(8,128)(2,1)S(1)}, bf16[512,128]{1,0:T(8,128)(2,1)}, u32[]{:S(2)}) copy-start(bf16[512,128]{1,0:T(8,128)(2,1)} %outputs_ref.1) | copy-start | bytes 393220
  65.6 33.9 %copy-start.7 = (s32[1,128]{1,0:T(1,128)S(1)}, s32[1,128]{1,0:T(1,128)}, u32[]{:S(2)}) copy-start(s32[1,128]{1,0:T(1,128)} %table_ref.3) | copy-start | bytes 1540
  65.6 3.4 %collective-permute-start.7 = (f32[512,128]{1,0:T(8,128)S(1)}, f32[512,128]{1,0:T(8,128)S(1)}, u32[]{:S(2)}, u32[]{:S(2)}) collective-permute-start(f32[512,128]{1,0:T(8,128)S(1)} %get-tuple-element.32), channel_id=1, source_target_pairs={{0,1},{1,0},{2,3},{3,2},{4,5},{5,4},{6,7},{7,6},{8,9},{9,8},{10,11... | collective-permute-start | bytes 786440 | tf_op jit(solution)/shard_map/ppermute | solution.py:391
  70.1 39.7 %all-to-all-start = ((bf16[4,544,128]{2,1,0:T(8,128)(2,1)}), bf16[4,544,128]{2,1,0:T(8,128)(2,1)}, u32[]{:S(2)}, u32[]{:S(2)}) async-start(bf16[4,544,128]{2,1,0:T(8,128)(2,1)} %broadcast_in_dim.2), calls=%async_computation | async-start | bytes 1114112 | tf_op jit(solution)/shard_map/all_to_all | solution.py:408
  98.5 30.4 %copy-start = (bf16[8960,128]{1,0:T(8,128)(2,1)S(1)}, bf16[8960,128]{1,0:T(8,128)(2,1)}, u32[]{:S(2)}) copy-start(bf16[8960,128]{1,0:T(8,128)(2,1)} %all-gather.3.cloned.1.call-done) | copy-start | bytes 6881284
  99.5 37.7 %copy-start.9 = (s32[1,8]{1,0:T(1,128)S(1)}, s32[1,8]{1,0:T(1,128)}, u32[]{:S(2)}) copy-start(s32[1,8]{1,0:T(1,128)} %param.18) | copy-start | bytes 100
  109.8 27.3 %copy-start.2 = (bf16[1,8,512,128]{3,2,1,0:T(8,128)(2,1)S(1)}, bf16[1,8,512,128]{3,2,1,0:T(8,128)(2,1)}, u32[]{:S(2)}) copy-start(bf16[1,8,512,128]{3,2,1,0:T(8,128)(2,1)} %refs_16_.1) | copy-start | bytes 3145732
  109.8 27.3 %copy-start.3 = (bf16[1,8,512,128]{3,2,1,0:T(8,128)(2,1)S(1)}, bf16[1,8,512,128]{3,2,1,0:T(8,128)(2,1)}, u32[]{:S(2)}) copy-start(bf16[1,8,512,128]{3,2,1,0:T(8,128)(2,1)} %refs_17_.1) | copy-start | bytes 3145732
  113.3 19.2 %collective-permute-start.10 = (bf16[4,272,128]{2,1,0:T(8,128)(2,1)S(1)}, bf16[4,272,128]{2,1,0:T(8,128)(2,1)S(1)}, u32[]{:S(2)}, u32[]{:S(2)}) collective-permute-start(bf16[4,272,128]{2,1,0:T(8,128)(2,1)S(1)} %get-tuple-element.36), channel_id=1, source_target_pairs={{0,64},{1,449},{2,66},{3,451},{4,68},{5,453},{6,70},{7,455},{8,72}... | collective-permute-start | bytes 835592 | tf_op jit(solution)/shard_map/ppermute | solution.py:401
  121.7 15.5 %collective-permute-start.8 = (bf16[4,272,128]{2,1,0:T(8,128)(2,1)S(1)}, bf16[4,272,128]{2,1,0:T(8,128)(2,1)S(1)}, u32[]{:S(2)}, u32[]{:S(2)}) collective-permute-start(bf16[4,272,128]{2,1,0:T(8,128)(2,1)S(1)} %get-tuple-element.34), channel_id=1, source_target_pairs={{0,32},{1,33},{2,34},{3,35},{4,36},{5,37},{6,38},{7,39},{8,40},{9,... | collective-permute-start | bytes 835592 | tf_op jit(solution)/shard_map/ppermute | solution.py:401
  123.6 13.6 %collective-permute-start.9 = (bf16[4,272,128]{2,1,0:T(8,128)(2,1)S(1)}, bf16[4,272,128]{2,1,0:T(8,128)(2,1)S(1)}, u32[]{:S(2)}, u32[]{:S(2)}) collective-permute-start(bf16[4,272,128]{2,1,0:T(8,128)(2,1)S(1)} %get-tuple-element.35), channel_id=1, source_target_pairs={{0,480},{1,481},{2,482},{3,483},{4,484},{5,485},{6,486},{7,487},{8... | collective-permute-start | bytes 835592 | tf_op jit(solution)/shard_map/ppermute | solution.py:401
  145.7 8.9 %collective-permute-start.11 = (bf16[4,256,128]{2,1,0:T(8,128)(2,1)S(1)}, bf16[4,256,128]{2,1,0:T(8,128)(2,1)S(1)}, u32[]{:S(2)}, u32[]{:S(2)}) collective-permute-start(bf16[4,256,128]{2,1,0:T(8,128)(2,1)S(1)} %get-tuple-element.38), channel_id=1, source_target_pairs={{0,480},{1,481},{2,482},{3,483},{4,484},{5,485},{6,486},{7,487},{8... | collective-permute-start | bytes 786440 | tf_op jit(solution)/shard_map/ppermute | solution.py:401
  148.5 15.0 %collective-permute-start.12 = (bf16[4,256,128]{2,1,0:T(8,128)(2,1)S(1)}, bf16[4,256,128]{2,1,0:T(8,128)(2,1)S(1)}, u32[]{:S(2)}, u32[]{:S(2)}) collective-permute-start(bf16[4,256,128]{2,1,0:T(8,128)(2,1)S(1)} %get-tuple-element.39), channel_id=1, source_target_pairs={{0,32},{1,33},{2,34},{3,35},{4,36},{5,37},{6,38},{7,39},{8,40},{9,... | collective-permute-start | bytes 786440 | tf_op jit(solution)/shard_map/ppermute | solution.py:401
  151.5 11.9 %collective-permute-start.13 = (bf16[4,256,128]{2,1,0:T(8,128)(2,1)S(1)}, bf16[4,256,128]{2,1,0:T(8,128)(2,1)S(1)}, u32[]{:S(2)}, u32[]{:S(2)}) collective-permute-start(bf16[4,256,128]{2,1,0:T(8,128)(2,1)S(1)} %get-tuple-element.40), channel_id=1, source_target_pairs={{0,448},{1,65},{2,450},{3,67},{4,452},{5,69},{6,454},{7,71},{8,456... | collective-permute-start | bytes 786440 | tf_op jit(solution)/shard_map/ppermute | solution.py:401
Sparse Core Ops, SparseCore 0:
  9.7 88.7 all-gather.2

commit v3 on v2

--- a/solution.py
+++ b/solution.py
@@ -53,33 +53,50 @@
     return jnp.where(earlier < later, 1.0, 0.0).astype(BF16)
 
 
-def rank_kernel(table_ref, held_ref, packed_ref, ranks_ref):
+def rank_kernel(table_ref, held_ref, payload_ref, ranks_ref, packed_ref, arrived):
     blocks, clusters, tokens = ranks_ref.shape
+    start = tokens + EXTRA * tokens // 128
+    copies = [
+        pltpu.make_async_copy(
+            payload_ref.at[held_ref[b], pl.ds(start, packed_ref.shape[1]), :],
+            packed_ref.at[b],
+            arrived.at[b],
+        )
+        for b in range(blocks)
+    ]
+    for copy in copies:
+        copy.start()
     cluster = lax.broadcasted_iota(jnp.int32, (clusters, tokens), 0).astype(F32)
     slot = lax.broadcasted_iota(jnp.int32, (clusters, clusters), 0)
     table = jnp.where(table_ref[...] == slot, 1.0, 0.0).astype(BF16)
     before = earlier_tokens(tokens)
     for b in range(blocks):
+        copies[b].wait()
         named = jnp.zeros((clusters, tokens), F32)
-        for row in probe_rows(packed_ref[held_ref[b]], tokens):
+        for row in probe_rows(packed_ref[b], tokens):
             named += jnp.where(row == cluster, 1.0, 0.0)
         marked = jnp.dot(table, named.astype(BF16), preferred_element_type=F32)
         ranking = jnp.dot(marked.astype(BF16), before, preferred_element_type=F32)
         ranks_ref[b] = jnp.where(marked > 0.5, ranking, -1.0)
 
 
-def rank_slots(held, packed, table, tokens):
+def rank_slots(held, payloads, table, tokens):
     blocks, clusters = held.shape[0], table.shape[1]
+    packed = payloads.shape[1] - tokens - EXTRA * tokens // 128
     return pl.pallas_call(
         rank_kernel,
         in_specs=[
             pl.BlockSpec(memory_space=pltpu.VMEM),
             pl.BlockSpec(memory_space=pltpu.SMEM),
-            pl.BlockSpec(memory_space=pltpu.VMEM),
+            pl.BlockSpec(memory_space=pl.ANY),
         ],
         out_shape=jax.ShapeDtypeStruct((blocks, clusters, tokens), F32),
-        compiler_params=params(),
-    )(table, held, packed)
+        scratch_shapes=[
+            pltpu.VMEM((blocks, packed, 128), BF16),
+            pltpu.SemaphoreType.DMA((blocks,)),
+        ],
+        compiler_params=params(),
+    )(table, held, payloads)
 
 
 def query_kernel(query_ref, norm_ref, probes_ref, out_ref):
@@ -318,62 +335,54 @@
 
 
 def block_kernel(capacity, sides, counts_ref, *refs):
-    query_refs, query_extras = refs[:sides], refs[sides : 2 * sides]
-    grad_refs, grad_extras = refs[2 * sides : 3 * sides], refs[3 * sides : 4 * sides]
-    key_ref, value_ref = refs[4 * sides : 4 * sides + 2]
-    out_refs = refs[4 * sides + 2 : 5 * sides + 2]
-    norm_ref, delta_ref = refs[5 * sides + 2 :]
-    cluster = pl.program_id(0)
+    query_refs, grad_refs = refs[:sides], refs[sides : 2 * sides]
+    key_ref, value_ref = refs[2 * sides : 2 * sides + 2]
+    out_refs = refs[2 * sides + 2 : 3 * sides + 2]
+    norm_ref, delta_ref = refs[3 * sides + 2 :]
     senders, _, width = query_refs[0].shape
-    span = key_ref.shape[2]
+    local_clusters, span = key_ref.shape[1:3]
     score_scale = width ** (-0.5)
     each = senders * capacity
     arrivals = sides * each
-
-    @pl.when(cluster == 0)
-    def _():
-        unpack_extra(query_extras, norm_ref, capacity)
-        unpack_extra(grad_extras, delta_ref, capacity)
-
-    keys, vals = key_ref[0, 0], value_ref[0, 0]
-    query = jnp.concatenate([ref[...].reshape(each, width) for ref in query_refs], axis=0)
-    grad = jnp.concatenate([ref[...].reshape(each, width) for ref in grad_refs], axis=0)
-    scores = lax.dot_general(keys, query, NT, preferred_element_type=F32) * score_scale
+    behind = slice(local_clusters * capacity, local_clusters * capacity + 2 * EXTRA)
+    unpack_extra([ref.at[:, behind, :] for ref in query_refs], norm_ref, capacity)
+    unpack_extra([ref.at[:, behind, :] for ref in grad_refs], delta_ref, capacity)
     place = lax.broadcasted_iota(jnp.int32, (span, arrivals), 0)
-    weights = jnp.where(
-        place < counts_ref[cluster], jnp.exp(scores - norm_ref[pl.ds(cluster, 1), :]), 0.0
-    )
-    grad_prob = lax.dot_general(vals, grad, NT, preferred_element_type=F32)
-    grad_score = (weights * (grad_prob - delta_ref[pl.ds(cluster, 1), :])).astype(BF16)
-    partial = lax.dot_general(keys, grad_score, TN, preferred_element_type=F32) * score_scale
-    partial = partial.T.astype(BF16)
-    for i, out_ref in enumerate(out_refs):
-        out_ref[...] = partial[i * each : (i + 1) * each].reshape(senders, capacity, width)
+
+    for c in range(local_clusters):
+        mine = slice(c * capacity, (c + 1) * capacity)
+        query, grad = (
+            jnp.concatenate([ref[:, mine, :].reshape(each, width) for ref in side], axis=0)
+            for side in (query_refs, grad_refs)
+        )
+        keys = key_ref[0, c]
+        scores = lax.dot_general(keys, query, NT, preferred_element_type=F32) * score_scale
+        weights = jnp.where(
+            place < counts_ref[c], jnp.exp(scores - norm_ref[c : c + 1, :]), 0.0
+        )
+        grad_prob = lax.dot_general(value_ref[0, c], grad, NT, preferred_element_type=F32)
+        grad_score = (weights * (grad_prob - delta_ref[c : c + 1, :])).astype(BF16)
+        partial = lax.dot_general(keys, grad_score, TN, preferred_element_type=F32)
+        partial = (partial * score_scale).T.astype(BF16)
+        for i, out_ref in enumerate(out_refs):
+            rows = partial[i * each : (i + 1) * each]
+            out_ref[:, mine, :] = rows.reshape(senders, capacity, width)
 
 
 def block_grads(counts, query_rows, grad_rows, keys, values, capacity):
     sides = len(query_rows)
     senders, _, width = query_rows[0].shape
-    local_clusters, span = keys.shape[1:3]
+    local_clusters = keys.shape[1]
     picked = local_clusters * capacity
-    rows = pl.BlockSpec((senders, capacity, width), lambda c, _: (0, c, 0))
-    extra = pl.BlockSpec(
-        (senders, 2 * EXTRA, width), lambda c, _: (0, picked // (2 * EXTRA), 0)
-    )
-    stored = pl.BlockSpec((1, 1, span, width), lambda c, _: (0, c, 0, 0))
     arrivals = sides * senders * capacity
     return pl.pallas_call(
         functools.partial(block_kernel, capacity, sides),
-        grid_spec=pltpu.PrefetchScalarGridSpec(
-            num_scalar_prefetch=1,
-            grid=(local_clusters,),
-            in_specs=([rows] * sides + [extra] * sides) * 2 + [stored, stored],
-            out_specs=[rows] * sides,
-            scratch_shapes=[pltpu.VMEM((local_clusters, arrivals), F32)] * 2,
-        ),
+        in_specs=[pl.BlockSpec(memory_space=pltpu.SMEM)]
+        + [pl.BlockSpec(memory_space=pltpu.VMEM)] * (2 * sides + 2),
         out_shape=[jax.ShapeDtypeStruct((senders, picked, width), BF16)] * sides,
-        compiler_params=params(),
-    )(counts, *query_rows, *query_rows, *grad_rows, *grad_rows, keys, values)
+        scratch_shapes=[pltpu.VMEM((local_clusters, arrivals), F32)] * 2,
+        compiler_params=params(),
+    )(counts, *query_rows, *grad_rows, keys, values)
 
 
 def plane_shift(array, turn, phase):
@@ -401,15 +410,9 @@
     return lax.ppermute(array, ("grp", "pb"), pairs)
 
 
-def exchange_far(blocks):
-    groups, count = lax.axis_size("grp"), blocks.shape[0]
-    apart = groups // count
-    sets = [[g + apart * i for i in range(count)] for g in range(apart)]
-    return lax.all_to_all(blocks, "grp", 0, 0, axis_index_groups=sets)
-
-
-def share(payload):
-    return exchange_far(jnp.broadcast_to(payload[None], (SHARED,) + payload.shape))
+def far_sets():
+    apart = lax.axis_size("grp") // SHARED
+    return [[g + apart * i for i in range(SHARED)] for g in range(apart)]
 
 
 def shards(
@@ -454,12 +457,13 @@
         xs[None, :] * SIDE + ys[:, None],
         xs[:, None] * SIDE + ys[None, :],
     ).reshape(-1)
-    sums = partial_product(0, order, own, other, [first], [])
-    sums = partial_product(1, order, own, other, second, sums)
-    grads_held = share(grad_payload(sums[0], swap_cores(sums[1]), outputs))
-
-    packed = query_all[:, token_count + EXTRA * token_count // 128 :]
-    ranks = rank_slots(held, packed, owner_slots, token_count)
+    sums = []
+    for i, pieces in enumerate([first] + second):
+        sums = partial_product(i, order, own, other, [pieces], sums)
+    payload = grad_payload(sums[0], swap_cores(sums[1]), outputs)
+    grads_held = lax.all_gather(payload, "grp", axis_index_groups=far_sets())
+
+    ranks = rank_slots(held, query_all, owner_slots, token_count)
     query_rows = own_rows(
         group.reshape(1), sources, owner_slots, query_all, token_count, local_clusters, capacity
     )
@@ -471,7 +475,8 @@
     returned = [partials[0]] + [
         group_shift(p, [-n for n in steps]) for p, steps in zip(partials[1:], NEAR)
     ]
-    summed = exchange_far(scatter_rows(owners, ranks, returned, capacity))
+    summed = scatter_rows(owners, ranks, returned, capacity)
+    summed = lax.all_to_all(summed, "grp", 0, 0, axis_index_groups=far_sets())
     return jnp.sum(summed.astype(F32), axis=0).astype(BF16)
 
 

time: 207 us -> 195 us (0.942)
  the two profiles are of different devices: /device:TPU:24 before, /device:TPU:56 now
where the time goes in v3:
time: 195 us; the launch traced here: 194 us
  blocking collectives  71.2 us (37%)
  starting transfers between devices  43.6 us (22%)
  waiting for transfers between devices  34.8 us (18%)
  Pallas kernels  22.8 us (12%)
  between operations  13.8 us (7%)
  local copies, waits for them, and re-layouts  5.64 us (3%)
  other arithmetic  2.33 us (1%)
    all_to_all x1, blocking collectives, shards(): summed = lax.all_to_all(summed, 'grp', 0, 0, axis_index_groups=far_sets())  37.1 us
    all_gather x1, blocking collectives, shards(): grads_held = lax.all_gather(payload, 'grp', axis_index_groups=far_sets())  34.1 us
    ppermute x6, waiting for transfers between devices, plane_shift(): return lax.ppermute(array, 'pb', pairs)  22 us
    ppermute x6, starting transfers between devices, group_shift(): return lax.ppermute(array, ('grp', 'pb'), pairs)  20.6 us
    ppermute x6, starting transfers between devices, plane_shift(): return lax.ppermute(array, 'pb', pairs)  19.2 us
    ppermute x6, waiting for transfers between devices, group_shift(): return lax.ppermute(array, ('grp', 'pb'), pairs)  11.4 us
    pallas_call x4, Pallas kernels, partial_product(): pl.pallas_call(functools.partial(product_kernel, first, len(pieces), len(...  6.19 us
    unnamed x26, local copies, waits for them, and re-layouts  5.56 us
  transfers between devices with their start and end apart: 15, of which 8 were waited for; matrix products, arithmetic and copies ran while one was open for 1% of the time, Pallas kernels for 6%

profile of v3, /device:TPU:56, one launch (start us, length us, event | category | flops | bytes accessed | tf_op | source)
XLA Modules:
  0.0 194.2 jit_solution(3463962007951094643)
XLA Ops:
  9.5 4.7 %collective-permute-start.2 = (bf16[512,256]{1,0:T(8,128)(2,1)}, bf16[512,256]{1,0:T(8,128)(2,1)}, u32[]{:S(2)}, u32[]{:S(2)}) collective-permute-start(bf16[512,256]{1,0:T(8,128)(2,1)} %param.13), channel_id=1, source_target_pairs={{0,24},{1,7},{2,26},{3,1},{4,28},{5,3},{6,30},{7,5},{8,0},{9,15},{... | collective-permute-start | bytes 786440 | tf_op jit(solution)/shard_map/ppermute | solution.py:396
  14.2 2.7 %collective-permute-start.3 = (bf16[512,256]{1,0:T(8,128)(2,1)}, bf16[512,256]{1,0:T(8,128)(2,1)}, u32[]{:S(2)}, u32[]{:S(2)}) collective-permute-start(bf16[512,256]{1,0:T(8,128)(2,1)} %param.13), channel_id=1, source_target_pairs={{0,16},{1,5},{2,18},{3,7},{4,20},{5,1},{6,22},{7,3},{8,24},{9,13},... | collective-permute-start | bytes 786440 | tf_op jit(solution)/shard_map/ppermute | solution.py:396
  16.9 2.8 %collective-permute-start.1 = (bf16[512,256]{1,0:T(8,128)(2,1)}, bf16[512,256]{1,0:T(8,128)(2,1)}, u32[]{:S(2)}, u32[]{:S(2)}) collective-permute-start(bf16[512,256]{1,0:T(8,128)(2,1)} %param.13), channel_id=1, source_target_pairs={{0,8},{1,3},{2,10},{3,5},{4,12},{5,7},{6,14},{7,1},{8,16},{9,11},{... | collective-permute-start | bytes 786440 | tf_op jit(solution)/shard_map/ppermute | solution.py:396
  19.8 1.6 copy-done.2
  22.6 1.9 collective-permute-start
  24.5 2.6 %collective-permute-done.1 = bf16[512,256]{1,0:T(8,128)(2,1)} collective-permute-done((bf16[512,256]{1,0:T(8,128)(2,1)}, bf16[512,256]{1,0:T(8,128)(2,1)}, u32[]{:S(2)}, u32[]{:S(2)}) %collective-permute-start.1) | collective-permute-done | bytes 262176 | tf_op jit(solution)/shard_map/ppermute | solution.py:396
  28.4 2.1 %collective-permute-start.6 = (bf16[4,512,256]{2,1,0:T(8,128)(2,1)S(1)}, bf16[4,512,256]{2,1,0:T(8,128)(2,1)}, u32[]{:S(2)}, u32[]{:S(2)}) collective-permute-start(bf16[4,512,256]{2,1,0:T(8,128)(2,1)S(1)} %pad_maximum_fusion.refs_0_), channel_id=1, source_target_pairs={{0,2},{1,9},{2,4},{3,11},{4,6},{5,13},{6,0},{7,15},{8,10},{9,17},{... | collective-permute-start | bytes 3145736 | tf_op jit(solution)/shard_map/ppermute | solution.py:396
  30.5 3.7 %collective-permute-start.5 = (bf16[4,512,256]{2,1,0:T(8,128)(2,1)S(1)}, bf16[4,512,256]{2,1,0:T(8,128)(2,1)}, u32[]{:S(2)}, u32[]{:S(2)}) collective-permute-start(bf16[4,512,256]{2,1,0:T(8,128)(2,1)S(1)} %pad_maximum_fusion.refs_0_), channel_id=1, source_target_pairs={{0,6},{1,25},{2,0},{3,27},{4,2},{5,29},{6,4},{7,31},{8,14},{9,1},{... | collective-permute-start | bytes 3145736 | tf_op jit(solution)/shard_map/ppermute | solution.py:396
  34.2 3.1 %collective-permute-start.4 = (bf16[4,512,256]{2,1,0:T(8,128)(2,1)S(1)}, bf16[4,512,256]{2,1,0:T(8,128)(2,1)}, u32[]{:S(2)}, u32[]{:S(2)}) collective-permute-start(bf16[4,512,256]{2,1,0:T(8,128)(2,1)S(1)} %pad_maximum_fusion.refs_0_), channel_id=1, source_target_pairs={{0,4},{1,17},{2,6},{3,19},{4,0},{5,21},{6,2},{7,23},{8,12},{9,25},... | collective-permute-start | bytes 3145736 | tf_op jit(solution)/shard_map/ppermute | solution.py:396
  38.6 6.5 %collective-permute-done.6.refs_0_ = bf16[4,512,256]{2,1,0:T(8,128)(2,1)} collective-permute-done((bf16[4,512,256]{2,1,0:T(8,128)(2,1)S(1)}, bf16[4,512,256]{2,1,0:T(8,128)(2,1)}, u32[]{:S(2)}, u32[]{:S(2)}) %collective-permute-start.6) | collective-permute-done | bytes 1048608 | tf_op jit(solution)/shard_map/ppermute | solution.py:396
  45.2 1.7 shard_map.114
  46.9 12.9 %collective-permute-done.5.refs_0_ = bf16[4,512,256]{2,1,0:T(8,128)(2,1)} collective-permute-done((bf16[4,512,256]{2,1,0:T(8,128)(2,1)S(1)}, bf16[4,512,256]{2,1,0:T(8,128)(2,1)}, u32[]{:S(2)}, u32[]{:S(2)}) %collective-permute-start.5) | collective-permute-done | bytes 1048608 | tf_op jit(solution)/shard_map/ppermute | solution.py:396
  59.7 1.7 shard_map.115
  61.5 1.8 shard_map.116
  63.3 1.9 collective-permute-start.7
  65.3 1.4 collective-permute-done.7.other_ref
  66.9 34.1 %all-gather.1 = bf16[2176,128]{1,0:T(8,128)(2,1)S(1)} all-gather(bf16[544,128]{1,0:T(8,128)(2,1)S(1)} %shard_map.117), channel_id=3, replica_groups={{0,128,256,384},{32,160,288,416},{64,192,320,448},{96,224,352,480},{1,1..., dimensions={0}, use_global_device_ids=true | all-gather | bytes 696320 | tf_op jit(solution)/shard_map/all_gather | solution.py:464
  101.0 1.6 copy-done
  102.6 2.2 %shard_map.110.ranks_ref = f32[4,128,512]{2,1,0:T(8,128)S(1)} custom-call(s32[1,128]{1,0:T(1,128)S(1)} %copy-done.9, s32[4]{0:T(128)S(1)} %broadcast_add_fusion.1.held_ref, bf16[16,560,128]{2,1,0:T(8,128)(2,1)S(1)} %bitcast.14), custom_call_target="tpu_custom_call" | custom-call | tf_op jit(solution)/shard_map/pallas_call | solution.py:86
  104.9 2.8 %shard_map.118 = (bf16[4,272,128]{2,1,0:T(8,128)(2,1)S(1)}, bf16[4,272,128]{2,1,0:T(8,128)(2,1)S(1)}, bf16[4,272,128]{2,1,0:T(8,128)(2,1)S(1)}, bf16[4,272,128]{2,1,0:T(8,128)(2,1)S(1)}) custom-call(s32[4]{0:T(128)S(1)} %and_select_fusion.4.owners_ref, f32[4,128,512]{2,1,0:T(8,128)S(1)} %shard_map.110.ranks_ref, bf16[4,544,128]{2,1,0:T(8,128)(2,1)S(1)} %bitcast.16), custom_call_target="tpu_custom_call" | custom-call | tf_op jit(solution)/shard_map/pallas_call | solution.py:238
  107.7 3.2 %collective-permute-start.10 = (bf16[4,272,128]{2,1,0:T(8,128)(2,1)S(1)}, bf16[4,272,128]{2,1,0:T(8,128)(2,1)S(1)}, u32[]{:S(2)}, u32[]{:S(2)}) collective-permute-start(bf16[4,272,128]{2,1,0:T(8,128)(2,1)S(1)} %get-tuple-element.44), channel_id=1, source_target_pairs={{0,64},{1,449},{2,66},{3,451},{4,68},{5,453},{6,70},{7,455},{8,72}... | collective-permute-start | bytes 835592 | tf_op jit(solution)/shard_map/ppermute | solution.py:410
  110.9 4.4 %collective-permute-start.8 = (bf16[4,272,128]{2,1,0:T(8,128)(2,1)S(1)}, bf16[4,272,128]{2,1,0:T(8,128)(2,1)S(1)}, u32[]{:S(2)}, u32[]{:S(2)}) collective-permute-start(bf16[4,272,128]{2,1,0:T(8,128)(2,1)S(1)} %get-tuple-element.42), channel_id=1, source_target_pairs={{0,32},{1,33},{2,34},{3,35},{4,36},{5,37},{6,38},{7,39},{8,40},{9,... | collective-permute-start | bytes 835592 | tf_op jit(solution)/shard_map/ppermute | solution.py:410
  115.2 2.1 %collective-permute-start.9 = (bf16[4,272,128]{2,1,0:T(8,128)(2,1)S(1)}, bf16[4,272,128]{2,1,0:T(8,128)(2,1)S(1)}, u32[]{:S(2)}, u32[]{:S(2)}) collective-permute-start(bf16[4,272,128]{2,1,0:T(8,128)(2,1)S(1)} %get-tuple-element.43), channel_id=1, source_target_pairs={{0,480},{1,481},{2,482},{3,483},{4,484},{5,485},{6,486},{7,487},{8... | collective-permute-start | bytes 835592 | tf_op jit(solution)/shard_map/ppermute | solution.py:410
  117.5 3.1 %shard_map.111 = (bf16[4,272,128]{2,1,0:T(8,128)(2,1)S(1)}, bf16[4,272,128]{2,1,0:T(8,128)(2,1)S(1)}, bf16[4,272,128]{2,1,0:T(8,128)(2,1)S(1)}, bf16[4,272,128]{2,1,0:T(8,128)(2,1)S(1)}) custom-call(s32[1]{0:T(128)} %bitcast.6.group_ref, s32[4,4]{1,0:T(4,128)S(1)} %broadcast_add_fusion.sources_ref, s32[1,128]{1,0:T(1,128)S(1)} %copy-done.9, ...), custom_call_target="tpu_custom_call" | custom-call | tf_op jit(solution)/shard_map/pallas_call | solution.py:280
  120.6 2.7 %collective-permute-done.10.refs_7_ = bf16[4,272,128]{2,1,0:T(8,128)(2,1)S(1)} collective-permute-done((bf16[4,272,128]{2,1,0:T(8,128)(2,1)S(1)}, bf16[4,272,128]{2,1,0:T(8,128)(2,1)S(1)}, u32[]{:S(2)}, u32[]{:S(2)}) %collective-permute-start.10) | collective-permute-done | bytes 278560 | tf_op jit(solution)/shard_map/ppermute | solution.py:410
  124.6 5.0 %shard_map.119 = (bf16[4,256,128]{2,1,0:T(8,128)(2,1)S(1)}, bf16[4,256,128]{2,1,0:T(8,128)(2,1)S(1)}, bf16[4,256,128]{2,1,0:T(8,128)(2,1)S(1)}, bf16[4,256,128]{2,1,0:T(8,128)(2,1)S(1)}) custom-call(s32[8]{0:T(128)S(1)} %bitcast.19, bf16[4,272,128]{2,1,0:T(8,128)(2,1)S(1)} %get-tuple-element.27.refs_0_, bf16[4,272,128]{2,1,0:T(8,128)(2,1)S(1)} %get-tuple-element.28.refs_1_, ...), custom_call_target="tpu_custom_call" | custom-call | tf_op jit(solution)/shard_map/pallas_call | solution.py:378
  129.6 4.1 %collective-permute-start.11 = (bf16[4,256,128]{2,1,0:T(8,128)(2,1)S(1)}, bf16[4,256,128]{2,1,0:T(8,128)(2,1)S(1)}, u32[]{:S(2)}, u32[]{:S(2)}) collective-permute-start(bf16[4,256,128]{2,1,0:T(8,128)(2,1)S(1)} %get-tuple-element.46), channel_id=1, source_target_pairs={{0,480},{1,481},{2,482},{3,483},{4,484},{5,485},{6,486},{7,487},{8... | collective-permute-start | bytes 786440 | tf_op jit(solution)/shard_map/ppermute | solution.py:410
  133.8 1.9 collective-permute-start.12
  135.7 4.9 %collective-permute-start.13 = (bf16[4,256,128]{2,1,0:T(8,128)(2,1)S(1)}, bf16[4,256,128]{2,1,0:T(8,128)(2,1)S(1)}, u32[]{:S(2)}, u32[]{:S(2)}) collective-permute-start(bf16[4,256,128]{2,1,0:T(8,128)(2,1)S(1)} %get-tuple-element.48), channel_id=1, source_target_pairs={{0,448},{1,65},{2,450},{3,67},{4,452},{5,69},{6,454},{7,71},{8,456... | collective-permute-start | bytes 786440 | tf_op jit(solution)/shard_map/ppermute | solution.py:410
  140.6 5.3 %collective-permute-done.12.refs_2_ = bf16[4,256,128]{2,1,0:T(8,128)(2,1)S(1)} collective-permute-done((bf16[4,256,128]{2,1,0:T(8,128)(2,1)S(1)}, bf16[4,256,128]{2,1,0:T(8,128)(2,1)S(1)}, u32[]{:S(2)}, u32[]{:S(2)}) %collective-permute-start.12) | collective-permute-done | bytes 262176 | tf_op jit(solution)/shard_map/ppermute | solution.py:410
  146.0 2.1 %collective-permute-done.13.refs_3_ = bf16[4,256,128]{2,1,0:T(8,128)(2,1)S(1)} collective-permute-done((bf16[4,256,128]{2,1,0:T(8,128)(2,1)S(1)}, bf16[4,256,128]{2,1,0:T(8,128)(2,1)S(1)}, u32[]{:S(2)}, u32[]{:S(2)}) %collective-permute-start.13) | collective-permute-done | bytes 262176 | tf_op jit(solution)/shard_map/ppermute | solution.py:410
  149.5 37.1 %all_to_all.5 = bf16[4,512,128]{2,1,0:T(8,128)(2,1)S(1)} all-to-all(bf16[4,512,128]{2,1,0:T(8,128)(2,1)S(1)} %shard_map.120), channel_id=1, replica_groups={{0,128,256,384},{32,160,288,416},{64,192,320,448},{96,224,352,480},{1,1..., dimensions={0} | all-to-all | bytes 1048576 | tf_op jit(solution)/shard_map/all_to_all | solution.py:479
  (48 shorter events, 10.5 us)
Async XLA Ops:
  6.5 94.5 %all-gather.4.cloned.1.call-start = ((), (), s32[]{:S(2)}) async-start(), calls=%async_computation.1 | async-start | bytes 2437120 | tf_op jit(solution)/shard_map/all_gather | solution.py:446
  6.5 0.9 copy-start.6
  7.4 0.7 copy-start.7
  8.1 0.7 copy-start.8
  8.8 18.3 %copy-start.11 = (bf16[512,256]{1,0:T(8,128)(2,1)S(1)}, bf16[512,256]{1,0:T(8,128)(2,1)}, u32[]{:S(2)}) copy-start(bf16[512,256]{1,0:T(8,128)(2,1)} %param.13) | copy-start | bytes 786436
  8.8 28.6 %copy-start.12 = (s32[4]{0:T(128)S(1)}, s32[4]{0:T(128)}, u32[]{:S(2)}) copy-start(s32[4]{0:T(128)} %constant.122) | copy-start | bytes 52
  9.5 15.0 %collective-permute-start.2 = (bf16[512,256]{1,0:T(8,128)(2,1)}, bf16[512,256]{1,0:T(8,128)(2,1)}, u32[]{:S(2)}, u32[]{:S(2)}) collective-permute-start(bf16[512,256]{1,0:T(8,128)(2,1)} %param.13), channel_id=1, source_target_pairs={{0,24},{1,7},{2,26},{3,1},{4,28},{5,3},{6,30},{7,5},{8,0},{9,15},{... | collective-permute-start | bytes 786440 | tf_op jit(solution)/shard_map/ppermute | solution.py:396
  14.2 10.3 %collective-permute-start.3 = (bf16[512,256]{1,0:T(8,128)(2,1)}, bf16[512,256]{1,0:T(8,128)(2,1)}, u32[]{:S(2)}, u32[]{:S(2)}) collective-permute-start(bf16[512,256]{1,0:T(8,128)(2,1)} %param.13), channel_id=1, source_target_pairs={{0,16},{1,5},{2,18},{3,7},{4,20},{5,1},{6,22},{7,3},{8,24},{9,13},... | collective-permute-start | bytes 786440 | tf_op jit(solution)/shard_map/ppermute | solution.py:396
  16.9 10.2 %collective-permute-start.1 = (bf16[512,256]{1,0:T(8,128)(2,1)}, bf16[512,256]{1,0:T(8,128)(2,1)}, u32[]{:S(2)}, u32[]{:S(2)}) collective-permute-start(bf16[512,256]{1,0:T(8,128)(2,1)} %param.13), channel_id=1, source_target_pairs={{0,8},{1,3},{2,10},{3,5},{4,12},{5,7},{6,14},{7,1},{8,16},{9,11},{... | collective-permute-start | bytes 786440 | tf_op jit(solution)/shard_map/ppermute | solution.py:396
  19.8 1.6 copy-start.2
  22.6 15.0 %collective-permute-start = (bf16[16,128,256]{2,1,0:T(8,128)(2,1)}, bf16[16,128,256]{2,1,0:T(8,128)(2,1)S(1)}, u32[]{:S(2)}, u32[]{:S(2)}) collective-permute-start(bf16[16,128,256]{2,1,0:T(8,128)(2,1)} %get-tuple-element.32), channel_id=1, source_target_pairs={{0,1},{1,0},{2,3},{3,2},{4,5},{5,4},{6,7},{7,6},{8,9},{9,8},{10,11... | collective-permute-start | bytes 3145736 | tf_op jit(solution)/shard_map/ppermute | solution.py:400
  28.4 16.8 %collective-permute-start.6 = (bf16[4,512,256]{2,1,0:T(8,128)(2,1)S(1)}, bf16[4,512,256]{2,1,0:T(8,128)(2,1)}, u32[]{:S(2)}, u32[]{:S(2)}) collective-permute-start(bf16[4,512,256]{2,1,0:T(8,128)(2,1)S(1)} %pad_maximum_fusion.refs_0_), channel_id=1, source_target_pairs={{0,2},{1,9},{2,4},{3,11},{4,6},{5,13},{6,0},{7,15},{8,10},{9,17},{... | collective-permute-start | bytes 3145736 | tf_op jit(solution)/shard_map/ppermute | solution.py:396
  30.5 29.2 %collective-permute-start.5 = (bf16[4,512,256]{2,1,0:T(8,128)(2,1)S(1)}, bf16[4,512,256]{2,1,0:T(8,128)(2,1)}, u32[]{:S(2)}, u32[]{:S(2)}) collective-permute-start(bf16[4,512,256]{2,1,0:T(8,128)(2,1)S(1)} %pad_maximum_fusion.refs_0_), channel_id=1, source_target_pairs={{0,6},{1,25},{2,0},{3,27},{4,2},{5,29},{6,4},{7,31},{8,14},{9,1},{... | collective-permute-start | bytes 3145736 | tf_op jit(solution)/shard_map/ppermute | solution.py:396
  34.2 27.2 %collective-permute-start.4 = (bf16[4,512,256]{2,1,0:T(8,128)(2,1)S(1)}, bf16[4,512,256]{2,1,0:T(8,128)(2,1)}, u32[]{:S(2)}, u32[]{:S(2)}) collective-permute-start(bf16[4,512,256]{2,1,0:T(8,128)(2,1)S(1)} %pad_maximum_fusion.refs_0_), channel_id=1, source_target_pairs={{0,4},{1,17},{2,6},{3,19},{4,0},{5,21},{6,2},{7,23},{8,12},{9,25},... | collective-permute-start | bytes 3145736 | tf_op jit(solution)/shard_map/ppermute | solution.py:396
  61.4 5.2 %copy-start.5 = (bf16[512,128]{1,0:T(8,128)(2,1)S(1)}, bf16[512,128]{1,0:T(8,128)(2,1)}, u32[]{:S(2)}) copy-start(bf16[512,128]{1,0:T(8,128)(2,1)} %outputs_ref.1) | copy-start | bytes 393220
  61.5 39.5 %copy-start.9 = (s32[1,128]{1,0:T(1,128)S(1)}, s32[1,128]{1,0:T(1,128)}, u32[]{:S(2)}) copy-start(s32[1,128]{1,0:T(1,128)} %table_ref.3) | copy-start | bytes 1540
  63.3 3.4 %collective-permute-start.7 = (f32[512,128]{1,0:T(8,128)S(1)}, f32[512,128]{1,0:T(8,128)S(1)}, u32[]{:S(2)}, u32[]{:S(2)}) collective-permute-start(f32[512,128]{1,0:T(8,128)S(1)} %get-tuple-element.40), channel_id=1, source_target_pairs={{0,1},{1,0},{2,3},{3,2},{4,5},{5,4},{6,7},{7,6},{8,9},{9,8},{10,11... | collective-permute-start | bytes 786440 | tf_op jit(solution)/shard_map/ppermute | solution.py:400
  101.0 1.6 copy-start
  102.6 14.9 %copy-start.1 = (bf16[8960,128]{1,0:T(8,128)(2,1)S(1)}, bf16[8960,128]{1,0:T(8,128)(2,1)}, u32[]{:S(2)}) copy-start(bf16[8960,128]{1,0:T(8,128)(2,1)} %all-gather.4.cloned.1.call-done) | copy-start | bytes 6881284
  104.8 19.8 %copy-start.3 = (bf16[1,8,512,128]{3,2,1,0:T(8,128)(2,1)S(1)}, bf16[1,8,512,128]{3,2,1,0:T(8,128)(2,1)}, u32[]{:S(2)}) copy-start(bf16[1,8,512,128]{3,2,1,0:T(8,128)(2,1)} %refs_8_.1) | copy-start | bytes 3145732
  104.9 19.8 %copy-start.4 = (bf16[1,8,512,128]{3,2,1,0:T(8,128)(2,1)S(1)}, bf16[1,8,512,128]{3,2,1,0:T(8,128)(2,1)}, u32[]{:S(2)}) copy-start(bf16[1,8,512,128]{3,2,1,0:T(8,128)(2,1)} %refs_9_.1) | copy-start | bytes 3145732
  104.9 19.8 %copy-start.10 = (s32[1,8]{1,0:T(1,128)S(1)}, s32[1,8]{1,0:T(1,128)}, u32[]{:S(2)}) copy-start(s32[1,8]{1,0:T(1,128)} %param.18) | copy-start | bytes 100
  107.7 15.6 %collective-permute-start.10 = (bf16[4,272,128]{2,1,0:T(8,128)(2,1)S(1)}, bf16[4,272,128]{2,1,0:T(8,128)(2,1)S(1)}, u32[]{:S(2)}, u32[]{:S(2)}) collective-permute-start(bf16[4,272,128]{2,1,0:T(8,128)(2,1)S(1)} %get-tuple-element.44), channel_id=1, source_target_pairs={{0,64},{1,449},{2,66},{3,451},{4,68},{5,453},{6,70},{7,455},{8,72}... | collective-permute-start | bytes 835592 | tf_op jit(solution)/shard_map/ppermute | solution.py:410
  110.9 13.7 %collective-permute-start.8 = (bf16[4,272,128]{2,1,0:T(8,128)(2,1)S(1)}, bf16[4,272,128]{2,1,0:T(8,128)(2,1)S(1)}, u32[]{:S(2)}, u32[]{:S(2)}) collective-permute-start(bf16[4,272,128]{2,1,0:T(8,128)(2,1)S(1)} %get-tuple-element.42), channel_id=1, source_target_pairs={{0,32},{1,33},{2,34},{3,35},{4,36},{5,37},{6,38},{7,39},{8,40},{9,... | collective-permute-start | bytes 835592 | tf_op jit(solution)/shard_map/ppermute | solution.py:410
  115.2 9.4 %collective-permute-start.9 = (bf16[4,272,128]{2,1,0:T(8,128)(2,1)S(1)}, bf16[4,272,128]{2,1,0:T(8,128)(2,1)S(1)}, u32[]{:S(2)}, u32[]{:S(2)}) collective-permute-start(bf16[4,272,128]{2,1,0:T(8,128)(2,1)S(1)} %get-tuple-element.43), channel_id=1, source_target_pairs={{0,480},{1,481},{2,482},{3,483},{4,484},{5,485},{6,486},{7,487},{8... | collective-permute-start | bytes 835592 | tf_op jit(solution)/shard_map/ppermute | solution.py:410
  129.6 11.0 %collective-permute-start.11 = (bf16[4,256,128]{2,1,0:T(8,128)(2,1)S(1)}, bf16[4,256,128]{2,1,0:T(8,128)(2,1)S(1)}, u32[]{:S(2)}, u32[]{:S(2)}) collective-permute-start(bf16[4,256,128]{2,1,0:T(8,128)(2,1)S(1)} %get-tuple-element.46), channel_id=1, source_target_pairs={{0,480},{1,481},{2,482},{3,483},{4,484},{5,485},{6,486},{7,487},{8... | collective-permute-start | bytes 786440 | tf_op jit(solution)/shard_map/ppermute | solution.py:410
  133.8 12.2 %collective-permute-start.12 = (bf16[4,256,128]{2,1,0:T(8,128)(2,1)S(1)}, bf16[4,256,128]{2,1,0:T(8,128)(2,1)S(1)}, u32[]{:S(2)}, u32[]{:S(2)}) collective-permute-start(bf16[4,256,128]{2,1,0:T(8,128)(2,1)S(1)} %get-tuple-element.47), channel_id=1, source_target_pairs={{0,32},{1,33},{2,34},{3,35},{4,36},{5,37},{6,38},{7,39},{8,40},{9,... | collective-permute-start | bytes 786440 | tf_op jit(solution)/shard_map/ppermute | solution.py:410
  135.7 12.4 %collective-permute-start.13 = (bf16[4,256,128]{2,1,0:T(8,128)(2,1)S(1)}, bf16[4,256,128]{2,1,0:T(8,128)(2,1)S(1)}, u32[]{:S(2)}, u32[]{:S(2)}) collective-permute-start(bf16[4,256,128]{2,1,0:T(8,128)(2,1)S(1)} %get-tuple-element.48), channel_id=1, source_target_pairs={{0,448},{1,65},{2,450},{3,67},{4,452},{5,69},{6,454},{7,71},{8,456... | collective-permute-start | bytes 786440 | tf_op jit(solution)/shard_map/ppermute | solution.py:410
Sparse Core Ops, SparseCore 0:
  9.7 80.5 all-gather.3

commit v4 on v3

v4 whole, which is shorter than its diff:
```python
import functools

import jax
import jax.numpy as jnp
from jax import lax
from jax.experimental import pallas as pl
from jax.experimental.pallas import tpu as pltpu
from jax.sharding import PartitionSpec as P

F32 = jnp.float32
BF16 = jnp.bfloat16
EXTRA = 8
NT = (((1,), (1,)), ((), ()))
TN = (((0,), (0,)), ((), ()))
SIDE, CORES = 4, 2
TURNS = (1, 3, 2)
SHARED = 4
FIRST, SECOND = (1, 3), (3, 1)
NEAR = ((1, 1), (-1, -1), (2, -2))
VMEM_BYTES = 48 * 1024 * 1024


def params():
    return pltpu.CompilerParams(vmem_limit_bytes=VMEM_BYTES)


def split_rows(row):
    high = row.astype(BF16).astype(F32)
    rest = row - high
    middle = rest.astype(BF16).astype(F32)
    low = (rest - middle).astype(BF16).astype(F32)
    pad = jnp.zeros((EXTRA - 3,) + row.shape[1:], F32)
    return jnp.concatenate([high, middle, low, pad], axis=0)


def store_extra(out_ref, extra, tokens):
    for i in range(0, tokens // 128, 2):
        both = [extra[:, (i + k) * 128 : (i + k + 1) * 128] for k in range(2)]
        start = tokens + i * EXTRA
        out_ref[start : start + 2 * EXTRA, :] = jnp.concatenate(both, axis=0).astype(BF16)


def probe_rows(packed, tokens):
    packed, pieces = packed.astype(F32), tokens // 128
    return [
        jnp.concatenate([packed[j + i : j + i + 1] for i in range(pieces)], axis=1)
        for j in range(0, packed.shape[0], pieces)
    ]


def earlier_tokens(tokens):
    earlier = lax.broadcasted_iota(jnp.int32, (tokens, tokens), 0)
    later = lax.broadcasted_iota(jnp.int32, (tokens, tokens), 1)
    return jnp.where(earlier < later, 1.0, 0.0).astype(BF16)


def rank_kernel(table_ref, payload_ref, ranks_ref):
    blocks, clusters, tokens = ranks_ref.shape
    cluster = lax.broadcasted_iota(jnp.int32, (clusters, tokens), 0).astype(F32)
    slot = lax.broadcasted_iota(jnp.int32, (clusters, clusters), 0)
    table = jnp.where(table_ref[...] == slot, 1.0, 0.0).astype(BF16)
    before = earlier_tokens(tokens)
    start = tokens + EXTRA * tokens // 128
    for b in range(blocks):
        named = jnp.zeros((clusters, tokens), F32)
        for row in probe_rows(payload_ref[b, start:, :], tokens):
            named += jnp.where(row == cluster, 1.0, 0.0)
        marked = jnp.dot(table, named.astype(BF16), preferred_element_type=F32)
        ranking = jnp.dot(marked.astype(BF16), before, preferred_element_type=F32)
        ranks_ref[b] = jnp.where(marked > 0.5, ranking, -1.0)


def rank_slots(payloads, table, tokens):
    return pl.pallas_call(
        rank_kernel,
        out_shape=jax.ShapeDtypeStruct((payloads.shape[0], table.shape[1], tokens), F32),
        compiler_params=params(),
    )(table, payloads)


def query_kernel(query_ref, norm_ref, probes_ref, out_ref, packed_ref):
    tokens = query_ref.shape[0]
    pieces = tokens // 128
    out_ref[0:tokens, :] = query_ref[...]
    store_extra(out_ref, split_rows(norm_ref[...]), tokens)
    numbers = probes_ref[...].astype(F32)
    rows = [
        numbers[j : j + 1, i * 128 : (i + 1) * 128]
        for j in range(numbers.shape[0])
        for i in range(pieces)
    ]
    packed = jnp.concatenate(rows, axis=0).astype(BF16)
    out_ref[tokens + EXTRA * pieces :, :] = packed
    packed_ref[...] = packed


def query_payload(queries, norm_row, probes_t):
    tokens, width = queries.shape
    packed = probes_t.shape[0] * tokens // 128
    rows = tokens + EXTRA * tokens // 128 + packed
    return pl.pallas_call(
        query_kernel,
        out_shape=[
            jax.ShapeDtypeStruct((rows, width), BF16),
            jax.ShapeDtypeStruct((packed, 128), BF16),
        ],
        compiler_params=params(),
    )(queries, norm_row, probes_t)


def weight_kernel(core_ref, weight_ref, own_ref, other_ref):
    pieces, _, piece = own_ref.shape
    core = core_ref[0]
    for i in range(pieces):
        for ref, side in ((own_ref, core), (other_ref, 1 - core)):
            start = pl.multiple_of((2 * i + side) * piece, piece)
            ref[i] = weight_ref[:, pl.ds(start, piece)]


def split_weight(core, weight, piece):
    width, depth = weight.shape
    half = jax.ShapeDtypeStruct((depth // piece // 2, width, piece), BF16)
    return pl.pallas_call(
        weight_kernel,
        in_specs=[
            pl.BlockSpec(memory_space=pltpu.SMEM),
            pl.BlockSpec(memory_space=pltpu.VMEM),
        ],
        out_shape=[half, half],
        compiler_params=params(),
    )(core, weight)


def product_kernel(turn, order_ref, own_ref, other_ref, *refs):
    halves, sums, results = refs[:2], refs[2:-2], refs[-2:]
    rows = halves[0].shape[1]
    for half, ref in enumerate(halves):
        span = slice(half * rows, (half + 1) * rows)
        total = None
        for m in range(ref.shape[0]):
            shard = order_ref[turn * ref.shape[0] + m]
            both = jnp.concatenate([own_ref[shard], other_ref[shard]], axis=0)
            term = lax.dot_general(ref[m], both, NT, preferred_element_type=F32)
            total = term if total is None else total + term
        width = total.shape[1] // 2
        for i, out_ref in enumerate(results):
            part = total[:, i * width : (i + 1) * width]
            out_ref[span, :] = part + sums[i][span, :] if sums else part


def partial_product(turn, order, own, other, halves, sums):
    result = jax.ShapeDtypeStruct((2 * halves[0].shape[1], own.shape[1]), F32)
    return pl.pallas_call(
        functools.partial(product_kernel, turn),
        in_specs=[pl.BlockSpec(memory_space=pltpu.SMEM)]
        + [pl.BlockSpec(memory_space=pltpu.VMEM)] * (4 + len(sums)),
        out_shape=[result, result],
        compiler_params=params(),
    )(order, own, other, *halves, *sums)


def grad_kernel(own_ref, other_ref, outputs_ref, packed_ref, out_ref):
    tokens = outputs_ref.shape[0]
    grad = (own_ref[...] + other_ref[...]).astype(BF16)
    out_ref[0:tokens, :] = grad
    product = grad.astype(F32) * outputs_ref[...].astype(F32)
    delta = jnp.sum(product.T, axis=0, keepdims=True)
    store_extra(out_ref, split_rows(delta), tokens)
    out_ref[tokens + EXTRA * tokens // 128 :, :] = packed_ref[...]


def grad_payload(own, other, outputs, packed):
    tokens, width = outputs.shape
    rows = tokens + EXTRA * tokens // 128 + packed.shape[0]
    return pl.pallas_call(
        grad_kernel,
        out_shape=jax.ShapeDtypeStruct((rows, width), BF16),
        compiler_params=params(),
    )(own, other, outputs, packed)


def choices(ranks, capacity):
    slots, tokens = ranks.shape
    place = lax.broadcasted_iota(jnp.int32, (capacity, tokens), 0).astype(F32)
    rows = [jnp.where(ranks[s : s + 1, :] == place, 1.0, 0.0) for s in range(slots)]
    return jnp.concatenate(rows, axis=0).astype(BF16)


def owner_ranks(ranks_ref, block, owner, local_clusters):
    start = pl.multiple_of(owner * local_clusters, local_clusters)
    return ranks_ref[block, pl.ds(start, local_clusters), :]


def pick_rows(payload_ref, chosen, tokens, out_ref):
    picked = chosen.shape[0]
    parts = [
        payload_ref[tokens + i * 2 * EXTRA : tokens + (i + 1) * 2 * EXTRA, :].astype(F32)
        for i in range(tokens // 256)
    ]
    wide = [part[k * EXTRA : (k + 1) * EXTRA] for part in parts for k in range(2)]
    extra = jnp.concatenate(wide, axis=1).astype(BF16)
    out_ref[0:picked, :] = jnp.dot(
        chosen, payload_ref[0:tokens, :], preferred_element_type=F32
    ).astype(BF16)
    moved = lax.dot_general(extra, chosen, NT, preferred_element_type=F32)
    both = [moved[:, k * 128 : (k + 1) * 128] for k in range(picked // 128)]
    out_ref[picked:, :] = jnp.concatenate(both, axis=0).astype(BF16)


def gather_kernel(capacity, local_clusters, owners_ref, ranks_ref, payload_ref, *refs):
    blocks, _, tokens = ranks_ref.shape
    for b in range(blocks):
        for i, out_ref in enumerate(refs):
            chosen = choices(
                owner_ranks(ranks_ref, b, owners_ref[i], local_clusters), capacity
            )
            pick_rows(payload_ref.at[b], chosen, tokens, out_ref.at[b])


def gather_rows(owners, ranks, payloads, local_clusters, capacity):
    blocks, width = ranks.shape[0], payloads.shape[-1]
    picked = local_clusters * capacity
    rows = jax.ShapeDtypeStruct((blocks, picked + EXTRA * picked // 128, width), BF16)
    return pl.pallas_call(
        functools.partial(gather_kernel, capacity, local_clusters),
        in_specs=[pl.BlockSpec(memory_space=pltpu.SMEM)]
        + [pl.BlockSpec(memory_space=pltpu.VMEM)] * 2,
        out_shape=[rows] * owners.shape[0],
        compiler_params=params(),
    )(owners, ranks, payloads)


def own_kernel(capacity, tokens, group_ref, sources_ref, table_ref, payload_ref, *refs):
    places = [(i, b) for i, ref in enumerate(refs) for b in range(ref.shape[0])]
    local_clusters = refs[0].shape[1] * 128 // (128 + EXTRA) // capacity
    clusters = table_ref.shape[1]
    slot = lax.broadcasted_iota(jnp.int32, (local_clusters, clusters), 0)
    cluster = lax.broadcasted_iota(jnp.int32, (local_clusters, clusters), 1)
    mine = table_ref[...] == slot + group_ref[0] * local_clusters
    stored = jnp.sum(jnp.where(mine, cluster.astype(F32), 0.0), axis=1, keepdims=True)
    start = tokens + EXTRA * tokens // 128
    marks = []
    for k in range(len(places)):
        named = jnp.zeros((local_clusters, tokens), F32)
        for row in probe_rows(payload_ref[sources_ref[k], start:, :], tokens):
            named += jnp.where(row == stored, 1.0, 0.0)
        marks.append(named)
    marks = jnp.concatenate(marks, axis=0)
    ranking = jnp.dot(marks.astype(BF16), earlier_tokens(tokens), preferred_element_type=F32)
    ranks = jnp.where(marks > 0.5, ranking, -1.0)
    for k, (i, b) in enumerate(places):
        chosen = choices(ranks[k * local_clusters : (k + 1) * local_clusters], capacity)
        pick_rows(payload_ref.at[sources_ref[k]], chosen, tokens, refs[i].at[b])


def own_rows(group, sources, counts, table, payloads, tokens, local_clusters, capacity):
    picked = local_clusters * capacity
    width = payloads.shape[-1]
    rows = [(count, picked + EXTRA * picked // 128, width) for count in counts]
    return pl.pallas_call(
        functools.partial(own_kernel, capacity, tokens),
        in_specs=[pl.BlockSpec(memory_space=pltpu.SMEM)] * 2
        + [pl.BlockSpec(memory_space=pltpu.VMEM)] * 2,
        out_shape=[jax.ShapeDtypeStruct(shape, BF16) for shape in rows],
        compiler_params=params(),
    )(group, sources, table, payloads)


def scatter_kernel(capacity, owners_ref, held_ref, ranks_ref, *refs):
    partial_refs, (own_ref, pair_ref, kept_ref) = refs[:-3], refs[-3:]
    local_clusters = partial_refs[0].shape[1] // capacity
    places = (own_ref, pair_ref.at[0], kept_ref, pair_ref.at[1])
    for k in (1, 3, 2, 0):
        b = held_ref[k]
        total = None
        for i, partial_ref in enumerate(partial_refs):
            chosen = choices(
                owner_ranks(ranks_ref, b, owners_ref[i], local_clusters), capacity
            )
            term = lax.dot_general(partial_ref[b], chosen, TN, preferred_element_type=F32)
            total = term if total is None else total + term
        places[k][...] = total.T.astype(places[k].dtype)


def scatter_rows(owners, held, ranks, partials, capacity):
    tokens, width = ranks.shape[2], partials[0].shape[2]
    return pl.pallas_call(
        functools.partial(scatter_kernel, capacity),
        in_specs=[pl.BlockSpec(memory_space=pltpu.SMEM)] * 2
        + [pl.BlockSpec(memory_space=pltpu.VMEM)] * (1 + len(partials)),
        out_shape=[
            jax.ShapeDtypeStruct((tokens, width), F32),
            jax.ShapeDtypeStruct((2, tokens, width), BF16),
            jax.ShapeDtypeStruct((tokens, width), F32),
        ],
        compiler_params=params(),
    )(owners, held, ranks, *partials)


def unpack_extra(extra_refs, rows_ref, capacity):
    places = [(i, b) for i, ref in enumerate(extra_refs) for b in range(ref.shape[0])]
    senders = len(places)
    per_row = 128 // capacity
    lane = lax.broadcasted_iota(jnp.int32, (2 * EXTRA, 128), 1) // capacity
    for sub in range(per_row):
        for group in range(senders // per_row):
            total = jnp.zeros((2 * EXTRA, 128), F32)
            for k in range(per_row):
                side, sender = places[group * per_row + k]
                packed = extra_refs[side][sender].astype(F32)
                turn = (k - sub) * capacity % 128
                if turn:
                    packed = pltpu.roll(packed, turn, 1)
                total += jnp.where(lane == k, packed, 0.0)
            lanes = slice(group * 128, (group + 1) * 128)
            for half in range(2):
                rows = total[half * EXTRA : half * EXTRA + 3]
                cluster = half * per_row + sub
                rows_ref[cluster : cluster + 1, lanes] = rows[0:1] + rows[1:2] + rows[2:3]


def block_kernel(capacity, sides, counts_ref, *refs):
    query_refs, grad_refs = refs[:sides], refs[sides : 2 * sides]
    key_ref, value_ref = refs[2 * sides : 2 * sides + 2]
    out_refs = refs[2 * sides + 2 : 3 * sides + 2]
    norm_ref, delta_ref = refs[3 * sides + 2 :]
    width = query_refs[0].shape[2]
    local_clusters, span = key_ref.shape[1:3]
    score_scale = width ** (-0.5)
    arrivals = norm_ref.shape[1]
    behind = slice(local_clusters * capacity, local_clusters * capacity + 2 * EXTRA)
    unpack_extra([ref.at[:, behind, :] for ref in query_refs], norm_ref, capacity)
    unpack_extra([ref.at[:, behind, :] for ref in grad_refs], delta_ref, capacity)
    place = lax.broadcasted_iota(jnp.int32, (span, arrivals), 0)

    for c in range(local_clusters):
        mine = slice(c * capacity, (c + 1) * capacity)
        query, grad = (
            jnp.concatenate([ref[:, mine, :].reshape(-1, width) for ref in side], axis=0)
            for side in (query_refs, grad_refs)
        )
        keys = key_ref[0, c]
        scores = lax.dot_general(keys, query, NT, preferred_element_type=F32) * score_scale
        weights = jnp.where(
            place < counts_ref[c], jnp.exp(scores - norm_ref[c : c + 1, :]), 0.0
        )
        grad_prob = lax.dot_general(value_ref[0, c], grad, NT, preferred_element_type=F32)
        grad_score = (weights * (grad_prob - delta_ref[c : c + 1, :])).astype(BF16)
        partial = lax.dot_general(keys, grad_score, TN, preferred_element_type=F32)
        partial = (partial * score_scale).T.astype(BF16)
        start = 0
        for out_ref in out_refs:
            stop = start + out_ref.shape[0] * capacity
            out_ref[:, mine, :] = partial[start:stop].reshape(-1, capacity, width)
            start = stop


def block_grads(counts, query_rows, grad_rows, keys, values, capacity):
    sides = len(query_rows)
    width = query_rows[0].shape[2]
    local_clusters = keys.shape[1]
    picked = local_clusters * capacity
    senders = [rows.shape[0] for rows in query_rows]
    arrivals = sum(senders) * capacity
    return pl.pallas_call(
        functools.partial(block_kernel, capacity, sides),
        in_specs=[pl.BlockSpec(memory_space=pltpu.SMEM)]
        + [pl.BlockSpec(memory_space=pltpu.VMEM)] * (2 * sides + 2),
        out_shape=[jax.ShapeDtypeStruct((count, picked, width), BF16) for count in senders],
        scratch_shapes=[pltpu.VMEM((local_clusters, arrivals), F32)] * 2,
        compiler_params=params(),
    )(counts, *query_rows, *grad_rows, keys, values)


def plane_shift(array, turn, phase):
    pairs = []
    for x in range(SIDE):
        for y in range(SIDE):
            for core in range(CORES):
                across, along = (turn, 0) if core == phase else (0, turn)
                target = (x + across) % SIDE * SIDE + (y + along) % SIDE
                pairs.append(((x * SIDE + y) * CORES + core, target * CORES + core))
    return lax.ppermute(array, "pb", pairs)


def swap_cores(array):
    return lax.ppermute(array, "pb", [(i, i ^ 1) for i in range(SIDE * SIDE * CORES)])


def group_shift(array, *steps):
    groups, width = lax.axis_size("grp"), lax.axis_size("pb")
    pairs = [
        (g * width + p, (g + steps[p % len(steps)]) % groups * width + p)
        for g in range(groups)
        for p in range(width)
    ]
    return lax.ppermute(array, ("grp", "pb"), pairs)


def partner_swap(array, partner):
    groups, width = lax.axis_size("grp"), lax.axis_size("pb")
    apart = groups // SHARED
    pairs = [
        (g * width + p, (g ^ (partner[p % CORES] * apart)) * width + p)
        for g in range(groups)
        for p in range(width)
    ]
    return lax.ppermute(array, ("grp", "pb"), pairs)


def shards(
    queries,
    outputs,
    readout_grad,
    readout_weight,
    log_norm,
    probes,
    owner_slots,
    counts,
    cluster_keys,
    values,
):
    token_count = queries.shape[0]
    probe_count = probes.shape[2]
    local_clusters = cluster_keys.shape[1]
    clusters = owner_slots.shape[1]
    capacity = 2 * token_count * probe_count // clusters
    groups = lax.axis_size("grp")
    group, place = lax.axis_index("grp"), lax.axis_index("pb")
    core, column, line = place % CORES, place // (CORES * SIDE), place // CORES % SIDE
    apart = groups // SHARED
    sets = [[g + apart * i for i in range(SHARED)] for g in range(apart)]
    near = [0, 1, -1, 2 - 4 * core]
    owners = jnp.stack([(group + n) % groups for n in near])
    sources = [(group - n) % groups % apart + apart * b for n in near for b in range(SHARED)]

    payload, packed = query_payload(queries, log_norm.reshape(1, token_count), probes[0].T)
    query_all = lax.all_gather(payload, "grp")

    piece = readout_grad.shape[1]
    first = [readout_grad] + [plane_shift(readout_grad, d, 0) for d in TURNS]
    half = token_count // 2
    upper = jnp.stack([p[:half] for p in first])
    lower = jnp.stack([p[half:] for p in first])
    own, other = split_weight(core.reshape(1), readout_weight, piece)
    other = swap_cores(other)
    before_up, after_low = plane_shift(upper, 1, 1), plane_shift(lower, -1, 1)
    before_low, after_up = plane_shift(lower, 1, 1), plane_shift(upper, -1, 1)
    far_up, far_low = plane_shift(before_up, 1, 1), plane_shift(after_low, -1, 1)
    turns = jnp.asarray((0,) + TURNS, jnp.int32)
    xs, ys = (column - turns) % SIDE, (line - turns) % SIDE
    order = jnp.where(
        core == 0,
        xs[None, :] * SIDE + ys[:, None],
        xs[:, None] * SIDE + ys[None, :],
    ).reshape(-1)
    arrivals = [(upper, lower), (before_up, before_low), (after_up, after_low), (far_up, far_low)]
    sums = []
    for turn, halves in enumerate(arrivals):
        sums = partial_product(turn, order, own, other, halves, sums)
    payload = grad_payload(sums[0], swap_cores(sums[1]), outputs, packed)
    held = lax.all_gather(payload, "grp", axis_index_groups=sets)
    ranks = rank_slots(held, owner_slots, token_count)
    grad_rows = []
    for i, n in enumerate(NEAR):
        (rows,) = gather_rows(owners[i + 1 : i + 2], ranks, held, local_clusters, capacity)
        grad_rows.append(group_shift(rows, *n))
    grad_rows = list(gather_rows(owners[:1], ranks, held, local_clusters, capacity)) + grad_rows
    query_rows = own_rows(
        group.reshape(1),
        jnp.stack(sources),
        [SHARED] * len(near),
        owner_slots,
        query_all,
        token_count,
        local_clusters,
        capacity,
    )
    partials = block_grads(
        counts.reshape(local_clusters), query_rows, grad_rows, cluster_keys, values, capacity
    )
    returned = [partials[0]] + [
        group_shift(p, *[-n for n in steps]) for p, steps in zip(partials[1:], NEAR)
    ]
    partners = [0, *(core * (p[1] - p[0]) + p[0] for p in (FIRST, SECOND)), SHARED // 2]
    blocks = jnp.stack([group // apart ^ p for p in partners])
    mine, pair, kept = scatter_rows(owners, blocks, ranks, returned, capacity)
    came = partner_swap(pair, FIRST).astype(F32)
    last = partner_swap((kept + came[1]).astype(BF16), SECOND).astype(F32)
    return (mine + came[0] + last).astype(BF16)


def solution(mesh):
    placed = (
        P("grp", "pb"),
        P("grp", "pb"),
        P("grp", "pb"),
        P("pb", None),
        P("grp", "pb"),
        P("pb", "grp", None),
        P("pb", None),
        P("pb", "grp"),
        P("pb", "grp", None, None),
        P("pb", "grp", None, None),
    )
    return jax.shard_map(
        shards, mesh=mesh, in_specs=placed, out_specs=P("grp", "pb"), check_vma=False
    )
```

time: 195 us -> 186 us (0.954)
  the two profiles are of different devices: /device:TPU:56 before, /device:TPU:24 now
where the time goes in v4:
time: 186 us; the launch traced here: 184 us
  starting transfers between devices  64.8 us (35%)
  waiting for transfers between devices  42.2 us (23%)
  blocking collectives  31.7 us (17%)
  Pallas kernels  24.7 us (13%)
  between operations  14 us (8%)
  local copies, waits for them, and re-layouts  5.79 us (3%)
    ppermute x9, starting transfers between devices, plane_shift(): return lax.ppermute(array, 'pb', pairs)  34.3 us
    all_gather x1, blocking collectives, shards(): held = lax.all_gather(payload, 'grp', axis_index_groups=sets)  31.7 us
    ppermute x2, waiting for transfers between devices, partner_swap(): return lax.ppermute(array, ('grp', 'pb'), pairs)  23.2 us
    ppermute x6, starting transfers between devices, group_shift(): return lax.ppermute(array, ('grp', 'pb'), pairs)  18.7 us
    ppermute x6, waiting for transfers between devices, group_shift(): return lax.ppermute(array, ('grp', 'pb'), pairs)  10.3 us
    ppermute x2, starting transfers between devices, partner_swap(): return lax.ppermute(array, ('grp', 'pb'), pairs)  7.82 us
    ppermute x9, waiting for transfers between devices, plane_shift(): return lax.ppermute(array, 'pb', pairs)  7.25 us
    pallas_call x1, Pallas kernels, block_grads(): pl.pallas_call(functools.partial(block_kernel, capacity, sides), in_specs...  6.37 us
  transfers between devices with their start and end apart: 20, of which 9 were waited for; matrix products, arithmetic and copies ran while one was open for 0% of the time, Pallas kernels for 9%

profile of v4, /device:TPU:24, one launch (start us, length us, event | category | flops | bytes accessed | tf_op | source)
XLA Modules:
  0.0 184.3 jit_solution(18109298895245960370)
XLA Ops:
  9.5 3.4 %collective-permute-start.1 = (bf16[512,256]{1,0:T(8,128)(2,1)}, bf16[512,256]{1,0:T(8,128)(2,1)S(1)}, u32[]{:S(2)}, u32[]{:S(2)}) collective-permute-start(bf16[512,256]{1,0:T(8,128)(2,1)} %param.13), channel_id=1, source_target_pairs={{0,8},{1,3},{2,10},{3,5},{4,12},{5,7},{6,14},{7,1},{8,16},{9,11},{... | collective-permute-start | bytes 786440 | tf_op jit(solution)/shard_map/ppermute | solution.py:383
  12.9 3.7 %collective-permute-start.2 = (bf16[512,256]{1,0:T(8,128)(2,1)}, bf16[512,256]{1,0:T(8,128)(2,1)S(1)}, u32[]{:S(2)}, u32[]{:S(2)}) collective-permute-start(bf16[512,256]{1,0:T(8,128)(2,1)} %param.13), channel_id=1, source_target_pairs={{0,24},{1,7},{2,26},{3,1},{4,28},{5,3},{6,30},{7,5},{8,0},{9,15},{... | collective-permute-start | bytes 786440 | tf_op jit(solution)/shard_map/ppermute | solution.py:383
  16.6 3.7 %collective-permute-start.3 = (bf16[512,256]{1,0:T(8,128)(2,1)}, bf16[512,256]{1,0:T(8,128)(2,1)S(1)}, u32[]{:S(2)}, u32[]{:S(2)}) collective-permute-start(bf16[512,256]{1,0:T(8,128)(2,1)} %param.13), channel_id=1, source_target_pairs={{0,16},{1,5},{2,18},{3,7},{4,20},{5,1},{6,22},{7,3},{8,24},{9,13},... | collective-permute-start | bytes 786440 | tf_op jit(solution)/shard_map/ppermute | solution.py:383
  20.4 1.6 copy-done.1
  23.2 2.0 %collective-permute-start = (bf16[16,128,256]{2,1,0:T(8,128)(2,1)}, bf16[16,128,256]{2,1,0:T(8,128)(2,1)S(1)}, u32[]{:S(2)}, u32[]{:S(2)}) collective-permute-start(bf16[16,128,256]{2,1,0:T(8,128)(2,1)} %get-tuple-element.29), channel_id=1, source_target_pairs={{0,1},{1,0},{2,3},{3,2},{4,5},{5,4},{6,7},{7,6},{8,9},{9,8},{10,11... | collective-permute-start | bytes 3145736 | tf_op jit(solution)/shard_map/ppermute | solution.py:387
  26.7 7.5 %collective-permute-start.4 = (bf16[4,256,256]{2,1,0:T(8,128)(2,1)S(1)}, bf16[4,256,256]{2,1,0:T(8,128)(2,1)}, u32[]{:S(2)}, u32[]{:S(2)}) collective-permute-start(bf16[4,256,256]{2,1,0:T(8,128)(2,1)S(1)} %pad_maximum_fusion.refs_0_), channel_id=1, source_target_pairs={{0,2},{1,9},{2,4},{3,11},{4,6},{5,13},{6,0},{7,15},{8,10},{9,17},{... | collective-permute-start | bytes 1572872 | tf_op jit(solution)/shard_map/ppermute | solution.py:383
  34.3 1.9 %collective-permute-start.6 = (bf16[4,256,256]{2,1,0:T(8,128)(2,1)S(1)}, bf16[4,256,256]{2,1,0:T(8,128)(2,1)}, u32[]{:S(2)}, u32[]{:S(2)}) collective-permute-start(bf16[4,256,256]{2,1,0:T(8,128)(2,1)S(1)} %pad_maximum_fusion.1.refs_1_), channel_id=1, source_target_pairs={{0,6},{1,25},{2,0},{3,27},{4,2},{5,29},{6,4},{7,31},{8,14},{9,1},{... | collective-permute-start | bytes 1572872 | tf_op jit(solution)/shard_map/ppermute | solution.py:383
  36.2 5.1 %collective-permute-start.9 = (bf16[4,256,256]{2,1,0:T(8,128)(2,1)S(1)}, bf16[4,256,256]{2,1,0:T(8,128)(2,1)}, u32[]{:S(2)}, u32[]{:S(2)}) collective-permute-start(bf16[4,256,256]{2,1,0:T(8,128)(2,1)S(1)} %pad_maximum_fusion.1.refs_1_), channel_id=1, source_target_pairs={{0,2},{1,9},{2,4},{3,11},{4,6},{5,13},{6,0},{7,15},{8,10},{9,17},{... | collective-permute-start | bytes 1572872 | tf_op jit(solution)/shard_map/ppermute | solution.py:383
  41.4 1.9 %collective-permute-start.8 = (bf16[4,256,256]{2,1,0:T(8,128)(2,1)S(1)}, bf16[4,256,256]{2,1,0:T(8,128)(2,1)}, u32[]{:S(2)}, u32[]{:S(2)}) collective-permute-start(bf16[4,256,256]{2,1,0:T(8,128)(2,1)S(1)} %pad_maximum_fusion.refs_0_), channel_id=1, source_target_pairs={{0,6},{1,25},{2,0},{3,27},{4,2},{5,29},{6,4},{7,31},{8,14},{9,1},{... | collective-permute-start | bytes 1572872 | tf_op jit(solution)/shard_map/ppermute | solution.py:383
  43.3 5.1 %collective-permute-start.5 = (bf16[4,256,256]{2,1,0:T(8,128)(2,1)}, bf16[4,256,256]{2,1,0:T(8,128)(2,1)}, u32[]{:S(2)}, u32[]{:S(2)}) collective-permute-start(bf16[4,256,256]{2,1,0:T(8,128)(2,1)} %collective-permute-done.4.refs_0_), channel_id=1, source_target_pairs={{0,2},{1,9},{2,4},{3,11},{4,6},{5,13},{6,0},{7,15},{8,10},{9,17},{... | collective-permute-start | bytes 1572872 | tf_op jit(solution)/shard_map/ppermute | solution.py:383
  48.4 1.9 %collective-permute-start.7 = (bf16[4,256,256]{2,1,0:T(8,128)(2,1)}, bf16[4,256,256]{2,1,0:T(8,128)(2,1)}, u32[]{:S(2)}, u32[]{:S(2)}) collective-permute-start(bf16[4,256,256]{2,1,0:T(8,128)(2,1)} %collective-permute-done.6.refs_1_), channel_id=1, source_target_pairs={{0,6},{1,25},{2,0},{3,27},{4,2},{5,29},{6,4},{7,31},{8,14},{9,1},{... | collective-permute-start | bytes 1572872 | tf_op jit(solution)/shard_map/ppermute | solution.py:383
  51.6 1.7 shard_map.111
  53.7 1.7 shard_map.112
  55.5 5.6 %collective-permute-done.7.refs_1_ = bf16[4,256,256]{2,1,0:T(8,128)(2,1)} collective-permute-done((bf16[4,256,256]{2,1,0:T(8,128)(2,1)}, bf16[4,256,256]{2,1,0:T(8,128)(2,1)}, u32[]{:S(2)}, u32[]{:S(2)}) %collective-permute-start.7) | collective-permute-done | bytes 524320 | tf_op jit(solution)/shard_map/ppermute | solution.py:383
  61.0 1.7 shard_map.113
  62.7 1.9 %collective-permute-start.10 = (f32[512,128]{1,0:T(8,128)S(1)}, f32[512,128]{1,0:T(8,128)S(1)}, u32[]{:S(2)}, u32[]{:S(2)}) collective-permute-start(f32[512,128]{1,0:T(8,128)S(1)} %get-tuple-element.37), channel_id=1, source_target_pairs={{0,1},{1,0},{2,3},{3,2},{4,5},{5,4},{6,7},{7,6},{8,9},{9,8},{10,11... | collective-permute-start | bytes 786440 | tf_op jit(solution)/shard_map/ppermute | solution.py:387
  66.3 31.7 %all-gather = bf16[2240,128]{1,0:T(8,128)(2,1)S(1)} all-gather(bf16[560,128]{1,0:T(8,128)(2,1)S(1)} %shard_map.115), channel_id=2, replica_groups={{0,128,256,384},{32,160,288,416},{64,192,320,448},{96,224,352,480},{1,1..., dimensions={0}, use_global_device_ids=true | all-gather | bytes 716800 | tf_op jit(solution)/shard_map/all_gather | solution.py:462
  100.4 2.9 %collective-permute-start.13 = (bf16[4,272,128]{2,1,0:T(8,128)(2,1)}, bf16[4,272,128]{2,1,0:T(8,128)(2,1)S(1)}, u32[]{:S(2)}, u32[]{:S(2)}) collective-permute-start(bf16[4,272,128]{2,1,0:T(8,128)(2,1)} %shard_map.121), channel_id=1, source_target_pairs={{0,64},{1,449},{2,66},{3,451},{4,68},{5,453},{6,70},{7,455},{8,72}... | collective-permute-start | bytes 835592 | tf_op jit(solution)/shard_map/ppermute | solution.py:397
  104.7 3.6 %collective-permute-start.12 = (bf16[4,272,128]{2,1,0:T(8,128)(2,1)}, bf16[4,272,128]{2,1,0:T(8,128)(2,1)S(1)}, u32[]{:S(2)}, u32[]{:S(2)}) collective-permute-start(bf16[4,272,128]{2,1,0:T(8,128)(2,1)} %shard_map.120), channel_id=1, source_target_pairs={{0,480},{1,481},{2,482},{3,483},{4,484},{5,485},{6,486},{7,487},{8... | collective-permute-start | bytes 835592 | tf_op jit(solution)/shard_map/ppermute | solution.py:397
  109.6 2.6 %collective-permute-start.11 = (bf16[4,272,128]{2,1,0:T(8,128)(2,1)}, bf16[4,272,128]{2,1,0:T(8,128)(2,1)}, u32[]{:S(2)}, u32[]{:S(2)}) collective-permute-start(bf16[4,272,128]{2,1,0:T(8,128)(2,1)} %shard_map.119), channel_id=1, source_target_pairs={{0,32},{1,33},{2,34},{3,35},{4,36},{5,37},{6,38},{7,39},{8,40},{9,... | collective-permute-start | bytes 835592 | tf_op jit(solution)/shard_map/ppermute | solution.py:397
  113.1 1.6 copy-done
  114.7 3.1 %shard_map.117 = (bf16[4,272,128]{2,1,0:T(8,128)(2,1)S(1)}, bf16[4,272,128]{2,1,0:T(8,128)(2,1)S(1)}, bf16[4,272,128]{2,1,0:T(8,128)(2,1)S(1)}, bf16[4,272,128]{2,1,0:T(8,128)(2,1)S(1)}) custom-call(s32[1]{0:T(128)} %bitcast.22.group_ref, s32[16]{0:T(128)S(1)} %stack.147.sources_ref, s32[1,128]{1,0:T(1,128)S(1)} %copy-done.8, bf16[16,560,128]{2,1,0:T(8,128)(2,1)S(1)} %bitcast.68), custom_call_target="tpu_custom_call" | custom-call | tf_op jit(solution)/shard_map/pallas_call | solution.py:260
  117.8 2.3 %collective-permute-done.11.refs_5_ = bf16[4,272,128]{2,1,0:T(8,128)(2,1)} collective-permute-done((bf16[4,272,128]{2,1,0:T(8,128)(2,1)}, bf16[4,272,128]{2,1,0:T(8,128)(2,1)}, u32[]{:S(2)}, u32[]{:S(2)}) %collective-permute-start.11) | collective-permute-done | bytes 278560 | tf_op jit(solution)/shard_map/ppermute | solution.py:397
  120.2 6.4 %shard_map.122 = (bf16[4,256,128]{2,1,0:T(8,128)(2,1)S(1)}, bf16[4,256,128]{2,1,0:T(8,128)(2,1)}, bf16[4,256,128]{2,1,0:T(8,128)(2,1)}, bf16[4,256,128]{2,1,0:T(8,128)(2,1)}) custom-call(s32[8]{0:T(128)S(1)} %bitcast.71, bf16[4,272,128]{2,1,0:T(8,128)(2,1)S(1)} %get-tuple-element.40.refs_0_, bf16[4,272,128]{2,1,0:T(8,128)(2,1)S(1)} %get-tuple-element.41.refs_1_, ...), custom_call_target="tpu_custom_call" | custom-call | tf_op jit(solution)/shard_map/pallas_call | solution.py:365
  126.5 2.7 %collective-permute-start.14 = (bf16[4,256,128]{2,1,0:T(8,128)(2,1)}, bf16[4,256,128]{2,1,0:T(8,128)(2,1)S(1)}, u32[]{:S(2)}, u32[]{:S(2)}) collective-permute-start(bf16[4,256,128]{2,1,0:T(8,128)(2,1)} %get-tuple-element.45), channel_id=1, source_target_pairs={{0,480},{1,481},{2,482},{3,483},{4,484},{5,485},{6,486},{7,487},{8... | collective-permute-start | bytes 786440 | tf_op jit(solution)/shard_map/ppermute | solution.py:397
  129.2 3.2 %collective-permute-start.15 = (bf16[4,256,128]{2,1,0:T(8,128)(2,1)}, bf16[4,256,128]{2,1,0:T(8,128)(2,1)S(1)}, u32[]{:S(2)}, u32[]{:S(2)}) collective-permute-start(bf16[4,256,128]{2,1,0:T(8,128)(2,1)} %get-tuple-element.46), channel_id=1, source_target_pairs={{0,32},{1,33},{2,34},{3,35},{4,36},{5,37},{6,38},{7,39},{8,40},{9,... | collective-permute-start | bytes 786440 | tf_op jit(solution)/shard_map/ppermute | solution.py:397
  132.4 3.8 %collective-permute-start.16 = (bf16[4,256,128]{2,1,0:T(8,128)(2,1)}, bf16[4,256,128]{2,1,0:T(8,128)(2,1)S(1)}, u32[]{:S(2)}, u32[]{:S(2)}) collective-permute-start(bf16[4,256,128]{2,1,0:T(8,128)(2,1)} %get-tuple-element.47), channel_id=1, source_target_pairs={{0,448},{1,65},{2,450},{3,67},{4,452},{5,69},{6,454},{7,71},{8,456... | collective-permute-start | bytes 786440 | tf_op jit(solution)/shard_map/ppermute | solution.py:397
  136.3 7.3 %collective-permute-done.15.refs_2_ = bf16[4,256,128]{2,1,0:T(8,128)(2,1)S(1)} collective-permute-done((bf16[4,256,128]{2,1,0:T(8,128)(2,1)}, bf16[4,256,128]{2,1,0:T(8,128)(2,1)S(1)}, u32[]{:S(2)}, u32[]{:S(2)}) %collective-permute-start.15) | collective-permute-done | bytes 262176 | tf_op jit(solution)/shard_map/ppermute | solution.py:397
  145.7 5.3 %collective-permute-start.17 = (bf16[2,512,128]{2,1,0:T(8,128)(2,1)S(1)}, bf16[2,512,128]{2,1,0:T(8,128)(2,1)S(1)}, u32[]{:S(2)}, u32[]{:S(2)}) collective-permute-start(bf16[2,512,128]{2,1,0:T(8,128)(2,1)S(1)} %get-tuple-element.49), channel_id=1, source_target_pairs={{0,128},{1,385},{2,130},{3,387},{4,132},{5,389},{6,134},{7,391},{8... | collective-permute-start | bytes 786440 | tf_op jit(solution)/shard_map/ppermute | solution.py:408
  150.9 14.1 %collective-permute-done.17 = bf16[2,512,128]{2,1,0:T(8,128)(2,1)S(1)} collective-permute-done((bf16[2,512,128]{2,1,0:T(8,128)(2,1)S(1)}, bf16[2,512,128]{2,1,0:T(8,128)(2,1)S(1)}, u32[]{:S(2)}, u32[]{:S(2)}) %collective-permute-start.17) | collective-permute-done | bytes 262176 | tf_op jit(solution)/shard_map/ppermute | solution.py:408
  165.2 2.5 %collective-permute-start.18 = (bf16[512,128]{1,0:T(8,128)(2,1)S(1)}, bf16[512,128]{1,0:T(8,128)(2,1)S(1)}, u32[]{:S(2)}, u32[]{:S(2)}) collective-permute-start(bf16[512,128]{1,0:T(8,128)(2,1)S(1)} %fusion.1), channel_id=1, source_target_pairs={{0,384},{1,129},{2,386},{3,131},{4,388},{5,133},{6,390},{7,135},{8... | collective-permute-start | bytes 393224 | tf_op jit(solution)/shard_map/ppermute | solution.py:408
  167.7 9.0 %collective-permute-done.18 = bf16[512,128]{1,0:T(8,128)(2,1)S(1)} collective-permute-done((bf16[512,128]{1,0:T(8,128)(2,1)S(1)}, bf16[512,128]{1,0:T(8,128)(2,1)S(1)}, u32[]{:S(2)}, u32[]{:S(2)}) %collective-permute-start.18) | collective-permute-done | bytes 131104 | tf_op jit(solution)/shard_map/ppermute | solution.py:408
  (63 shorter events, 17.7 us)
Async XLA Ops:
  6.5 106.5 %all-gather.4.cloned.1.call-start = ((), (), s32[]{:S(2)}) async-start(), calls=%async_computation | async-start | bytes 2437120 | tf_op jit(solution)/shard_map/all_gather | solution.py:438
  6.5 0.9 copy-start.5
  7.4 0.7 copy-start.6
  8.1 0.7 copy-start.7
  8.8 16.4 %copy-start.10 = (bf16[512,256]{1,0:T(8,128)(2,1)S(1)}, bf16[512,256]{1,0:T(8,128)(2,1)}, u32[]{:S(2)}) copy-start(bf16[512,256]{1,0:T(8,128)(2,1)} %param.13) | copy-start | bytes 786436
  9.5 15.8 %collective-permute-start.1 = (bf16[512,256]{1,0:T(8,128)(2,1)}, bf16[512,256]{1,0:T(8,128)(2,1)S(1)}, u32[]{:S(2)}, u32[]{:S(2)}) collective-permute-start(bf16[512,256]{1,0:T(8,128)(2,1)} %param.13), channel_id=1, source_target_pairs={{0,8},{1,3},{2,10},{3,5},{4,12},{5,7},{6,14},{7,1},{8,16},{9,11},{... | collective-permute-start | bytes 786440 | tf_op jit(solution)/shard_map/ppermute | solution.py:383
  12.9 12.4 %collective-permute-start.2 = (bf16[512,256]{1,0:T(8,128)(2,1)}, bf16[512,256]{1,0:T(8,128)(2,1)S(1)}, u32[]{:S(2)}, u32[]{:S(2)}) collective-permute-start(bf16[512,256]{1,0:T(8,128)(2,1)} %param.13), channel_id=1, source_target_pairs={{0,24},{1,7},{2,26},{3,1},{4,28},{5,3},{6,30},{7,5},{8,0},{9,15},{... | collective-permute-start | bytes 786440 | tf_op jit(solution)/shard_map/ppermute | solution.py:383
  16.6 10.0 %collective-permute-start.3 = (bf16[512,256]{1,0:T(8,128)(2,1)}, bf16[512,256]{1,0:T(8,128)(2,1)S(1)}, u32[]{:S(2)}, u32[]{:S(2)}) collective-permute-start(bf16[512,256]{1,0:T(8,128)(2,1)} %param.13), channel_id=1, source_target_pairs={{0,16},{1,5},{2,18},{3,7},{4,20},{5,1},{6,22},{7,3},{8,24},{9,13},... | collective-permute-start | bytes 786440 | tf_op jit(solution)/shard_map/ppermute | solution.py:383
  20.4 1.6 copy-start.1
  23.2 27.2 %copy-start.11 = (s32[4]{0:T(128)S(1)}, s32[4]{0:T(128)}, u32[]{:S(2)}) copy-start(s32[4]{0:T(128)} %constant.198) | copy-start | bytes 52
  23.2 27.4 %collective-permute-start = (bf16[16,128,256]{2,1,0:T(8,128)(2,1)}, bf16[16,128,256]{2,1,0:T(8,128)(2,1)S(1)}, u32[]{:S(2)}, u32[]{:S(2)}) collective-permute-start(bf16[16,128,256]{2,1,0:T(8,128)(2,1)} %get-tuple-element.29), channel_id=1, source_target_pairs={{0,1},{1,0},{2,3},{3,2},{4,5},{5,4},{6,7},{7,6},{8,9},{9,8},{10,11... | collective-permute-start | bytes 3145736 | tf_op jit(solution)/shard_map/ppermute | solution.py:387
  26.7 16.6 %collective-permute-start.4 = (bf16[4,256,256]{2,1,0:T(8,128)(2,1)S(1)}, bf16[4,256,256]{2,1,0:T(8,128)(2,1)}, u32[]{:S(2)}, u32[]{:S(2)}) collective-permute-start(bf16[4,256,256]{2,1,0:T(8,128)(2,1)S(1)} %pad_maximum_fusion.refs_0_), channel_id=1, source_target_pairs={{0,2},{1,9},{2,4},{3,11},{4,6},{5,13},{6,0},{7,15},{8,10},{9,17},{... | collective-permute-start | bytes 1572872 | tf_op jit(solution)/shard_map/ppermute | solution.py:383
  34.3 14.2 %collective-permute-start.6 = (bf16[4,256,256]{2,1,0:T(8,128)(2,1)S(1)}, bf16[4,256,256]{2,1,0:T(8,128)(2,1)}, u32[]{:S(2)}, u32[]{:S(2)}) collective-permute-start(bf16[4,256,256]{2,1,0:T(8,128)(2,1)S(1)} %pad_maximum_fusion.1.refs_1_), channel_id=1, source_target_pairs={{0,6},{1,25},{2,0},{3,27},{4,2},{5,29},{6,4},{7,31},{8,14},{9,1},{... | collective-permute-start | bytes 1572872 | tf_op jit(solution)/shard_map/ppermute | solution.py:383
  36.2 15.4 %collective-permute-start.9 = (bf16[4,256,256]{2,1,0:T(8,128)(2,1)S(1)}, bf16[4,256,256]{2,1,0:T(8,128)(2,1)}, u32[]{:S(2)}, u32[]{:S(2)}) collective-permute-start(bf16[4,256,256]{2,1,0:T(8,128)(2,1)S(1)} %pad_maximum_fusion.1.refs_1_), channel_id=1, source_target_pairs={{0,2},{1,9},{2,4},{3,11},{4,6},{5,13},{6,0},{7,15},{8,10},{9,17},{... | collective-permute-start | bytes 1572872 | tf_op jit(solution)/shard_map/ppermute | solution.py:383
  41.4 12.4 %collective-permute-start.8 = (bf16[4,256,256]{2,1,0:T(8,128)(2,1)S(1)}, bf16[4,256,256]{2,1,0:T(8,128)(2,1)}, u32[]{:S(2)}, u32[]{:S(2)}) collective-permute-start(bf16[4,256,256]{2,1,0:T(8,128)(2,1)S(1)} %pad_maximum_fusion.refs_0_), channel_id=1, source_target_pairs={{0,6},{1,25},{2,0},{3,27},{4,2},{5,29},{6,4},{7,31},{8,14},{9,1},{... | collective-permute-start | bytes 1572872 | tf_op jit(solution)/shard_map/ppermute | solution.py:383
  43.3 12.2 %collective-permute-start.5 = (bf16[4,256,256]{2,1,0:T(8,128)(2,1)}, bf16[4,256,256]{2,1,0:T(8,128)(2,1)}, u32[]{:S(2)}, u32[]{:S(2)}) collective-permute-start(bf16[4,256,256]{2,1,0:T(8,128)(2,1)} %collective-permute-done.4.refs_0_), channel_id=1, source_target_pairs={{0,2},{1,9},{2,4},{3,11},{4,6},{5,13},{6,0},{7,15},{8,10},{9,17},{... | collective-permute-start | bytes 1572872 | tf_op jit(solution)/shard_map/ppermute | solution.py:383
  48.4 12.6 %collective-permute-start.7 = (bf16[4,256,256]{2,1,0:T(8,128)(2,1)}, bf16[4,256,256]{2,1,0:T(8,128)(2,1)}, u32[]{:S(2)}, u32[]{:S(2)}) collective-permute-start(bf16[4,256,256]{2,1,0:T(8,128)(2,1)} %collective-permute-done.6.refs_1_), channel_id=1, source_target_pairs={{0,6},{1,25},{2,0},{3,27},{4,2},{5,29},{6,4},{7,31},{8,14},{9,1},{... | collective-permute-start | bytes 1572872 | tf_op jit(solution)/shard_map/ppermute | solution.py:383
  55.4 10.7 %copy-start.4 = (bf16[512,128]{1,0:T(8,128)(2,1)S(1)}, bf16[512,128]{1,0:T(8,128)(2,1)}, u32[]{:S(2)}) copy-start(bf16[512,128]{1,0:T(8,128)(2,1)} %outputs_ref.1) | copy-start | bytes 393220
  61.0 37.0 %copy-start.8 = (s32[1,128]{1,0:T(1,128)S(1)}, s32[1,128]{1,0:T(1,128)}, u32[]{:S(2)}) copy-start(s32[1,128]{1,0:T(1,128)} %table_ref.3) | copy-start | bytes 1540
  62.7 3.4 %collective-permute-start.10 = (f32[512,128]{1,0:T(8,128)S(1)}, f32[512,128]{1,0:T(8,128)S(1)}, u32[]{:S(2)}, u32[]{:S(2)}) collective-permute-start(f32[512,128]{1,0:T(8,128)S(1)} %get-tuple-element.37), channel_id=1, source_target_pairs={{0,1},{1,0},{2,3},{3,2},{4,5},{5,4},{6,7},{7,6},{8,9},{9,8},{10,11... | collective-permute-start | bytes 786440 | tf_op jit(solution)/shard_map/ppermute | solution.py:387
  100.4 17.4 %collective-permute-start.13 = (bf16[4,272,128]{2,1,0:T(8,128)(2,1)}, bf16[4,272,128]{2,1,0:T(8,128)(2,1)S(1)}, u32[]{:S(2)}, u32[]{:S(2)}) collective-permute-start(bf16[4,272,128]{2,1,0:T(8,128)(2,1)} %shard_map.121), channel_id=1, source_target_pairs={{0,64},{1,449},{2,66},{3,451},{4,68},{5,453},{6,70},{7,455},{8,72}... | collective-permute-start | bytes 835592 | tf_op jit(solution)/shard_map/ppermute | solution.py:397
  104.7 13.1 %collective-permute-start.12 = (bf16[4,272,128]{2,1,0:T(8,128)(2,1)}, bf16[4,272,128]{2,1,0:T(8,128)(2,1)S(1)}, u32[]{:S(2)}, u32[]{:S(2)}) collective-permute-start(bf16[4,272,128]{2,1,0:T(8,128)(2,1)} %shard_map.120), channel_id=1, source_target_pairs={{0,480},{1,481},{2,482},{3,483},{4,484},{5,485},{6,486},{7,487},{8... | collective-permute-start | bytes 835592 | tf_op jit(solution)/shard_map/ppermute | solution.py:397
  109.6 10.6 %copy-start.2 = (bf16[1,8,512,128]{3,2,1,0:T(8,128)(2,1)S(1)}, bf16[1,8,512,128]{3,2,1,0:T(8,128)(2,1)}, u32[]{:S(2)}) copy-start(bf16[1,8,512,128]{3,2,1,0:T(8,128)(2,1)} %refs_8_.1) | copy-start | bytes 3145732
  109.6 10.6 %copy-start.9 = (s32[1,8]{1,0:T(1,128)S(1)}, s32[1,8]{1,0:T(1,128)}, u32[]{:S(2)}) copy-start(s32[1,8]{1,0:T(1,128)} %param.18) | copy-start | bytes 100
  109.6 10.5 %collective-permute-start.11 = (bf16[4,272,128]{2,1,0:T(8,128)(2,1)}, bf16[4,272,128]{2,1,0:T(8,128)(2,1)}, u32[]{:S(2)}, u32[]{:S(2)}) collective-permute-start(bf16[4,272,128]{2,1,0:T(8,128)(2,1)} %shard_map.119), channel_id=1, source_target_pairs={{0,32},{1,33},{2,34},{3,35},{4,36},{5,37},{6,38},{7,39},{8,40},{9,... | collective-permute-start | bytes 835592 | tf_op jit(solution)/shard_map/ppermute | solution.py:397
  113.1 1.6 copy-start
  114.7 5.4 %copy-start.3 = (bf16[1,8,512,128]{3,2,1,0:T(8,128)(2,1)S(1)}, bf16[1,8,512,128]{3,2,1,0:T(8,128)(2,1)}, u32[]{:S(2)}) copy-start(bf16[1,8,512,128]{3,2,1,0:T(8,128)(2,1)} %refs_9_.1) | copy-start | bytes 3145732
  126.5 9.8 %collective-permute-start.14 = (bf16[4,256,128]{2,1,0:T(8,128)(2,1)}, bf16[4,256,128]{2,1,0:T(8,128)(2,1)S(1)}, u32[]{:S(2)}, u32[]{:S(2)}) collective-permute-start(bf16[4,256,128]{2,1,0:T(8,128)(2,1)} %get-tuple-element.45), channel_id=1, source_target_pairs={{0,480},{1,481},{2,482},{3,483},{4,484},{5,485},{6,486},{7,487},{8... | collective-permute-start | bytes 786440 | tf_op jit(solution)/shard_map/ppermute | solution.py:397
  129.2 14.4 %collective-permute-start.15 = (bf16[4,256,128]{2,1,0:T(8,128)(2,1)}, bf16[4,256,128]{2,1,0:T(8,128)(2,1)S(1)}, u32[]{:S(2)}, u32[]{:S(2)}) collective-permute-start(bf16[4,256,128]{2,1,0:T(8,128)(2,1)} %get-tuple-element.46), channel_id=1, source_target_pairs={{0,32},{1,33},{2,34},{3,35},{4,36},{5,37},{6,38},{7,39},{8,40},{9,... | collective-permute-start | bytes 786440 | tf_op jit(solution)/shard_map/ppermute | solution.py:397
  132.4 11.9 %collective-permute-start.16 = (bf16[4,256,128]{2,1,0:T(8,128)(2,1)}, bf16[4,256,128]{2,1,0:T(8,128)(2,1)S(1)}, u32[]{:S(2)}, u32[]{:S(2)}) collective-permute-start(bf16[4,256,128]{2,1,0:T(8,128)(2,1)} %get-tuple-element.47), channel_id=1, source_target_pairs={{0,448},{1,65},{2,450},{3,67},{4,452},{5,69},{6,454},{7,71},{8,456... | collective-permute-start | bytes 786440 | tf_op jit(solution)/shard_map/ppermute | solution.py:397
  145.7 19.4 %collective-permute-start.17 = (bf16[2,512,128]{2,1,0:T(8,128)(2,1)S(1)}, bf16[2,512,128]{2,1,0:T(8,128)(2,1)S(1)}, u32[]{:S(2)}, u32[]{:S(2)}) collective-permute-start(bf16[2,512,128]{2,1,0:T(8,128)(2,1)S(1)} %get-tuple-element.49), channel_id=1, source_target_pairs={{0,128},{1,385},{2,130},{3,387},{4,132},{5,389},{6,134},{7,391},{8... | collective-permute-start | bytes 786440 | tf_op jit(solution)/shard_map/ppermute | solution.py:408
  165.2 11.6 %collective-permute-start.18 = (bf16[512,128]{1,0:T(8,128)(2,1)S(1)}, bf16[512,128]{1,0:T(8,128)(2,1)S(1)}, u32[]{:S(2)}, u32[]{:S(2)}) collective-permute-start(bf16[512,128]{1,0:T(8,128)(2,1)S(1)} %fusion.1), channel_id=1, source_target_pairs={{0,384},{1,129},{2,386},{3,131},{4,388},{5,133},{6,390},{7,135},{8... | collective-permute-start | bytes 393224 | tf_op jit(solution)/shard_map/ppermute | solution.py:408
Sparse Core Ops, SparseCore 0:
  9.7 89.5 all-gather.3

commit v5 on v4

--- a/solution.py
+++ b/solution.py
@@ -29,8 +29,7 @@
     rest = row - high
     middle = rest.astype(BF16).astype(F32)
     low = (rest - middle).astype(BF16).astype(F32)
-    pad = jnp.zeros((EXTRA - 3,) + row.shape[1:], F32)
-    return jnp.concatenate([high, middle, low, pad], axis=0)
+    return [high, middle, low]
 
 
 def store_extra(out_ref, extra, tokens):
@@ -76,36 +75,6 @@
         out_shape=jax.ShapeDtypeStruct((payloads.shape[0], table.shape[1], tokens), F32),
         compiler_params=params(),
     )(table, payloads)
-
-
-def query_kernel(query_ref, norm_ref, probes_ref, out_ref, packed_ref):
-    tokens = query_ref.shape[0]
-    pieces = tokens // 128
-    out_ref[0:tokens, :] = query_ref[...]
-    store_extra(out_ref, split_rows(norm_ref[...]), tokens)
-    numbers = probes_ref[...].astype(F32)
-    rows = [
-        numbers[j : j + 1, i * 128 : (i + 1) * 128]
-        for j in range(numbers.shape[0])
-        for i in range(pieces)
-    ]
-    packed = jnp.concatenate(rows, axis=0).astype(BF16)
-    out_ref[tokens + EXTRA * pieces :, :] = packed
-    packed_ref[...] = packed
-
-
-def query_payload(queries, norm_row, probes_t):
-    tokens, width = queries.shape
-    packed = probes_t.shape[0] * tokens // 128
-    rows = tokens + EXTRA * tokens // 128 + packed
-    return pl.pallas_call(
-        query_kernel,
-        out_shape=[
-            jax.ShapeDtypeStruct((rows, width), BF16),
-            jax.ShapeDtypeStruct((packed, 128), BF16),
-        ],
-        compiler_params=params(),
-    )(queries, norm_row, probes_t)
 
 
 def weight_kernel(core_ref, weight_ref, own_ref, other_ref):
@@ -159,24 +128,26 @@
     )(order, own, other, *halves, *sums)
 
 
-def grad_kernel(own_ref, other_ref, outputs_ref, packed_ref, out_ref):
+def grad_kernel(own_ref, other_ref, outputs_ref, norm_ref, packed_ref, out_ref):
     tokens = outputs_ref.shape[0]
     grad = (own_ref[...] + other_ref[...]).astype(BF16)
     out_ref[0:tokens, :] = grad
     product = grad.astype(F32) * outputs_ref[...].astype(F32)
     delta = jnp.sum(product.T, axis=0, keepdims=True)
-    store_extra(out_ref, split_rows(delta), tokens)
+    sides = split_rows(delta) + split_rows(norm_ref[...])
+    sides.append(jnp.zeros((EXTRA - len(sides), tokens), F32))
+    store_extra(out_ref, jnp.concatenate(sides, axis=0), tokens)
     out_ref[tokens + EXTRA * tokens // 128 :, :] = packed_ref[...]
 
 
-def grad_payload(own, other, outputs, packed):
+def grad_payload(own, other, outputs, norm_row, packed):
     tokens, width = outputs.shape
     rows = tokens + EXTRA * tokens // 128 + packed.shape[0]
     return pl.pallas_call(
         grad_kernel,
         out_shape=jax.ShapeDtypeStruct((rows, width), BF16),
         compiler_params=params(),
-    )(own, other, outputs, packed)
+    )(own, other, outputs, norm_row, packed)
 
 
 def choices(ranks, capacity):
@@ -232,17 +203,16 @@
 
 def own_kernel(capacity, tokens, group_ref, sources_ref, table_ref, payload_ref, *refs):
     places = [(i, b) for i, ref in enumerate(refs) for b in range(ref.shape[0])]
-    local_clusters = refs[0].shape[1] * 128 // (128 + EXTRA) // capacity
+    local_clusters = refs[0].shape[1] // capacity
     clusters = table_ref.shape[1]
     slot = lax.broadcasted_iota(jnp.int32, (local_clusters, clusters), 0)
     cluster = lax.broadcasted_iota(jnp.int32, (local_clusters, clusters), 1)
     mine = table_ref[...] == slot + group_ref[0] * local_clusters
     stored = jnp.sum(jnp.where(mine, cluster.astype(F32), 0.0), axis=1, keepdims=True)
-    start = tokens + EXTRA * tokens // 128
     marks = []
     for k in range(len(places)):
         named = jnp.zeros((local_clusters, tokens), F32)
-        for row in probe_rows(payload_ref[sources_ref[k], start:, :], tokens):
+        for row in probe_rows(payload_ref[sources_ref[k], tokens:, :], tokens):
             named += jnp.where(row == stored, 1.0, 0.0)
         marks.append(named)
     marks = jnp.concatenate(marks, axis=0)
@@ -250,13 +220,14 @@
     ranks = jnp.where(marks > 0.5, ranking, -1.0)
     for k, (i, b) in enumerate(places):
         chosen = choices(ranks[k * local_clusters : (k + 1) * local_clusters], capacity)
-        pick_rows(payload_ref.at[sources_ref[k]], chosen, tokens, refs[i].at[b])
+        rows = payload_ref[sources_ref[k], 0:tokens, :]
+        refs[i][b] = jnp.dot(chosen, rows, preferred_element_type=F32).astype(BF16)
 
 
 def own_rows(group, sources, counts, table, payloads, tokens, local_clusters, capacity):
     picked = local_clusters * capacity
     width = payloads.shape[-1]
-    rows = [(count, picked + EXTRA * picked // 128, width) for count in counts]
+    rows = [(count, picked, width) for count in counts]
     return pl.pallas_call(
         functools.partial(own_kernel, capacity, tokens),
         in_specs=[pl.BlockSpec(memory_space=pltpu.SMEM)] * 2
@@ -267,10 +238,9 @@
 
 
 def scatter_kernel(capacity, owners_ref, held_ref, ranks_ref, *refs):
-    partial_refs, (own_ref, pair_ref, kept_ref) = refs[:-3], refs[-3:]
+    partial_refs, places = refs[:-4], refs[-4:]
     local_clusters = partial_refs[0].shape[1] // capacity
-    places = (own_ref, pair_ref.at[0], kept_ref, pair_ref.at[1])
-    for k in (1, 3, 2, 0):
+    for k in (3, 1, 2, 0):
         b = held_ref[k]
         total = None
         for i, partial_ref in enumerate(partial_refs):
@@ -289,21 +259,18 @@
         in_specs=[pl.BlockSpec(memory_space=pltpu.SMEM)] * 2
         + [pl.BlockSpec(memory_space=pltpu.VMEM)] * (1 + len(partials)),
         out_shape=[
-            jax.ShapeDtypeStruct((tokens, width), F32),
-            jax.ShapeDtypeStruct((2, tokens, width), BF16),
-            jax.ShapeDtypeStruct((tokens, width), F32),
+            jax.ShapeDtypeStruct((tokens, width), kind) for kind in (F32, BF16, F32, BF16)
         ],
         compiler_params=params(),
     )(owners, held, ranks, *partials)
 
 
-def unpack_extra(extra_refs, rows_ref, capacity):
+def unpack_extra(extra_refs, delta_ref, norm_ref, capacity):
     places = [(i, b) for i, ref in enumerate(extra_refs) for b in range(ref.shape[0])]
-    senders = len(places)
     per_row = 128 // capacity
     lane = lax.broadcasted_iota(jnp.int32, (2 * EXTRA, 128), 1) // capacity
     for sub in range(per_row):
-        for group in range(senders // per_row):
+        for group in range(len(places) // per_row):
             total = jnp.zeros((2 * EXTRA, 128), F32)
             for k in range(per_row):
                 side, sender = places[group * per_row + k]
@@ -314,9 +281,10 @@
                 total += jnp.where(lane == k, packed, 0.0)
             lanes = slice(group * 128, (group + 1) * 128)
             for half in range(2):
-                rows = total[half * EXTRA : half * EXTRA + 3]
                 cluster = half * per_row + sub
-                rows_ref[cluster : cluster + 1, lanes] = rows[0:1] + rows[1:2] + rows[2:3]
+                for start, ref in ((half * EXTRA, delta_ref), (half * EXTRA + 3, norm_ref)):
+                    rows = [total[start + i : start + i + 1] for i in range(3)]
+                    ref[cluster : cluster + 1, lanes] = rows[0] + rows[1] + rows[2]
 
 
 def block_kernel(capacity, sides, counts_ref, *refs):
@@ -329,8 +297,7 @@
     score_scale = width ** (-0.5)
     arrivals = norm_ref.shape[1]
     behind = slice(local_clusters * capacity, local_clusters * capacity + 2 * EXTRA)
-    unpack_extra([ref.at[:, behind, :] for ref in query_refs], norm_ref, capacity)
-    unpack_extra([ref.at[:, behind, :] for ref in grad_refs], delta_ref, capacity)
+    unpack_extra([ref.at[:, behind, :] for ref in grad_refs], delta_ref, norm_ref, capacity)
     place = lax.broadcasted_iota(jnp.int32, (span, arrivals), 0)
 
     for c in range(local_clusters):
@@ -434,8 +401,8 @@
     owners = jnp.stack([(group + n) % groups for n in near])
     sources = [(group - n) % groups % apart + apart * b for n in near for b in range(SHARED)]
 
-    payload, packed = query_payload(queries, log_norm.reshape(1, token_count), probes[0].T)
-    query_all = lax.all_gather(payload, "grp")
+    packed = probes[0].T.reshape(-1, 128).astype(BF16)
+    query_all = lax.all_gather(jnp.concatenate([queries, packed], axis=0), "grp")
 
     piece = readout_grad.shape[1]
     first = [readout_grad] + [plane_shift(readout_grad, d, 0) for d in TURNS]
@@ -458,7 +425,8 @@
     sums = []
     for turn, halves in enumerate(arrivals):
         sums = partial_product(turn, order, own, other, halves, sums)
-    payload = grad_payload(sums[0], swap_cores(sums[1]), outputs, packed)
+    norm_row = log_norm.reshape(1, token_count)
+    payload = grad_payload(sums[0], swap_cores(sums[1]), outputs, norm_row, packed)
     held = lax.all_gather(payload, "grp", axis_index_groups=sets)
     ranks = rank_slots(held, owner_slots, token_count)
     grad_rows = []
@@ -484,10 +452,11 @@
     ]
     partners = [0, *(core * (p[1] - p[0]) + p[0] for p in (FIRST, SECOND)), SHARED // 2]
     blocks = jnp.stack([group // apart ^ p for p in partners])
-    mine, pair, kept = scatter_rows(owners, blocks, ranks, returned, capacity)
-    came = partner_swap(pair, FIRST).astype(F32)
-    last = partner_swap((kept + came[1]).astype(BF16), SECOND).astype(F32)
-    return (mine + came[0] + last).astype(BF16)
+    mine, near_by, kept, passed = scatter_rows(owners, blocks, ranks, returned, capacity)
+    kept = kept + partner_swap(passed, FIRST).astype(F32)
+    came = partner_swap(near_by, FIRST).astype(F32)
+    last = partner_swap(kept.astype(BF16), SECOND).astype(F32)
+    return (mine + came + last).astype(BF16)
 
 
 def solution(mesh):

time: 186 us -> 183 us (0.984)
  waiting for transfers between devices: 42.2 us -> 35.7 us
  starting transfers between devices: 64.8 us -> 70.1 us
  local copies, waits for them, and re-layouts: 5.79 us -> 3.49 us
  other arithmetic: 1.08 us -> 3.35 us
    ppermute x2 -> x3, waiting for transfers between devices: 23.2 us -> 15.2 us  [partner_swap(): return lax.ppermute(array, ('grp', 'pb'), pairs)]
    ppermute x2 -> x3, starting transfers between devices: 7.82 us -> 13.8 us  [partner_swap(): return lax.ppermute(array, ('grp', 'pb'), pairs)]
    unnamed x24 -> x20, local copies, waits for them, and re-layouts: 5.54 us -> 3.22 us
  transfers between devices with their start and end apart: 20 -> 21, of which waited for: 9 -> 9; matrix products, arithmetic and copies ran while one was open for 0% -> 0% of each run, Pallas kernels for 9% -> 8%
where the time goes in v5:
time: 183 us; the launch traced here: 182 us
  starting transfers between devices  70.1 us (38%)
  waiting for transfers between devices  35.7 us (20%)
  blocking collectives  32 us (17%)
  Pallas kernels  23 us (13%)
  between operations  14 us (8%)
  local copies, waits for them, and re-layouts  3.49 us (2%)
  other arithmetic  3.35 us (2%)
    ppermute x9, starting transfers between devices, plane_shift(): return lax.ppermute(array, 'pb', pairs)  34.3 us
    all_gather x1, blocking collectives, shards(): held = lax.all_gather(payload, 'grp', axis_index_groups=sets)  32 us
    ppermute x6, starting transfers between devices, group_shift(): return lax.ppermute(array, ('grp', 'pb'), pairs)  18.1 us
    ppermute x3, waiting for transfers between devices, partner_swap(): return lax.ppermute(array, ('grp', 'pb'), pairs)  15.2 us
    ppermute x3, starting transfers between devices, partner_swap(): return lax.ppermute(array, ('grp', 'pb'), pairs)  13.8 us
    ppermute x6, waiting for transfers between devices, group_shift(): return lax.ppermute(array, ('grp', 'pb'), pairs)  11.8 us
    ppermute x9, waiting for transfers between devices, plane_shift(): return lax.ppermute(array, 'pb', pairs)  7.25 us
    pallas_call x1, Pallas kernels, block_grads(): pl.pallas_call(functools.partial(block_kernel, capacity, sides), in_specs...  6.38 us
  transfers between devices with their start and end apart: 21, of which 9 were waited for; matrix products, arithmetic and copies ran while one was open for 0% of the time, Pallas kernels for 8%

profile of v5, /device:TPU:24, one launch (start us, length us, event | category | flops | bytes accessed | tf_op | source)
XLA Modules:
  0.0 181.8 jit_solution(7696884545493029177)
XLA Ops:
  8.9 3.4 %collective-permute-start.1 = (bf16[512,256]{1,0:T(8,128)(2,1)}, bf16[512,256]{1,0:T(8,128)(2,1)S(1)}, u32[]{:S(2)}, u32[]{:S(2)}) collective-permute-start(bf16[512,256]{1,0:T(8,128)(2,1)} %param.13), channel_id=1, source_target_pairs={{0,8},{1,3},{2,10},{3,5},{4,12},{5,7},{6,14},{7,1},{8,16},{9,11},{... | collective-permute-start | bytes 786440 | tf_op jit(solution)/shard_map/ppermute | solution.py:350
  12.3 3.7 %collective-permute-start.2 = (bf16[512,256]{1,0:T(8,128)(2,1)}, bf16[512,256]{1,0:T(8,128)(2,1)S(1)}, u32[]{:S(2)}, u32[]{:S(2)}) collective-permute-start(bf16[512,256]{1,0:T(8,128)(2,1)} %param.13), channel_id=1, source_target_pairs={{0,24},{1,7},{2,26},{3,1},{4,28},{5,3},{6,30},{7,5},{8,0},{9,15},{... | collective-permute-start | bytes 786440 | tf_op jit(solution)/shard_map/ppermute | solution.py:350
  16.0 3.7 %collective-permute-start.3 = (bf16[512,256]{1,0:T(8,128)(2,1)}, bf16[512,256]{1,0:T(8,128)(2,1)S(1)}, u32[]{:S(2)}, u32[]{:S(2)}) collective-permute-start(bf16[512,256]{1,0:T(8,128)(2,1)} %param.13), channel_id=1, source_target_pairs={{0,16},{1,5},{2,18},{3,7},{4,20},{5,1},{6,22},{7,3},{8,24},{9,13},... | collective-permute-start | bytes 786440 | tf_op jit(solution)/shard_map/ppermute | solution.py:350
  22.5 2.0 %collective-permute-start = (bf16[16,128,256]{2,1,0:T(8,128)(2,1)}, bf16[16,128,256]{2,1,0:T(8,128)(2,1)S(1)}, u32[]{:S(2)}, u32[]{:S(2)}) collective-permute-start(bf16[16,128,256]{2,1,0:T(8,128)(2,1)} %get-tuple-element.28), channel_id=1, source_target_pairs={{0,1},{1,0},{2,3},{3,2},{4,5},{5,4},{6,7},{7,6},{8,9},{9,8},{10,11... | collective-permute-start | bytes 3145736 | tf_op jit(solution)/shard_map/ppermute | solution.py:354
  26.0 7.5 %collective-permute-start.4 = (bf16[4,256,256]{2,1,0:T(8,128)(2,1)S(1)}, bf16[4,256,256]{2,1,0:T(8,128)(2,1)}, u32[]{:S(2)}, u32[]{:S(2)}) collective-permute-start(bf16[4,256,256]{2,1,0:T(8,128)(2,1)S(1)} %pad_maximum_fusion.refs_0_), channel_id=1, source_target_pairs={{0,2},{1,9},{2,4},{3,11},{4,6},{5,13},{6,0},{7,15},{8,10},{9,17},{... | collective-permute-start | bytes 1572872 | tf_op jit(solution)/shard_map/ppermute | solution.py:350
  33.6 1.9 %collective-permute-start.6 = (bf16[4,256,256]{2,1,0:T(8,128)(2,1)S(1)}, bf16[4,256,256]{2,1,0:T(8,128)(2,1)}, u32[]{:S(2)}, u32[]{:S(2)}) collective-permute-start(bf16[4,256,256]{2,1,0:T(8,128)(2,1)S(1)} %pad_maximum_fusion.1.refs_1_), channel_id=1, source_target_pairs={{0,6},{1,25},{2,0},{3,27},{4,2},{5,29},{6,4},{7,31},{8,14},{9,1},{... | collective-permute-start | bytes 1572872 | tf_op jit(solution)/shard_map/ppermute | solution.py:350
  35.6 5.1 %collective-permute-start.9 = (bf16[4,256,256]{2,1,0:T(8,128)(2,1)S(1)}, bf16[4,256,256]{2,1,0:T(8,128)(2,1)}, u32[]{:S(2)}, u32[]{:S(2)}) collective-permute-start(bf16[4,256,256]{2,1,0:T(8,128)(2,1)S(1)} %pad_maximum_fusion.1.refs_1_), channel_id=1, source_target_pairs={{0,2},{1,9},{2,4},{3,11},{4,6},{5,13},{6,0},{7,15},{8,10},{9,17},{... | collective-permute-start | bytes 1572872 | tf_op jit(solution)/shard_map/ppermute | solution.py:350
  40.7 1.9 %collective-permute-start.8 = (bf16[4,256,256]{2,1,0:T(8,128)(2,1)S(1)}, bf16[4,256,256]{2,1,0:T(8,128)(2,1)}, u32[]{:S(2)}, u32[]{:S(2)}) collective-permute-start(bf16[4,256,256]{2,1,0:T(8,128)(2,1)S(1)} %pad_maximum_fusion.refs_0_), channel_id=1, source_target_pairs={{0,6},{1,25},{2,0},{3,27},{4,2},{5,29},{6,4},{7,31},{8,14},{9,1},{... | collective-permute-start | bytes 1572872 | tf_op jit(solution)/shard_map/ppermute | solution.py:350
  42.6 5.1 %collective-permute-start.5 = (bf16[4,256,256]{2,1,0:T(8,128)(2,1)}, bf16[4,256,256]{2,1,0:T(8,128)(2,1)}, u32[]{:S(2)}, u32[]{:S(2)}) collective-permute-start(bf16[4,256,256]{2,1,0:T(8,128)(2,1)} %collective-permute-done.4.refs_0_), channel_id=1, source_target_pairs={{0,2},{1,9},{2,4},{3,11},{4,6},{5,13},{6,0},{7,15},{8,10},{9,17},{... | collective-permute-start | bytes 1572872 | tf_op jit(solution)/shard_map/ppermute | solution.py:350
  47.8 1.9 %collective-permute-start.7 = (bf16[4,256,256]{2,1,0:T(8,128)(2,1)}, bf16[4,256,256]{2,1,0:T(8,128)(2,1)}, u32[]{:S(2)}, u32[]{:S(2)}) collective-permute-start(bf16[4,256,256]{2,1,0:T(8,128)(2,1)} %collective-permute-done.6.refs_1_), channel_id=1, source_target_pairs={{0,6},{1,25},{2,0},{3,27},{4,2},{5,29},{6,4},{7,31},{8,14},{9,1},{... | collective-permute-start | bytes 1572872 | tf_op jit(solution)/shard_map/ppermute | solution.py:350
  51.0 1.7 shard_map.111
  53.1 1.7 shard_map.112
  54.8 5.6 %collective-permute-done.7.refs_1_ = bf16[4,256,256]{2,1,0:T(8,128)(2,1)} collective-permute-done((bf16[4,256,256]{2,1,0:T(8,128)(2,1)}, bf16[4,256,256]{2,1,0:T(8,128)(2,1)}, u32[]{:S(2)}, u32[]{:S(2)}) %collective-permute-start.7) | collective-permute-done | bytes 524320 | tf_op jit(solution)/shard_map/ppermute | solution.py:350
  60.4 1.7 shard_map.113
  62.1 1.9 %collective-permute-start.10 = (f32[512,128]{1,0:T(8,128)S(1)}, f32[512,128]{1,0:T(8,128)S(1)}, u32[]{:S(2)}, u32[]{:S(2)}) collective-permute-start(f32[512,128]{1,0:T(8,128)S(1)} %get-tuple-element.36), channel_id=1, source_target_pairs={{0,1},{1,0},{2,3},{3,2},{4,5},{5,4},{6,7},{7,6},{8,9},{9,8},{10,11... | collective-permute-start | bytes 786440 | tf_op jit(solution)/shard_map/ppermute | solution.py:354
  65.7 32.0 %all-gather = bf16[2240,128]{1,0:T(8,128)(2,1)S(1)} all-gather(bf16[560,128]{1,0:T(8,128)(2,1)S(1)} %shard_map.114), channel_id=2, replica_groups={{0,128,256,384},{32,160,288,416},{64,192,320,448},{96,224,352,480},{1,1..., dimensions={0}, use_global_device_ids=true | all-gather | bytes 716800 | tf_op jit(solution)/shard_map/all_gather | solution.py:430
  100.1 3.0 %collective-permute-start.13 = (bf16[4,272,128]{2,1,0:T(8,128)(2,1)}, bf16[4,272,128]{2,1,0:T(8,128)(2,1)S(1)}, u32[]{:S(2)}, u32[]{:S(2)}) collective-permute-start(bf16[4,272,128]{2,1,0:T(8,128)(2,1)} %shard_map.120), channel_id=1, source_target_pairs={{0,64},{1,449},{2,66},{3,451},{4,68},{5,453},{6,70},{7,455},{8,72}... | collective-permute-start | bytes 835592 | tf_op jit(solution)/shard_map/ppermute | solution.py:364
  104.5 2.8 %collective-permute-start.12 = (bf16[4,272,128]{2,1,0:T(8,128)(2,1)}, bf16[4,272,128]{2,1,0:T(8,128)(2,1)S(1)}, u32[]{:S(2)}, u32[]{:S(2)}) collective-permute-start(bf16[4,272,128]{2,1,0:T(8,128)(2,1)} %shard_map.119), channel_id=1, source_target_pairs={{0,480},{1,481},{2,482},{3,483},{4,484},{5,485},{6,486},{7,487},{8... | collective-permute-start | bytes 835592 | tf_op jit(solution)/shard_map/ppermute | solution.py:364
  108.7 3.3 %collective-permute-start.11 = (bf16[4,272,128]{2,1,0:T(8,128)(2,1)}, bf16[4,272,128]{2,1,0:T(8,128)(2,1)}, u32[]{:S(2)}, u32[]{:S(2)}) collective-permute-start(bf16[4,272,128]{2,1,0:T(8,128)(2,1)} %shard_map.118), channel_id=1, source_target_pairs={{0,32},{1,33},{2,34},{3,35},{4,36},{5,37},{6,38},{7,39},{8,40},{9,... | collective-permute-start | bytes 835592 | tf_op jit(solution)/shard_map/ppermute | solution.py:364
  114.5 2.0 %shard_map.116 = (bf16[4,256,128]{2,1,0:T(8,128)(2,1)S(1)}, bf16[4,256,128]{2,1,0:T(8,128)(2,1)S(1)}, bf16[4,256,128]{2,1,0:T(8,128)(2,1)S(1)}, bf16[4,256,128]{2,1,0:T(8,128)(2,1)S(1)}) custom-call(s32[1]{0:T(128)} %bitcast.22.group_ref, s32[16]{0:T(128)S(1)} %stack.147.sources_ref, s32[1,128]{1,0:T(1,128)S(1)} %copy-done.6, bf16[16,528,128]{2,1,0:T(8,128)(2,1)S(1)} %bitcast.55), custom_call_target="tpu_custom_call" | custom-call | tf_op jit(solution)/shard_map/pallas_call | solution.py:231
  116.5 3.3 %collective-permute-done.11.refs_5_ = bf16[4,272,128]{2,1,0:T(8,128)(2,1)} collective-permute-done((bf16[4,272,128]{2,1,0:T(8,128)(2,1)}, bf16[4,272,128]{2,1,0:T(8,128)(2,1)}, u32[]{:S(2)}, u32[]{:S(2)}) %collective-permute-start.11) | collective-permute-done | bytes 278560 | tf_op jit(solution)/shard_map/ppermute | solution.py:364
  119.9 6.4 %shard_map.121 = (bf16[4,256,128]{2,1,0:T(8,128)(2,1)S(1)}, bf16[4,256,128]{2,1,0:T(8,128)(2,1)}, bf16[4,256,128]{2,1,0:T(8,128)(2,1)}, bf16[4,256,128]{2,1,0:T(8,128)(2,1)}) custom-call(s32[8]{0:T(128)S(1)} %bitcast.57, bf16[4,256,128]{2,1,0:T(8,128)(2,1)S(1)} %get-tuple-element.37.refs_0_, bf16[4,256,128]{2,1,0:T(8,128)(2,1)S(1)} %get-tuple-element.38.refs_1_, ...), custom_call_target="tpu_custom_call" | custom-call | tf_op jit(solution)/shard_map/pallas_call | solution.py:332
  126.2 2.6 %collective-permute-start.14 = (bf16[4,256,128]{2,1,0:T(8,128)(2,1)}, bf16[4,256,128]{2,1,0:T(8,128)(2,1)S(1)}, u32[]{:S(2)}, u32[]{:S(2)}) collective-permute-start(bf16[4,256,128]{2,1,0:T(8,128)(2,1)} %get-tuple-element.42), channel_id=1, source_target_pairs={{0,480},{1,481},{2,482},{3,483},{4,484},{5,485},{6,486},{7,487},{8... | collective-permute-start | bytes 786440 | tf_op jit(solution)/shard_map/ppermute | solution.py:364
  128.8 3.3 %collective-permute-start.15 = (bf16[4,256,128]{2,1,0:T(8,128)(2,1)}, bf16[4,256,128]{2,1,0:T(8,128)(2,1)S(1)}, u32[]{:S(2)}, u32[]{:S(2)}) collective-permute-start(bf16[4,256,128]{2,1,0:T(8,128)(2,1)} %get-tuple-element.43), channel_id=1, source_target_pairs={{0,32},{1,33},{2,34},{3,35},{4,36},{5,37},{6,38},{7,39},{8,40},{9,... | collective-permute-start | bytes 786440 | tf_op jit(solution)/shard_map/ppermute | solution.py:364
  132.1 3.1 %collective-permute-start.16 = (bf16[4,256,128]{2,1,0:T(8,128)(2,1)}, bf16[4,256,128]{2,1,0:T(8,128)(2,1)S(1)}, u32[]{:S(2)}, u32[]{:S(2)}) collective-permute-start(bf16[4,256,128]{2,1,0:T(8,128)(2,1)} %get-tuple-element.44), channel_id=1, source_target_pairs={{0,448},{1,65},{2,450},{3,67},{4,452},{5,69},{6,454},{7,71},{8,456... | collective-permute-start | bytes 786440 | tf_op jit(solution)/shard_map/ppermute | solution.py:364
  135.3 8.4 %collective-permute-done.15.refs_2_ = bf16[4,256,128]{2,1,0:T(8,128)(2,1)S(1)} collective-permute-done((bf16[4,256,128]{2,1,0:T(8,128)(2,1)}, bf16[4,256,128]{2,1,0:T(8,128)(2,1)S(1)}, u32[]{:S(2)}, u32[]{:S(2)}) %collective-permute-start.15) | collective-permute-done | bytes 262176 | tf_op jit(solution)/shard_map/ppermute | solution.py:364
  145.2 4.9 %collective-permute-start.18 = (bf16[512,128]{1,0:T(8,128)(2,1)S(1)}, bf16[512,128]{1,0:T(8,128)(2,1)S(1)}, u32[]{:S(2)}, u32[]{:S(2)}) collective-permute-start(bf16[512,128]{1,0:T(8,128)(2,1)S(1)} %get-tuple-element.48), channel_id=1, source_target_pairs={{0,128},{1,385},{2,130},{3,387},{4,132},{5,389},{6,134},{7,391},{8... | collective-permute-start | bytes 393224 | tf_op jit(solution)/shard_map/ppermute | solution.py:375
  150.1 4.9 %collective-permute-start.17 = (bf16[512,128]{1,0:T(8,128)(2,1)S(1)}, bf16[512,128]{1,0:T(8,128)(2,1)S(1)}, u32[]{:S(2)}, u32[]{:S(2)}) collective-permute-start(bf16[512,128]{1,0:T(8,128)(2,1)S(1)} %get-tuple-element.46), channel_id=1, source_target_pairs={{0,128},{1,385},{2,130},{3,387},{4,132},{5,389},{6,134},{7,391},{8... | collective-permute-start | bytes 393224 | tf_op jit(solution)/shard_map/ppermute | solution.py:375
  154.9 4.8 %collective-permute-done.18 = bf16[512,128]{1,0:T(8,128)(2,1)S(1)} collective-permute-done((bf16[512,128]{1,0:T(8,128)(2,1)S(1)}, bf16[512,128]{1,0:T(8,128)(2,1)S(1)}, u32[]{:S(2)}, u32[]{:S(2)}) %collective-permute-start.18) | collective-permute-done | bytes 131104 | tf_op jit(solution)/shard_map/ppermute | solution.py:375
  159.8 4.0 %collective-permute-start.19 = (bf16[512,128]{1,0:T(8,128)(2,1)S(1)}, bf16[512,128]{1,0:T(8,128)(2,1)S(1)}, u32[]{:S(2)}, u32[]{:S(2)}) collective-permute-start(bf16[512,128]{1,0:T(8,128)(2,1)S(1)} %add_convert_fusion.1), channel_id=1, source_target_pairs={{0,384},{1,129},{2,386},{3,131},{4,388},{5,133},{6,390},{7,135},{8... | collective-permute-start | bytes 393224 | tf_op jit(solution)/shard_map/ppermute | solution.py:375
  163.8 5.5 %collective-permute-done.17 = bf16[512,128]{1,0:T(8,128)(2,1)S(1)} collective-permute-done((bf16[512,128]{1,0:T(8,128)(2,1)S(1)}, bf16[512,128]{1,0:T(8,128)(2,1)S(1)}, u32[]{:S(2)}, u32[]{:S(2)}) %collective-permute-start.17) | collective-permute-done | bytes 131104 | tf_op jit(solution)/shard_map/ppermute | solution.py:375
  169.4 4.8 %collective-permute-done.19 = bf16[512,128]{1,0:T(8,128)(2,1)S(1)} collective-permute-done((bf16[512,128]{1,0:T(8,128)(2,1)S(1)}, bf16[512,128]{1,0:T(8,128)(2,1)S(1)}, u32[]{:S(2)}, u32[]{:S(2)}) %collective-permute-start.19) | collective-permute-done | bytes 131104 | tf_op jit(solution)/shard_map/ppermute | solution.py:375
  (62 shorter events, 19.5 us)
Async XLA Ops:
  6.5 18.0 %copy-start.8 = (bf16[512,256]{1,0:T(8,128)(2,1)S(1)}, bf16[512,256]{1,0:T(8,128)(2,1)}, u32[]{:S(2)}) copy-start(bf16[512,256]{1,0:T(8,128)(2,1)} %param.13) | copy-start | bytes 786436
  6.5 106.3 %all-gather.4.cloned.1.call-start = ((), (), s32[]{:S(2)}) async-start(), calls=%async_computation | async-start | bytes 2297856 | tf_op jit(solution)/shard_map/all_gather | solution.py:405
  8.9 15.7 %collective-permute-start.1 = (bf16[512,256]{1,0:T(8,128)(2,1)}, bf16[512,256]{1,0:T(8,128)(2,1)S(1)}, u32[]{:S(2)}, u32[]{:S(2)}) collective-permute-start(bf16[512,256]{1,0:T(8,128)(2,1)} %param.13), channel_id=1, source_target_pairs={{0,8},{1,3},{2,10},{3,5},{4,12},{5,7},{6,14},{7,1},{8,16},{9,11},{... | collective-permute-start | bytes 786440 | tf_op jit(solution)/shard_map/ppermute | solution.py:350
  12.3 12.4 %collective-permute-start.2 = (bf16[512,256]{1,0:T(8,128)(2,1)}, bf16[512,256]{1,0:T(8,128)(2,1)S(1)}, u32[]{:S(2)}, u32[]{:S(2)}) collective-permute-start(bf16[512,256]{1,0:T(8,128)(2,1)} %param.13), channel_id=1, source_target_pairs={{0,24},{1,7},{2,26},{3,1},{4,28},{5,3},{6,30},{7,5},{8,0},{9,15},{... | collective-permute-start | bytes 786440 | tf_op jit(solution)/shard_map/ppermute | solution.py:350
  16.0 10.0 %collective-permute-start.3 = (bf16[512,256]{1,0:T(8,128)(2,1)}, bf16[512,256]{1,0:T(8,128)(2,1)S(1)}, u32[]{:S(2)}, u32[]{:S(2)}) collective-permute-start(bf16[512,256]{1,0:T(8,128)(2,1)} %param.13), channel_id=1, source_target_pairs={{0,16},{1,5},{2,18},{3,7},{4,20},{5,1},{6,22},{7,3},{8,24},{9,13},... | collective-permute-start | bytes 786440 | tf_op jit(solution)/shard_map/ppermute | solution.py:350
  19.7 1.6 copy-start.1
  22.5 27.2 %copy-start.9 = (s32[4]{0:T(128)S(1)}, s32[4]{0:T(128)}, u32[]{:S(2)}) copy-start(s32[4]{0:T(128)} %constant.198) | copy-start | bytes 52
  22.5 27.4 %collective-permute-start = (bf16[16,128,256]{2,1,0:T(8,128)(2,1)}, bf16[16,128,256]{2,1,0:T(8,128)(2,1)S(1)}, u32[]{:S(2)}, u32[]{:S(2)}) collective-permute-start(bf16[16,128,256]{2,1,0:T(8,128)(2,1)} %get-tuple-element.28), channel_id=1, source_target_pairs={{0,1},{1,0},{2,3},{3,2},{4,5},{5,4},{6,7},{7,6},{8,9},{9,8},{10,11... | collective-permute-start | bytes 3145736 | tf_op jit(solution)/shard_map/ppermute | solution.py:354
  26.0 16.6 %collective-permute-start.4 = (bf16[4,256,256]{2,1,0:T(8,128)(2,1)S(1)}, bf16[4,256,256]{2,1,0:T(8,128)(2,1)}, u32[]{:S(2)}, u32[]{:S(2)}) collective-permute-start(bf16[4,256,256]{2,1,0:T(8,128)(2,1)S(1)} %pad_maximum_fusion.refs_0_), channel_id=1, source_target_pairs={{0,2},{1,9},{2,4},{3,11},{4,6},{5,13},{6,0},{7,15},{8,10},{9,17},{... | collective-permute-start | bytes 1572872 | tf_op jit(solution)/shard_map/ppermute | solution.py:350
  33.6 14.2 %collective-permute-start.6 = (bf16[4,256,256]{2,1,0:T(8,128)(2,1)S(1)}, bf16[4,256,256]{2,1,0:T(8,128)(2,1)}, u32[]{:S(2)}, u32[]{:S(2)}) collective-permute-start(bf16[4,256,256]{2,1,0:T(8,128)(2,1)S(1)} %pad_maximum_fusion.1.refs_1_), channel_id=1, source_target_pairs={{0,6},{1,25},{2,0},{3,27},{4,2},{5,29},{6,4},{7,31},{8,14},{9,1},{... | collective-permute-start | bytes 1572872 | tf_op jit(solution)/shard_map/ppermute | solution.py:350
  35.6 15.4 %collective-permute-start.9 = (bf16[4,256,256]{2,1,0:T(8,128)(2,1)S(1)}, bf16[4,256,256]{2,1,0:T(8,128)(2,1)}, u32[]{:S(2)}, u32[]{:S(2)}) collective-permute-start(bf16[4,256,256]{2,1,0:T(8,128)(2,1)S(1)} %pad_maximum_fusion.1.refs_1_), channel_id=1, source_target_pairs={{0,2},{1,9},{2,4},{3,11},{4,6},{5,13},{6,0},{7,15},{8,10},{9,17},{... | collective-permute-start | bytes 1572872 | tf_op jit(solution)/shard_map/ppermute | solution.py:350
  40.7 12.4 %collective-permute-start.8 = (bf16[4,256,256]{2,1,0:T(8,128)(2,1)S(1)}, bf16[4,256,256]{2,1,0:T(8,128)(2,1)}, u32[]{:S(2)}, u32[]{:S(2)}) collective-permute-start(bf16[4,256,256]{2,1,0:T(8,128)(2,1)S(1)} %pad_maximum_fusion.refs_0_), channel_id=1, source_target_pairs={{0,6},{1,25},{2,0},{3,27},{4,2},{5,29},{6,4},{7,31},{8,14},{9,1},{... | collective-permute-start | bytes 1572872 | tf_op jit(solution)/shard_map/ppermute | solution.py:350
  42.6 12.2 %collective-permute-start.5 = (bf16[4,256,256]{2,1,0:T(8,128)(2,1)}, bf16[4,256,256]{2,1,0:T(8,128)(2,1)}, u32[]{:S(2)}, u32[]{:S(2)}) collective-permute-start(bf16[4,256,256]{2,1,0:T(8,128)(2,1)} %collective-permute-done.4.refs_0_), channel_id=1, source_target_pairs={{0,2},{1,9},{2,4},{3,11},{4,6},{5,13},{6,0},{7,15},{8,10},{9,17},{... | collective-permute-start | bytes 1572872 | tf_op jit(solution)/shard_map/ppermute | solution.py:350
  47.8 12.6 %collective-permute-start.7 = (bf16[4,256,256]{2,1,0:T(8,128)(2,1)}, bf16[4,256,256]{2,1,0:T(8,128)(2,1)}, u32[]{:S(2)}, u32[]{:S(2)}) collective-permute-start(bf16[4,256,256]{2,1,0:T(8,128)(2,1)} %collective-permute-done.6.refs_1_), channel_id=1, source_target_pairs={{0,6},{1,25},{2,0},{3,27},{4,2},{5,29},{6,4},{7,31},{8,14},{9,1},{... | collective-permute-start | bytes 1572872 | tf_op jit(solution)/shard_map/ppermute | solution.py:350
  54.8 10.8 %copy-start.4 = (bf16[512,128]{1,0:T(8,128)(2,1)S(1)}, bf16[512,128]{1,0:T(8,128)(2,1)}, u32[]{:S(2)}) copy-start(bf16[512,128]{1,0:T(8,128)(2,1)} %outputs_ref.1) | copy-start | bytes 393220
  54.8 10.7 %copy-start.5 = (f32[512,1]{0,1:T(1,128)S(1)}, f32[512,1]{0,1:T(1,128)}, u32[]{:S(2)}) copy-start(f32[512,1]{0,1:T(1,128)} %param.15) | copy-start | bytes 6148
  60.4 37.3 %copy-start.6 = (s32[1,128]{1,0:T(1,128)S(1)}, s32[1,128]{1,0:T(1,128)}, u32[]{:S(2)}) copy-start(s32[1,128]{1,0:T(1,128)} %table_ref.3) | copy-start | bytes 1540
  62.1 3.4 %collective-permute-start.10 = (f32[512,128]{1,0:T(8,128)S(1)}, f32[512,128]{1,0:T(8,128)S(1)}, u32[]{:S(2)}, u32[]{:S(2)}) collective-permute-start(f32[512,128]{1,0:T(8,128)S(1)} %get-tuple-element.36), channel_id=1, source_target_pairs={{0,1},{1,0},{2,3},{3,2},{4,5},{5,4},{6,7},{7,6},{8,9},{9,8},{10,11... | collective-permute-start | bytes 786440 | tf_op jit(solution)/shard_map/ppermute | solution.py:354
  100.1 16.4 %collective-permute-start.13 = (bf16[4,272,128]{2,1,0:T(8,128)(2,1)}, bf16[4,272,128]{2,1,0:T(8,128)(2,1)S(1)}, u32[]{:S(2)}, u32[]{:S(2)}) collective-permute-start(bf16[4,272,128]{2,1,0:T(8,128)(2,1)} %shard_map.120), channel_id=1, source_target_pairs={{0,64},{1,449},{2,66},{3,451},{4,68},{5,453},{6,70},{7,455},{8,72}... | collective-permute-start | bytes 835592 | tf_op jit(solution)/shard_map/ppermute | solution.py:364
  104.5 12.0 %collective-permute-start.12 = (bf16[4,272,128]{2,1,0:T(8,128)(2,1)}, bf16[4,272,128]{2,1,0:T(8,128)(2,1)S(1)}, u32[]{:S(2)}, u32[]{:S(2)}) collective-permute-start(bf16[4,272,128]{2,1,0:T(8,128)(2,1)} %shard_map.119), channel_id=1, source_target_pairs={{0,480},{1,481},{2,482},{3,483},{4,484},{5,485},{6,486},{7,487},{8... | collective-permute-start | bytes 835592 | tf_op jit(solution)/shard_map/ppermute | solution.py:364
  108.7 11.2 %copy-start.2 = (bf16[1,8,512,128]{3,2,1,0:T(8,128)(2,1)S(1)}, bf16[1,8,512,128]{3,2,1,0:T(8,128)(2,1)}, u32[]{:S(2)}) copy-start(bf16[1,8,512,128]{3,2,1,0:T(8,128)(2,1)} %refs_8_.1) | copy-start | bytes 3145732
  108.7 11.2 %copy-start.7 = (s32[1,8]{1,0:T(1,128)S(1)}, s32[1,8]{1,0:T(1,128)}, u32[]{:S(2)}) copy-start(s32[1,8]{1,0:T(1,128)} %param.18) | copy-start | bytes 100
  108.7 11.2 %collective-permute-start.11 = (bf16[4,272,128]{2,1,0:T(8,128)(2,1)}, bf16[4,272,128]{2,1,0:T(8,128)(2,1)}, u32[]{:S(2)}, u32[]{:S(2)}) collective-permute-start(bf16[4,272,128]{2,1,0:T(8,128)(2,1)} %shard_map.118), channel_id=1, source_target_pairs={{0,32},{1,33},{2,34},{3,35},{4,36},{5,37},{6,38},{7,39},{8,40},{9,... | collective-permute-start | bytes 835592 | tf_op jit(solution)/shard_map/ppermute | solution.py:364
  112.8 1.6 copy-start
  114.4 5.4 %copy-start.3 = (bf16[1,8,512,128]{3,2,1,0:T(8,128)(2,1)S(1)}, bf16[1,8,512,128]{3,2,1,0:T(8,128)(2,1)}, u32[]{:S(2)}) copy-start(bf16[1,8,512,128]{3,2,1,0:T(8,128)(2,1)} %refs_9_.1) | copy-start | bytes 3145732
  126.2 9.1 %collective-permute-start.14 = (bf16[4,256,128]{2,1,0:T(8,128)(2,1)}, bf16[4,256,128]{2,1,0:T(8,128)(2,1)S(1)}, u32[]{:S(2)}, u32[]{:S(2)}) collective-permute-start(bf16[4,256,128]{2,1,0:T(8,128)(2,1)} %get-tuple-element.42), channel_id=1, source_target_pairs={{0,480},{1,481},{2,482},{3,483},{4,484},{5,485},{6,486},{7,487},{8... | collective-permute-start | bytes 786440 | tf_op jit(solution)/shard_map/ppermute | solution.py:364
  128.8 14.9 %collective-permute-start.15 = (bf16[4,256,128]{2,1,0:T(8,128)(2,1)}, bf16[4,256,128]{2,1,0:T(8,128)(2,1)S(1)}, u32[]{:S(2)}, u32[]{:S(2)}) collective-permute-start(bf16[4,256,128]{2,1,0:T(8,128)(2,1)} %get-tuple-element.43), channel_id=1, source_target_pairs={{0,32},{1,33},{2,34},{3,35},{4,36},{5,37},{6,38},{7,39},{8,40},{9,... | collective-permute-start | bytes 786440 | tf_op jit(solution)/shard_map/ppermute | solution.py:364
  132.1 11.7 %collective-permute-start.16 = (bf16[4,256,128]{2,1,0:T(8,128)(2,1)}, bf16[4,256,128]{2,1,0:T(8,128)(2,1)S(1)}, u32[]{:S(2)}, u32[]{:S(2)}) collective-permute-start(bf16[4,256,128]{2,1,0:T(8,128)(2,1)} %get-tuple-element.44), channel_id=1, source_target_pairs={{0,448},{1,65},{2,450},{3,67},{4,452},{5,69},{6,454},{7,71},{8,456... | collective-permute-start | bytes 786440 | tf_op jit(solution)/shard_map/ppermute | solution.py:364
  145.2 14.6 %collective-permute-start.18 = (bf16[512,128]{1,0:T(8,128)(2,1)S(1)}, bf16[512,128]{1,0:T(8,128)(2,1)S(1)}, u32[]{:S(2)}, u32[]{:S(2)}) collective-permute-start(bf16[512,128]{1,0:T(8,128)(2,1)S(1)} %get-tuple-element.48), channel_id=1, source_target_pairs={{0,128},{1,385},{2,130},{3,387},{4,132},{5,389},{6,134},{7,391},{8... | collective-permute-start | bytes 393224 | tf_op jit(solution)/shard_map/ppermute | solution.py:375
  150.1 19.3 %collective-permute-start.17 = (bf16[512,128]{1,0:T(8,128)(2,1)S(1)}, bf16[512,128]{1,0:T(8,128)(2,1)S(1)}, u32[]{:S(2)}, u32[]{:S(2)}) collective-permute-start(bf16[512,128]{1,0:T(8,128)(2,1)S(1)} %get-tuple-element.46), channel_id=1, source_target_pairs={{0,128},{1,385},{2,130},{3,387},{4,132},{5,389},{6,134},{7,391},{8... | collective-permute-start | bytes 393224 | tf_op jit(solution)/shard_map/ppermute | solution.py:375
  159.8 14.4 %collective-permute-start.19 = (bf16[512,128]{1,0:T(8,128)(2,1)S(1)}, bf16[512,128]{1,0:T(8,128)(2,1)S(1)}, u32[]{:S(2)}, u32[]{:S(2)}) collective-permute-start(bf16[512,128]{1,0:T(8,128)(2,1)S(1)} %add_convert_fusion.1), channel_id=1, source_target_pairs={{0,384},{1,129},{2,386},{3,131},{4,388},{5,133},{6,390},{7,135},{8... | collective-permute-start | bytes 393224 | tf_op jit(solution)/shard_map/ppermute | solution.py:375
Sparse Core Ops, SparseCore 0:
  9.4 87.9 all-gather.3

commit v6 on v5

--- a/solution.py
+++ b/solution.py
@@ -16,7 +16,7 @@
 TURNS = (1, 3, 2)
 SHARED = 4
 FIRST, SECOND = (1, 3), (3, 1)
-NEAR = ((1, 1), (-1, -1), (2, -2))
+NEAR = ((1, -1), (-1, 1), (2, -2))
 VMEM_BYTES = 48 * 1024 * 1024
 
 
@@ -397,7 +397,7 @@
     core, column, line = place % CORES, place // (CORES * SIDE), place // CORES % SIDE
     apart = groups // SHARED
     sets = [[g + apart * i for i in range(SHARED)] for g in range(apart)]
-    near = [0, 1, -1, 2 - 4 * core]
+    near = [0] + [core * (n[1] - n[0]) + n[0] for n in NEAR]
     owners = jnp.stack([(group + n) % groups for n in near])
     sources = [(group - n) % groups % apart + apart * b for n in near for b in range(SHARED)]
 
@@ -452,7 +452,10 @@
     ]
     partners = [0, *(core * (p[1] - p[0]) + p[0] for p in (FIRST, SECOND)), SHARED // 2]
     blocks = jnp.stack([group // apart ^ p for p in partners])
-    mine, near_by, kept, passed = scatter_rows(owners, blocks, ranks, returned, capacity)
+    back = (0, 3, 1, 2)
+    mine, near_by, kept, passed = scatter_rows(
+        jnp.stack([owners[i] for i in back]), blocks, ranks, [returned[i] for i in back], capacity
+    )
     kept = kept + partner_swap(passed, FIRST).astype(F32)
     came = partner_swap(near_by, FIRST).astype(F32)
     last = partner_swap(kept.astype(BF16), SECOND).astype(F32)

time: 183 us -> 181 us (0.989)
  starting transfers between devices: 70.1 us -> 67.6 us
    ppermute x3, starting transfers between devices: 13.8 us -> 11.7 us  [partner_swap(): return lax.ppermute(array, ('grp', 'pb'), pairs)]
  transfers between devices with their start and end apart: 21 -> 21, of which waited for: 9 -> 11; matrix products, arithmetic and copies ran while one was open for 0% -> 0% of each run, Pallas kernels for 8% -> 8%
where the time goes in v6:
time: 181 us; the launch traced here: 180 us
  starting transfers between devices  67.6 us (37%)
  waiting for transfers between devices  36.2 us (20%)
  blocking collectives  32 us (18%)
  Pallas kernels  23 us (13%)
  between operations  14.1 us (8%)
  local copies, waits for them, and re-layouts  3.49 us (2%)
  other arithmetic  3.35 us (2%)
    ppermute x9, starting transfers between devices, plane_shift(): return lax.ppermute(array, 'pb', pairs)  34.3 us
    all_gather x1, blocking collectives, shards(): held = lax.all_gather(payload, 'grp', axis_index_groups=sets)  32 us
    ppermute x6, starting transfers between devices, group_shift(): return lax.ppermute(array, ('grp', 'pb'), pairs)  17.6 us
    ppermute x3, waiting for transfers between devices, partner_swap(): return lax.ppermute(array, ('grp', 'pb'), pairs)  16.1 us
    ppermute x3, starting transfers between devices, partner_swap(): return lax.ppermute(array, ('grp', 'pb'), pairs)  11.7 us
    ppermute x6, waiting for transfers between devices, group_shift(): return lax.ppermute(array, ('grp', 'pb'), pairs)  11.4 us
    ppermute x9, waiting for transfers between devices, plane_shift(): return lax.ppermute(array, 'pb', pairs)  7.25 us
    pallas_call x1, Pallas kernels, block_grads(): pl.pallas_call(functools.partial(block_kernel, capacity, sides), in_specs...  6.38 us
  transfers between devices with their start and end apart: 21, of which 11 were waited for; matrix products, arithmetic and copies ran while one was open for 0% of the time, Pallas kernels for 8%

profile of v6, /device:TPU:24, one launch (start us, length us, event | category | flops | bytes accessed | tf_op | source)
XLA Modules:
  0.0 179.8 jit_solution(2211187251855394751)
XLA Ops:
  8.9 3.4 %collective-permute-start.1 = (bf16[512,256]{1,0:T(8,128)(2,1)}, bf16[512,256]{1,0:T(8,128)(2,1)S(1)}, u32[]{:S(2)}, u32[]{:S(2)}) collective-permute-start(bf16[512,256]{1,0:T(8,128)(2,1)} %param.13), channel_id=1, source_target_pairs={{0,8},{1,3},{2,10},{3,5},{4,12},{5,7},{6,14},{7,1},{8,16},{9,11},{... | collective-permute-start | bytes 786440 | tf_op jit(solution)/shard_map/ppermute | solution.py:350
  12.3 3.7 %collective-permute-start.2 = (bf16[512,256]{1,0:T(8,128)(2,1)}, bf16[512,256]{1,0:T(8,128)(2,1)S(1)}, u32[]{:S(2)}, u32[]{:S(2)}) collective-permute-start(bf16[512,256]{1,0:T(8,128)(2,1)} %param.13), channel_id=1, source_target_pairs={{0,24},{1,7},{2,26},{3,1},{4,28},{5,3},{6,30},{7,5},{8,0},{9,15},{... | collective-permute-start | bytes 786440 | tf_op jit(solution)/shard_map/ppermute | solution.py:350
  16.0 3.7 %collective-permute-start.3 = (bf16[512,256]{1,0:T(8,128)(2,1)}, bf16[512,256]{1,0:T(8,128)(2,1)S(1)}, u32[]{:S(2)}, u32[]{:S(2)}) collective-permute-start(bf16[512,256]{1,0:T(8,128)(2,1)} %param.13), channel_id=1, source_target_pairs={{0,16},{1,5},{2,18},{3,7},{4,20},{5,1},{6,22},{7,3},{8,24},{9,13},... | collective-permute-start | bytes 786440 | tf_op jit(solution)/shard_map/ppermute | solution.py:350
  22.5 2.0 %collective-permute-start = (bf16[16,128,256]{2,1,0:T(8,128)(2,1)}, bf16[16,128,256]{2,1,0:T(8,128)(2,1)S(1)}, u32[]{:S(2)}, u32[]{:S(2)}) collective-permute-start(bf16[16,128,256]{2,1,0:T(8,128)(2,1)} %get-tuple-element.28), channel_id=1, source_target_pairs={{0,1},{1,0},{2,3},{3,2},{4,5},{5,4},{6,7},{7,6},{8,9},{9,8},{10,11... | collective-permute-start | bytes 3145736 | tf_op jit(solution)/shard_map/ppermute | solution.py:354
  26.0 7.5 %collective-permute-start.4 = (bf16[4,256,256]{2,1,0:T(8,128)(2,1)S(1)}, bf16[4,256,256]{2,1,0:T(8,128)(2,1)}, u32[]{:S(2)}, u32[]{:S(2)}) collective-permute-start(bf16[4,256,256]{2,1,0:T(8,128)(2,1)S(1)} %pad_maximum_fusion.refs_0_), channel_id=1, source_target_pairs={{0,2},{1,9},{2,4},{3,11},{4,6},{5,13},{6,0},{7,15},{8,10},{9,17},{... | collective-permute-start | bytes 1572872 | tf_op jit(solution)/shard_map/ppermute | solution.py:350
  33.6 1.9 %collective-permute-start.6 = (bf16[4,256,256]{2,1,0:T(8,128)(2,1)S(1)}, bf16[4,256,256]{2,1,0:T(8,128)(2,1)}, u32[]{:S(2)}, u32[]{:S(2)}) collective-permute-start(bf16[4,256,256]{2,1,0:T(8,128)(2,1)S(1)} %pad_maximum_fusion.1.refs_1_), channel_id=1, source_target_pairs={{0,6},{1,25},{2,0},{3,27},{4,2},{5,29},{6,4},{7,31},{8,14},{9,1},{... | collective-permute-start | bytes 1572872 | tf_op jit(solution)/shard_map/ppermute | solution.py:350
  35.6 5.1 %collective-permute-start.9 = (bf16[4,256,256]{2,1,0:T(8,128)(2,1)S(1)}, bf16[4,256,256]{2,1,0:T(8,128)(2,1)}, u32[]{:S(2)}, u32[]{:S(2)}) collective-permute-start(bf16[4,256,256]{2,1,0:T(8,128)(2,1)S(1)} %pad_maximum_fusion.1.refs_1_), channel_id=1, source_target_pairs={{0,2},{1,9},{2,4},{3,11},{4,6},{5,13},{6,0},{7,15},{8,10},{9,17},{... | collective-permute-start | bytes 1572872 | tf_op jit(solution)/shard_map/ppermute | solution.py:350
  40.7 1.9 %collective-permute-start.8 = (bf16[4,256,256]{2,1,0:T(8,128)(2,1)S(1)}, bf16[4,256,256]{2,1,0:T(8,128)(2,1)}, u32[]{:S(2)}, u32[]{:S(2)}) collective-permute-start(bf16[4,256,256]{2,1,0:T(8,128)(2,1)S(1)} %pad_maximum_fusion.refs_0_), channel_id=1, source_target_pairs={{0,6},{1,25},{2,0},{3,27},{4,2},{5,29},{6,4},{7,31},{8,14},{9,1},{... | collective-permute-start | bytes 1572872 | tf_op jit(solution)/shard_map/ppermute | solution.py:350
  42.6 5.1 %collective-permute-start.5 = (bf16[4,256,256]{2,1,0:T(8,128)(2,1)}, bf16[4,256,256]{2,1,0:T(8,128)(2,1)}, u32[]{:S(2)}, u32[]{:S(2)}) collective-permute-start(bf16[4,256,256]{2,1,0:T(8,128)(2,1)} %collective-permute-done.4.refs_0_), channel_id=1, source_target_pairs={{0,2},{1,9},{2,4},{3,11},{4,6},{5,13},{6,0},{7,15},{8,10},{9,17},{... | collective-permute-start | bytes 1572872 | tf_op jit(solution)/shard_map/ppermute | solution.py:350
  47.8 1.9 %collective-permute-start.7 = (bf16[4,256,256]{2,1,0:T(8,128)(2,1)}, bf16[4,256,256]{2,1,0:T(8,128)(2,1)}, u32[]{:S(2)}, u32[]{:S(2)}) collective-permute-start(bf16[4,256,256]{2,1,0:T(8,128)(2,1)} %collective-permute-done.6.refs_1_), channel_id=1, source_target_pairs={{0,6},{1,25},{2,0},{3,27},{4,2},{5,29},{6,4},{7,31},{8,14},{9,1},{... | collective-permute-start | bytes 1572872 | tf_op jit(solution)/shard_map/ppermute | solution.py:350
  51.0 1.7 shard_map.111
  53.1 1.7 shard_map.112
  54.8 5.6 %collective-permute-done.7.refs_1_ = bf16[4,256,256]{2,1,0:T(8,128)(2,1)} collective-permute-done((bf16[4,256,256]{2,1,0:T(8,128)(2,1)}, bf16[4,256,256]{2,1,0:T(8,128)(2,1)}, u32[]{:S(2)}, u32[]{:S(2)}) %collective-permute-start.7) | collective-permute-done | bytes 524320 | tf_op jit(solution)/shard_map/ppermute | solution.py:350
  60.4 1.7 shard_map.113
  62.1 1.9 %collective-permute-start.10 = (f32[512,128]{1,0:T(8,128)S(1)}, f32[512,128]{1,0:T(8,128)S(1)}, u32[]{:S(2)}, u32[]{:S(2)}) collective-permute-start(f32[512,128]{1,0:T(8,128)S(1)} %get-tuple-element.36), channel_id=1, source_target_pairs={{0,1},{1,0},{2,3},{3,2},{4,5},{5,4},{6,7},{7,6},{8,9},{9,8},{10,11... | collective-permute-start | bytes 786440 | tf_op jit(solution)/shard_map/ppermute | solution.py:354
  65.7 32.0 %all-gather = bf16[2240,128]{1,0:T(8,128)(2,1)S(1)} all-gather(bf16[560,128]{1,0:T(8,128)(2,1)S(1)} %shard_map.114), channel_id=2, replica_groups={{0,128,256,384},{32,160,288,416},{64,192,320,448},{96,224,352,480},{1,1..., dimensions={0}, use_global_device_ids=true | all-gather | bytes 716800 | tf_op jit(solution)/shard_map/all_gather | solution.py:430
  100.1 3.0 %collective-permute-start.13 = (bf16[4,272,128]{2,1,0:T(8,128)(2,1)}, bf16[4,272,128]{2,1,0:T(8,128)(2,1)S(1)}, u32[]{:S(2)}, u32[]{:S(2)}) collective-permute-start(bf16[4,272,128]{2,1,0:T(8,128)(2,1)} %shard_map.120), channel_id=1, source_target_pairs={{0,64},{1,449},{2,66},{3,451},{4,68},{5,453},{6,70},{7,455},{8,72}... | collective-permute-start | bytes 835592 | tf_op jit(solution)/shard_map/ppermute | solution.py:364
  104.5 2.8 %collective-permute-start.12 = (bf16[4,272,128]{2,1,0:T(8,128)(2,1)}, bf16[4,272,128]{2,1,0:T(8,128)(2,1)S(1)}, u32[]{:S(2)}, u32[]{:S(2)}) collective-permute-start(bf16[4,272,128]{2,1,0:T(8,128)(2,1)} %shard_map.119), channel_id=1, source_target_pairs={{0,480},{1,33},{2,482},{3,35},{4,484},{5,37},{6,486},{7,39},{8,488... | collective-permute-start | bytes 835592 | tf_op jit(solution)/shard_map/ppermute | solution.py:364
  108.7 3.3 %collective-permute-start.11 = (bf16[4,272,128]{2,1,0:T(8,128)(2,1)}, bf16[4,272,128]{2,1,0:T(8,128)(2,1)}, u32[]{:S(2)}, u32[]{:S(2)}) collective-permute-start(bf16[4,272,128]{2,1,0:T(8,128)(2,1)} %shard_map.118), channel_id=1, source_target_pairs={{0,32},{1,481},{2,34},{3,483},{4,36},{5,485},{6,38},{7,487},{8,40}... | collective-permute-start | bytes 835592 | tf_op jit(solution)/shard_map/ppermute | solution.py:364
  114.5 2.0 %shard_map.116 = (bf16[4,256,128]{2,1,0:T(8,128)(2,1)S(1)}, bf16[4,256,128]{2,1,0:T(8,128)(2,1)S(1)}, bf16[4,256,128]{2,1,0:T(8,128)(2,1)S(1)}, bf16[4,256,128]{2,1,0:T(8,128)(2,1)S(1)}) custom-call(s32[1]{0:T(128)} %bitcast.22.group_ref, s32[16]{0:T(128)S(1)} %stack.147.sources_ref, s32[1,128]{1,0:T(1,128)S(1)} %copy-done.6, bf16[16,528,128]{2,1,0:T(8,128)(2,1)S(1)} %bitcast.55), custom_call_target="tpu_custom_call" | custom-call | tf_op jit(solution)/shard_map/pallas_call | solution.py:231
  116.7 2.7 %collective-permute-done.11.refs_5_ = bf16[4,272,128]{2,1,0:T(8,128)(2,1)} collective-permute-done((bf16[4,272,128]{2,1,0:T(8,128)(2,1)}, bf16[4,272,128]{2,1,0:T(8,128)(2,1)}, u32[]{:S(2)}, u32[]{:S(2)}) %collective-permute-start.11) | collective-permute-done | bytes 278560 | tf_op jit(solution)/shard_map/ppermute | solution.py:364
  119.4 6.4 %shard_map.121 = (bf16[4,256,128]{2,1,0:T(8,128)(2,1)S(1)}, bf16[4,256,128]{2,1,0:T(8,128)(2,1)}, bf16[4,256,128]{2,1,0:T(8,128)(2,1)}, bf16[4,256,128]{2,1,0:T(8,128)(2,1)}) custom-call(s32[8]{0:T(128)S(1)} %bitcast.57, bf16[4,256,128]{2,1,0:T(8,128)(2,1)S(1)} %get-tuple-element.37.refs_0_, bf16[4,256,128]{2,1,0:T(8,128)(2,1)S(1)} %get-tuple-element.38.refs_1_, ...), custom_call_target="tpu_custom_call" | custom-call | tf_op jit(solution)/shard_map/pallas_call | solution.py:332
  125.7 2.7 %collective-permute-start.14 = (bf16[4,256,128]{2,1,0:T(8,128)(2,1)}, bf16[4,256,128]{2,1,0:T(8,128)(2,1)S(1)}, u32[]{:S(2)}, u32[]{:S(2)}) collective-permute-start(bf16[4,256,128]{2,1,0:T(8,128)(2,1)} %get-tuple-element.42), channel_id=1, source_target_pairs={{0,448},{1,65},{2,450},{3,67},{4,452},{5,69},{6,454},{7,71},{8,456... | collective-permute-start | bytes 786440 | tf_op jit(solution)/shard_map/ppermute | solution.py:364
  128.4 2.0 %collective-permute-start.15 = (bf16[4,256,128]{2,1,0:T(8,128)(2,1)}, bf16[4,256,128]{2,1,0:T(8,128)(2,1)S(1)}, u32[]{:S(2)}, u32[]{:S(2)}) collective-permute-start(bf16[4,256,128]{2,1,0:T(8,128)(2,1)} %get-tuple-element.43), channel_id=1, source_target_pairs={{0,480},{1,33},{2,482},{3,35},{4,484},{5,37},{6,486},{7,39},{8,488... | collective-permute-start | bytes 786440 | tf_op jit(solution)/shard_map/ppermute | solution.py:364
  130.4 3.8 %collective-permute-start.16 = (bf16[4,256,128]{2,1,0:T(8,128)(2,1)}, bf16[4,256,128]{2,1,0:T(8,128)(2,1)S(1)}, u32[]{:S(2)}, u32[]{:S(2)}) collective-permute-start(bf16[4,256,128]{2,1,0:T(8,128)(2,1)} %get-tuple-element.44), channel_id=1, source_target_pairs={{0,32},{1,481},{2,34},{3,483},{4,36},{5,485},{6,38},{7,487},{8,40}... | collective-permute-start | bytes 786440 | tf_op jit(solution)/shard_map/ppermute | solution.py:364
  134.4 4.0 %collective-permute-done.14.refs_1_ = bf16[4,256,128]{2,1,0:T(8,128)(2,1)S(1)} collective-permute-done((bf16[4,256,128]{2,1,0:T(8,128)(2,1)}, bf16[4,256,128]{2,1,0:T(8,128)(2,1)S(1)}, u32[]{:S(2)}, u32[]{:S(2)}) %collective-permute-start.14) | collective-permute-done | bytes 262176 | tf_op jit(solution)/shard_map/ppermute | solution.py:364
  138.4 4.6 %collective-permute-done.15.refs_2_ = bf16[4,256,128]{2,1,0:T(8,128)(2,1)S(1)} collective-permute-done((bf16[4,256,128]{2,1,0:T(8,128)(2,1)}, bf16[4,256,128]{2,1,0:T(8,128)(2,1)S(1)}, u32[]{:S(2)}, u32[]{:S(2)}) %collective-permute-start.15) | collective-permute-done | bytes 262176 | tf_op jit(solution)/shard_map/ppermute | solution.py:364
  144.3 5.1 %collective-permute-start.18 = (bf16[512,128]{1,0:T(8,128)(2,1)S(1)}, bf16[512,128]{1,0:T(8,128)(2,1)S(1)}, u32[]{:S(2)}, u32[]{:S(2)}) collective-permute-start(bf16[512,128]{1,0:T(8,128)(2,1)S(1)} %get-tuple-element.48), channel_id=1, source_target_pairs={{0,128},{1,385},{2,130},{3,387},{4,132},{5,389},{6,134},{7,391},{8... | collective-permute-start | bytes 393224 | tf_op jit(solution)/shard_map/ppermute | solution.py:375
  149.5 4.6 %collective-permute-start.17 = (bf16[512,128]{1,0:T(8,128)(2,1)S(1)}, bf16[512,128]{1,0:T(8,128)(2,1)S(1)}, u32[]{:S(2)}, u32[]{:S(2)}) collective-permute-start(bf16[512,128]{1,0:T(8,128)(2,1)S(1)} %get-tuple-element.46), channel_id=1, source_target_pairs={{0,128},{1,385},{2,130},{3,387},{4,132},{5,389},{6,134},{7,391},{8... | collective-permute-start | bytes 393224 | tf_op jit(solution)/shard_map/ppermute | solution.py:375
  154.1 7.2 %collective-permute-done.18 = bf16[512,128]{1,0:T(8,128)(2,1)S(1)} collective-permute-done((bf16[512,128]{1,0:T(8,128)(2,1)S(1)}, bf16[512,128]{1,0:T(8,128)(2,1)S(1)}, u32[]{:S(2)}, u32[]{:S(2)}) %collective-permute-start.18) | collective-permute-done | bytes 131104 | tf_op jit(solution)/shard_map/ppermute | solution.py:375
  161.3 1.9 %collective-permute-start.19 = (bf16[512,128]{1,0:T(8,128)(2,1)S(1)}, bf16[512,128]{1,0:T(8,128)(2,1)S(1)}, u32[]{:S(2)}, u32[]{:S(2)}) collective-permute-start(bf16[512,128]{1,0:T(8,128)(2,1)S(1)} %add_convert_fusion.1), channel_id=1, source_target_pairs={{0,384},{1,129},{2,386},{3,131},{4,388},{5,133},{6,390},{7,135},{8... | collective-permute-start | bytes 393224 | tf_op jit(solution)/shard_map/ppermute | solution.py:375
  163.9 8.3 %collective-permute-done.19 = bf16[512,128]{1,0:T(8,128)(2,1)S(1)} collective-permute-done((bf16[512,128]{1,0:T(8,128)(2,1)S(1)}, bf16[512,128]{1,0:T(8,128)(2,1)S(1)}, u32[]{:S(2)}, u32[]{:S(2)}) %collective-permute-start.19) | collective-permute-done | bytes 131104 | tf_op jit(solution)/shard_map/ppermute | solution.py:375
  (62 shorter events, 20.3 us)
Async XLA Ops:
  6.5 18.0 %copy-start.8 = (bf16[512,256]{1,0:T(8,128)(2,1)S(1)}, bf16[512,256]{1,0:T(8,128)(2,1)}, u32[]{:S(2)}) copy-start(bf16[512,256]{1,0:T(8,128)(2,1)} %param.13) | copy-start | bytes 786436
  6.5 106.3 %all-gather.4.cloned.1.call-start = ((), (), s32[]{:S(2)}) async-start(), calls=%async_computation | async-start | bytes 2297856 | tf_op jit(solution)/shard_map/all_gather | solution.py:405
  8.9 15.7 %collective-permute-start.1 = (bf16[512,256]{1,0:T(8,128)(2,1)}, bf16[512,256]{1,0:T(8,128)(2,1)S(1)}, u32[]{:S(2)}, u32[]{:S(2)}) collective-permute-start(bf16[512,256]{1,0:T(8,128)(2,1)} %param.13), channel_id=1, source_target_pairs={{0,8},{1,3},{2,10},{3,5},{4,12},{5,7},{6,14},{7,1},{8,16},{9,11},{... | collective-permute-start | bytes 786440 | tf_op jit(solution)/shard_map/ppermute | solution.py:350
  12.3 12.4 %collective-permute-start.2 = (bf16[512,256]{1,0:T(8,128)(2,1)}, bf16[512,256]{1,0:T(8,128)(2,1)S(1)}, u32[]{:S(2)}, u32[]{:S(2)}) collective-permute-start(bf16[512,256]{1,0:T(8,128)(2,1)} %param.13), channel_id=1, source_target_pairs={{0,24},{1,7},{2,26},{3,1},{4,28},{5,3},{6,30},{7,5},{8,0},{9,15},{... | collective-permute-start | bytes 786440 | tf_op jit(solution)/shard_map/ppermute | solution.py:350
  16.0 10.0 %collective-permute-start.3 = (bf16[512,256]{1,0:T(8,128)(2,1)}, bf16[512,256]{1,0:T(8,128)(2,1)S(1)}, u32[]{:S(2)}, u32[]{:S(2)}) collective-permute-start(bf16[512,256]{1,0:T(8,128)(2,1)} %param.13), channel_id=1, source_target_pairs={{0,16},{1,5},{2,18},{3,7},{4,20},{5,1},{6,22},{7,3},{8,24},{9,13},... | collective-permute-start | bytes 786440 | tf_op jit(solution)/shard_map/ppermute | solution.py:350
  19.7 1.6 copy-start.1
  22.5 27.2 %copy-start.9 = (s32[4]{0:T(128)S(1)}, s32[4]{0:T(128)}, u32[]{:S(2)}) copy-start(s32[4]{0:T(128)} %constant.202) | copy-start | bytes 52
  22.5 27.4 %collective-permute-start = (bf16[16,128,256]{2,1,0:T(8,128)(2,1)}, bf16[16,128,256]{2,1,0:T(8,128)(2,1)S(1)}, u32[]{:S(2)}, u32[]{:S(2)}) collective-permute-start(bf16[16,128,256]{2,1,0:T(8,128)(2,1)} %get-tuple-element.28), channel_id=1, source_target_pairs={{0,1},{1,0},{2,3},{3,2},{4,5},{5,4},{6,7},{7,6},{8,9},{9,8},{10,11... | collective-permute-start | bytes 3145736 | tf_op jit(solution)/shard_map/ppermute | solution.py:354
  26.0 16.6 %collective-permute-start.4 = (bf16[4,256,256]{2,1,0:T(8,128)(2,1)S(1)}, bf16[4,256,256]{2,1,0:T(8,128)(2,1)}, u32[]{:S(2)}, u32[]{:S(2)}) collective-permute-start(bf16[4,256,256]{2,1,0:T(8,128)(2,1)S(1)} %pad_maximum_fusion.refs_0_), channel_id=1, source_target_pairs={{0,2},{1,9},{2,4},{3,11},{4,6},{5,13},{6,0},{7,15},{8,10},{9,17},{... | collective-permute-start | bytes 1572872 | tf_op jit(solution)/shard_map/ppermute | solution.py:350
  33.6 14.2 %collective-permute-start.6 = (bf16[4,256,256]{2,1,0:T(8,128)(2,1)S(1)}, bf16[4,256,256]{2,1,0:T(8,128)(2,1)}, u32[]{:S(2)}, u32[]{:S(2)}) collective-permute-start(bf16[4,256,256]{2,1,0:T(8,128)(2,1)S(1)} %pad_maximum_fusion.1.refs_1_), channel_id=1, source_target_pairs={{0,6},{1,25},{2,0},{3,27},{4,2},{5,29},{6,4},{7,31},{8,14},{9,1},{... | collective-permute-start | bytes 1572872 | tf_op jit(solution)/shard_map/ppermute | solution.py:350
  35.6 15.4 %collective-permute-start.9 = (bf16[4,256,256]{2,1,0:T(8,128)(2,1)S(1)}, bf16[4,256,256]{2,1,0:T(8,128)(2,1)}, u32[]{:S(2)}, u32[]{:S(2)}) collective-permute-start(bf16[4,256,256]{2,1,0:T(8,128)(2,1)S(1)} %pad_maximum_fusion.1.refs_1_), channel_id=1, source_target_pairs={{0,2},{1,9},{2,4},{3,11},{4,6},{5,13},{6,0},{7,15},{8,10},{9,17},{... | collective-permute-start | bytes 1572872 | tf_op jit(solution)/shard_map/ppermute | solution.py:350
  40.7 12.4 %collective-permute-start.8 = (bf16[4,256,256]{2,1,0:T(8,128)(2,1)S(1)}, bf16[4,256,256]{2,1,0:T(8,128)(2,1)}, u32[]{:S(2)}, u32[]{:S(2)}) collective-permute-start(bf16[4,256,256]{2,1,0:T(8,128)(2,1)S(1)} %pad_maximum_fusion.refs_0_), channel_id=1, source_target_pairs={{0,6},{1,25},{2,0},{3,27},{4,2},{5,29},{6,4},{7,31},{8,14},{9,1},{... | collective-permute-start | bytes 1572872 | tf_op jit(solution)/shard_map/ppermute | solution.py:350
  42.6 12.2 %collective-permute-start.5 = (bf16[4,256,256]{2,1,0:T(8,128)(2,1)}, bf16[4,256,256]{2,1,0:T(8,128)(2,1)}, u32[]{:S(2)}, u32[]{:S(2)}) collective-permute-start(bf16[4,256,256]{2,1,0:T(8,128)(2,1)} %collective-permute-done.4.refs_0_), channel_id=1, source_target_pairs={{0,2},{1,9},{2,4},{3,11},{4,6},{5,13},{6,0},{7,15},{8,10},{9,17},{... | collective-permute-start | bytes 1572872 | tf_op jit(solution)/shard_map/ppermute | solution.py:350
  47.8 12.6 %collective-permute-start.7 = (bf16[4,256,256]{2,1,0:T(8,128)(2,1)}, bf16[4,256,256]{2,1,0:T(8,128)(2,1)}, u32[]{:S(2)}, u32[]{:S(2)}) collective-permute-start(bf16[4,256,256]{2,1,0:T(8,128)(2,1)} %collective-permute-done.6.refs_1_), channel_id=1, source_target_pairs={{0,6},{1,25},{2,0},{3,27},{4,2},{5,29},{6,4},{7,31},{8,14},{9,1},{... | collective-permute-start | bytes 1572872 | tf_op jit(solution)/shard_map/ppermute | solution.py:350
  54.8 10.8 %copy-start.4 = (bf16[512,128]{1,0:T(8,128)(2,1)S(1)}, bf16[512,128]{1,0:T(8,128)(2,1)}, u32[]{:S(2)}) copy-start(bf16[512,128]{1,0:T(8,128)(2,1)} %outputs_ref.1) | copy-start | bytes 393220
  54.8 10.7 %copy-start.5 = (f32[512,1]{0,1:T(1,128)S(1)}, f32[512,1]{0,1:T(1,128)}, u32[]{:S(2)}) copy-start(f32[512,1]{0,1:T(1,128)} %param.15) | copy-start | bytes 6148
  60.4 37.3 %copy-start.6 = (s32[1,128]{1,0:T(1,128)S(1)}, s32[1,128]{1,0:T(1,128)}, u32[]{:S(2)}) copy-start(s32[1,128]{1,0:T(1,128)} %table_ref.3) | copy-start | bytes 1540
  62.1 3.4 %collective-permute-start.10 = (f32[512,128]{1,0:T(8,128)S(1)}, f32[512,128]{1,0:T(8,128)S(1)}, u32[]{:S(2)}, u32[]{:S(2)}) collective-permute-start(f32[512,128]{1,0:T(8,128)S(1)} %get-tuple-element.36), channel_id=1, source_target_pairs={{0,1},{1,0},{2,3},{3,2},{4,5},{5,4},{6,7},{7,6},{8,9},{9,8},{10,11... | collective-permute-start | bytes 786440 | tf_op jit(solution)/shard_map/ppermute | solution.py:354
  100.1 16.5 %collective-permute-start.13 = (bf16[4,272,128]{2,1,0:T(8,128)(2,1)}, bf16[4,272,128]{2,1,0:T(8,128)(2,1)S(1)}, u32[]{:S(2)}, u32[]{:S(2)}) collective-permute-start(bf16[4,272,128]{2,1,0:T(8,128)(2,1)} %shard_map.120), channel_id=1, source_target_pairs={{0,64},{1,449},{2,66},{3,451},{4,68},{5,453},{6,70},{7,455},{8,72}... | collective-permute-start | bytes 835592 | tf_op jit(solution)/shard_map/ppermute | solution.py:364
  104.5 12.2 %collective-permute-start.12 = (bf16[4,272,128]{2,1,0:T(8,128)(2,1)}, bf16[4,272,128]{2,1,0:T(8,128)(2,1)S(1)}, u32[]{:S(2)}, u32[]{:S(2)}) collective-permute-start(bf16[4,272,128]{2,1,0:T(8,128)(2,1)} %shard_map.119), channel_id=1, source_target_pairs={{0,480},{1,33},{2,482},{3,35},{4,484},{5,37},{6,486},{7,39},{8,488... | collective-permute-start | bytes 835592 | tf_op jit(solution)/shard_map/ppermute | solution.py:364
  108.7 10.7 %copy-start.2 = (bf16[1,8,512,128]{3,2,1,0:T(8,128)(2,1)S(1)}, bf16[1,8,512,128]{3,2,1,0:T(8,128)(2,1)}, u32[]{:S(2)}) copy-start(bf16[1,8,512,128]{3,2,1,0:T(8,128)(2,1)} %refs_8_.1) | copy-start | bytes 3145732
  108.7 10.7 %copy-start.7 = (s32[1,8]{1,0:T(1,128)S(1)}, s32[1,8]{1,0:T(1,128)}, u32[]{:S(2)}) copy-start(s32[1,8]{1,0:T(1,128)} %param.18) | copy-start | bytes 100
  108.7 10.7 %collective-permute-start.11 = (bf16[4,272,128]{2,1,0:T(8,128)(2,1)}, bf16[4,272,128]{2,1,0:T(8,128)(2,1)}, u32[]{:S(2)}, u32[]{:S(2)}) collective-permute-start(bf16[4,272,128]{2,1,0:T(8,128)(2,1)} %shard_map.118), channel_id=1, source_target_pairs={{0,32},{1,481},{2,34},{3,483},{4,36},{5,485},{6,38},{7,487},{8,40}... | collective-permute-start | bytes 835592 | tf_op jit(solution)/shard_map/ppermute | solution.py:364
  112.9 1.6 copy-start
  114.5 4.9 %copy-start.3 = (bf16[1,8,512,128]{3,2,1,0:T(8,128)(2,1)S(1)}, bf16[1,8,512,128]{3,2,1,0:T(8,128)(2,1)}, u32[]{:S(2)}) copy-start(bf16[1,8,512,128]{3,2,1,0:T(8,128)(2,1)} %refs_9_.1) | copy-start | bytes 3145732
  125.7 12.6 %collective-permute-start.14 = (bf16[4,256,128]{2,1,0:T(8,128)(2,1)}, bf16[4,256,128]{2,1,0:T(8,128)(2,1)S(1)}, u32[]{:S(2)}, u32[]{:S(2)}) collective-permute-start(bf16[4,256,128]{2,1,0:T(8,128)(2,1)} %get-tuple-element.42), channel_id=1, source_target_pairs={{0,448},{1,65},{2,450},{3,67},{4,452},{5,69},{6,454},{7,71},{8,456... | collective-permute-start | bytes 786440 | tf_op jit(solution)/shard_map/ppermute | solution.py:364
  128.4 14.5 %collective-permute-start.15 = (bf16[4,256,128]{2,1,0:T(8,128)(2,1)}, bf16[4,256,128]{2,1,0:T(8,128)(2,1)S(1)}, u32[]{:S(2)}, u32[]{:S(2)}) collective-permute-start(bf16[4,256,128]{2,1,0:T(8,128)(2,1)} %get-tuple-element.43), channel_id=1, source_target_pairs={{0,480},{1,33},{2,482},{3,35},{4,484},{5,37},{6,486},{7,39},{8,488... | collective-permute-start | bytes 786440 | tf_op jit(solution)/shard_map/ppermute | solution.py:364
  130.4 12.5 %collective-permute-start.16 = (bf16[4,256,128]{2,1,0:T(8,128)(2,1)}, bf16[4,256,128]{2,1,0:T(8,128)(2,1)S(1)}, u32[]{:S(2)}, u32[]{:S(2)}) collective-permute-start(bf16[4,256,128]{2,1,0:T(8,128)(2,1)} %get-tuple-element.44), channel_id=1, source_target_pairs={{0,32},{1,481},{2,34},{3,483},{4,36},{5,485},{6,38},{7,487},{8,40}... | collective-permute-start | bytes 786440 | tf_op jit(solution)/shard_map/ppermute | solution.py:364
  144.3 16.9 %collective-permute-start.18 = (bf16[512,128]{1,0:T(8,128)(2,1)S(1)}, bf16[512,128]{1,0:T(8,128)(2,1)S(1)}, u32[]{:S(2)}, u32[]{:S(2)}) collective-permute-start(bf16[512,128]{1,0:T(8,128)(2,1)S(1)} %get-tuple-element.48), channel_id=1, source_target_pairs={{0,128},{1,385},{2,130},{3,387},{4,132},{5,389},{6,134},{7,391},{8... | collective-permute-start | bytes 393224 | tf_op jit(solution)/shard_map/ppermute | solution.py:375
  149.5 14.5 %collective-permute-start.17 = (bf16[512,128]{1,0:T(8,128)(2,1)S(1)}, bf16[512,128]{1,0:T(8,128)(2,1)S(1)}, u32[]{:S(2)}, u32[]{:S(2)}) collective-permute-start(bf16[512,128]{1,0:T(8,128)(2,1)S(1)} %get-tuple-element.46), channel_id=1, source_target_pairs={{0,128},{1,385},{2,130},{3,387},{4,132},{5,389},{6,134},{7,391},{8... | collective-permute-start | bytes 393224 | tf_op jit(solution)/shard_map/ppermute | solution.py:375
  161.3 10.9 %collective-permute-start.19 = (bf16[512,128]{1,0:T(8,128)(2,1)S(1)}, bf16[512,128]{1,0:T(8,128)(2,1)S(1)}, u32[]{:S(2)}, u32[]{:S(2)}) collective-permute-start(bf16[512,128]{1,0:T(8,128)(2,1)S(1)} %add_convert_fusion.1), channel_id=1, source_target_pairs={{0,384},{1,129},{2,386},{3,131},{4,388},{5,133},{6,390},{7,135},{8... | collective-permute-start | bytes 393224 | tf_op jit(solution)/shard_map/ppermute | solution.py:375
Sparse Core Ops, SparseCore 0:
  9.4 87.9 all-gather.3
